TPU v7x, 512 devices: a whole 4x8x8 slice. The times are simulated.
512 devices in a mesh: rep: 8 (over y), day: 64 (over x, z, core).
Axes of the slice: x: 4, y: 8, z: 8, core: 2. Of those that a mesh axis runs over, the one named last changes fastest.
Arguments:
- events: bfloat16 [524288, 512], P(('rep', 'day')), may hold values from -6 to 6
- event_user: int32 [524288], P(('rep', 'day')), may hold values from 0 to 63, as said below
- event_day: int32 [524288], P(('rep', 'day')), may hold values from 0 to 3
- score_weight: bfloat16 [512, 8], replicated, may hold values from -0.25 to 0.25
- value_weight: bfloat16 [512, 512], replicated, may hold values from -0.25 to 0.25
- qkv_weight: bfloat16 [512, 1536], replicated, may hold values from -0.25 to 0.25
- cotangent: bfloat16 [512, 256, 512], P(('rep', 'day')), may hold values from -6 to 6
Outputs:
- grad_qkv_weight: float32 [512, 1536], P('day')
- grad_score_weight: float32 [512, 8], P('day')
Inputs may be any that keep to these rules, and one draw needn't show every extreme that they name: `event_user`: in every block of 1024 events each of the 64 users has at least one event on each of the 4 days.
All inputs are finite; a program needn't handle non-finite values.
Results may differ from a plain program's by a relative error of at most 0.015.
Values may be sent and summed in bfloat16 or wider, within the bound.
No kernel may reach another device: no remote copies, remote signals or barrier semaphores. Data moves between devices by JAX's collectives and lax.ppermute only.
A program may use at most 128 MiB of HBM per device.

v0:
```python
import math

import jax
import jax.numpy as jnp
from jax import lax
from jax.sharding import PartitionSpec as P


def attention_pass(summary_rows, cotangent_rows, qkv_weight, loss_scale, head_count):
    user_batch, day_count, model_width = summary_rows.shape
    head_size = model_width // head_count
    wide_summary = summary_rows.astype(jnp.float32)
    inverse_rms = lax.rsqrt(jnp.mean(wide_summary * wide_summary, axis=-1, keepdims=True) + 1e-06)
    normed = (wide_summary * inverse_rms).astype(jnp.bfloat16)
    flat_normed = normed.reshape(user_batch * day_count, model_width)
    projected = jnp.dot(flat_normed, qkv_weight, preferred_element_type=jnp.float32).astype(
        jnp.bfloat16
    )
    projected = projected.reshape(user_batch, day_count, 3, head_count, head_size)
    queries = projected[:, :, 0]
    key_rows = projected[:, :, 1]
    value_rows = projected[:, :, 2]
    cotangent_heads = cotangent_rows.reshape(user_batch, day_count, head_count, head_size)
    root_size = math.sqrt(head_size)
    logits = (
        jnp.einsum("bqhd,bkhd->bhqk", queries, key_rows, preferred_element_type=jnp.float32)
        / root_size
    )
    causal = jnp.arange(day_count)[:, None] >= jnp.arange(day_count)[None, :]
    exponent = jnp.where(causal, jnp.exp(logits), jnp.float32(0.0))
    attention = exponent / jnp.sum(exponent, axis=-1, keepdims=True)
    probabilities = attention.astype(jnp.bfloat16)
    grad_probs = (
        jnp.einsum(
            "bqhd,bkhd->bhqk", cotangent_heads, value_rows, preferred_element_type=jnp.float32
        )
        * loss_scale
    )
    grad_logits = (
        attention
        * (grad_probs - jnp.sum(grad_probs * attention, axis=-1, keepdims=True))
        / root_size
    )
    grad_logits = grad_logits.astype(jnp.bfloat16)
    grad_query = jnp.einsum(
        "bhqk,bkhd->bqhd", grad_logits, key_rows, preferred_element_type=jnp.float32
    )
    grad_key = jnp.einsum(
        "bhqk,bqhd->bkhd", grad_logits, queries, preferred_element_type=jnp.float32
    )
    grad_value = (
        jnp.einsum(
            "bhqk,bqhd->bkhd", probabilities, cotangent_heads, preferred_element_type=jnp.float32
        )
        * loss_scale
    )
    grad_qkv = jnp.stack([grad_query, grad_key, grad_value], axis=2).astype(jnp.bfloat16)
    grad_qkv = grad_qkv.reshape(user_batch * day_count, 3 * model_width)
    grad_weight = jnp.einsum("td,tf->df", flat_normed, grad_qkv, preferred_element_type=jnp.float32)
    grad_normed = jnp.einsum("tf,df->td", grad_qkv, qkv_weight, preferred_element_type=jnp.float32)
    grad_normed = grad_normed.reshape(user_batch, day_count, model_width)
    cubed = inverse_rms * inverse_rms * inverse_rms
    grad_summary = (
        cotangent_rows.astype(jnp.float32) * loss_scale
        + inverse_rms * grad_normed
        - wide_summary * cubed * jnp.mean(grad_normed * wide_summary, axis=-1, keepdims=True)
    )
    return (grad_weight, grad_summary.astype(jnp.bfloat16))


def shards(events, event_user, event_day, score_weight, value_weight, qkv_weight, cotangent):
    user_dev, day_total, model_width = cotangent.shape
    bucket_count = lax.axis_size("day")
    group_count = lax.axis_size("rep")
    head_count = score_weight.shape[1]
    head_size = model_width // head_count
    day_dev = day_total // bucket_count
    user_grp = user_dev * bucket_count
    slot_count = user_grp * day_dev
    event_count = events.shape[0]
    segment = event_user * day_dev + event_day
    logits = jnp.dot(events, score_weight, preferred_element_type=jnp.float32)
    exponent = jnp.exp(logits)
    denominator = jax.ops.segment_sum(exponent, segment, num_segments=slot_count)
    weight = exponent / denominator[segment]
    event_values = jnp.dot(events, value_weight, preferred_element_type=jnp.float32)
    weighted = (
        event_values.reshape(event_count, head_count, head_size) * weight[:, :, None]
    ).reshape(event_count, model_width)
    exact_summary = jax.ops.segment_sum(weighted, segment, num_segments=slot_count)
    summary = exact_summary.astype(jnp.bfloat16).reshape(user_grp, day_dev, model_width)
    by_user = lax.all_to_all(summary, "day", split_axis=0, concat_axis=1, tiled=True)
    loss_scale = 1.0 / math.sqrt(user_dev * bucket_count * group_count * day_total)
    grad_weight, grad_summary = attention_pass(
        by_user, cotangent, qkv_weight, loss_scale, head_count
    )
    grad_days = lax.all_to_all(
        grad_summary, "day", split_axis=1, concat_axis=0, tiled=True
    ).reshape(slot_count, model_width)
    grad_wide = grad_days.astype(jnp.float32)
    inner_terms = jnp.sum(
        (grad_wide * exact_summary).reshape(slot_count, head_count, head_size), axis=2
    )
    gathered = grad_days[segment]
    grad_pool = jnp.sum(
        (gathered.astype(jnp.float32) * event_values).reshape(event_count, head_count, head_size),
        axis=2,
    )
    grad_scores = (weight * (grad_pool - inner_terms[segment])).astype(jnp.bfloat16)
    score_grad = jnp.einsum("ed,eh->dh", events, grad_scores, preferred_element_type=jnp.float32)
    row_count = model_width // bucket_count
    summed_weight, summed_score = lax.psum((grad_weight, score_grad), ("rep", "day"))
    row_start = lax.axis_index("day") * row_count
    out_weight = lax.dynamic_slice_in_dim(summed_weight, row_start, row_count, 0)
    out_score = lax.dynamic_slice_in_dim(summed_score, row_start, row_count, 0)
    return (out_weight, out_score)


def solution(mesh):
    in_specs = (
        P(("rep", "day"), None),
        P(("rep", "day")),
        P(("rep", "day")),
        P(),
        P(),
        P(),
        P(("rep", "day"), None, None),
    )
    out_specs = (P("day", None), P("day", None))
    return jax.shard_map(shards, mesh=mesh, in_specs=in_specs, out_specs=out_specs, check_vma=False)
```

profile of v0, /device:TPU:1, one launch (start us, length us, event | category | flops | bytes accessed | tf_op | source)
XLA Modules:
  0.0 380.4 jit_solution(13723266077087965964)
XLA Ops:
  7.2 1.7 convolution_exponential_fusion
  9.8 6.0 %scatter_custom_fusion = f32[256,8]{1,0:T(8,128)S(1)} fusion(s32[1024]{0:T(1024)S(1)} %get-tuple-element.13, f32[1024,8]{1,0:T(8,128)S(1)} %copy.47, f32[]{:T(128)} %constant.11.clone.1), kind=kCustom, calls=%fused_computation.51 | custom fusion | flops 8192 | bytes 8196 | tf_op jit(solution)/shard_map/scatter-add | solution.py:84
  15.9 2.8 gather_fusion
  18.9 3.9 %bitcast_multiply_fusion.1 = (f32[1024,512]{0,1:T(8,128)}, f32[1024,512]{0,1:T(8,128)}) fusion(f32[1024,8]{0,1:T(8,128)S(1)} %div.24, bf16[1024,512]{1,0:T(8,128)(2,1)S(1)} %copy-done.1, bf16[512,512]{1,0:T(8,128)(2,1)} %param.11), kind=kOutput, calls=%fused_computation.13 | convolution fusion | flops 537395200 | bytes 5799936 | tf_op jit(solution)/shard_map/dot_general | solution.py:86
  22.8 2.9 copy.49
  25.7 7.4 %scatter_custom_fusion.1 = f32[256,512]{1,0:T(8,128)S(1)} fusion(s32[1024]{0:T(1024)S(1)} %get-tuple-element.13, f32[1024,512]{1,0:T(8,128)} %copy.49, f32[]{:T(128)} %constant.11.clone.1), kind=kCustom, calls=%fused_computation.48 | custom fusion | flops 524288 | bytes 524800 | tf_op jit(solution)/shard_map/scatter-add | solution.py:90
  34.0 14.8 %all-to-all-start = ((bf16[64,4,512]{2,1,0:T(4,128)(2,1)}), bf16[64,4,512]{2,1,0:T(4,128)(2,1)S(1)}, u32[]{:S(2)}, u32[]{:S(2)}) async-start(bf16[64,4,512]{2,1,0:T(4,128)(2,1)} %reshape.314), calls=%async_computation | async-start | bytes 524288 | tf_op jit(solution)/shard_map/all_to_all | solution.py:92
  49.0 1.8 copy.51
  50.9 9.9 %all-to-all-done = bf16[64,4,512]{2,1,0:T(4,128)(2,1)S(1)} async-done(((bf16[64,4,512]{2,1,0:T(4,128)(2,1)}), bf16[64,4,512]{2,1,0:T(4,128)(2,1)S(1)}, u32[]{:S(2)}, u32[]{:S(2)}) %all-to-all-start) | async-done | bytes 262176 | tf_op jit(solution)/shard_map/all_to_all | solution.py:92
  61.2 1.5 convolution_convert_fusion
  62.7 2.3 copy.50
  65.0 3.0 fusion.5
  68.1 2.8 fusion.16
  70.9 5.6 %convolution_bitcast_fusion.1 = bf16[1,256,1,8,64]{1,4,3,2,0:T(8,128)(2,1)} fusion(f32[8,256,256]{2,1,0:T(8,128)} %fusion.16, bf16[1,256,3,8,64]{1,4,3,2,0:T(8,128)(2,1)S(1)} %bitcast.99, f32[8,256,256]{1,2,0:T(8,128)} %get-tuple-element.17, f32[8,256]{1,0:T(8,128)S(1)} %get-tuple-element.16, pred[256,256]{0,1:T(8,128)(4,1)S(1)} %iota_compare_fusion), kind=kOutput, calls=%fused_computation.22 | convolution fusion | flops 73926912 | bytes 9060352 | tf_op jit(solution)/shard_map/bhqk,bkhd->bqhd/dot_general | solution.py:45
  76.5 5.7 %convolution_bitcast_fusion = bf16[1,256,1,8,64]{1,4,3,2,0:T(8,128)(2,1)} fusion(f32[8,256,256]{2,1,0:T(8,128)} %fusion.16, bf16[1,256,3,8,64]{1,4,3,2,0:T(8,128)(2,1)S(1)} %bitcast.100, f32[8,256,256]{1,2,0:T(8,128)} %get-tuple-element.17, f32[8,256]{1,0:T(8,128)S(1)} %get-tuple-element.16, pred[256,256]{0,1:T(8,128)(4,1)S(1)} %iota_compare_fusion), kind=kOutput, calls=%fused_computation.21 | convolution fusion | flops 73926912 | bytes 9060352 | tf_op jit(solution)/shard_map/bhqk,bqhd->bkhd/dot_general | solution.py:48
  82.2 2.3 fusion.6
  84.6 1.5 multiply_reduce_fusion
  86.1 1.8 reshape.323
  87.9 3.4 fusion.14
  93.1 1.3 fusion.12
  94.4 1.3 copy.68
  96.2 3.1 reduce.10
  100.2 6.0 %all-to-all-start.1 = ((bf16[64,2,1024]{2,1,0:T(2,128)(2,1)}), bf16[64,2,1024]{2,1,0:T(2,128)(2,1)S(1)}, u32[]{:S(2)}, u32[]{:S(2)}) async-start(bf16[64,2,1024]{2,1,0:T(2,128)(2,1)} %reshape.375), calls=%async_computation.1 | async-start | bytes 524288 | tf_op jit(solution)/shard_map/all_to_all | solution.py:97
  106.3 12.6 %all-to-all-done.1 = bf16[64,2,1024]{2,1,0:T(2,128)(2,1)S(1)} async-done(((bf16[64,2,1024]{2,1,0:T(2,128)(2,1)}), bf16[64,2,1024]{2,1,0:T(2,128)(2,1)S(1)}, u32[]{:S(2)}, u32[]{:S(2)}) %all-to-all-start.1) | async-done | bytes 262176 | tf_op jit(solution)/shard_map/all_to_all | solution.py:97
  119.8 2.0 convert_multiply_fusion.1
  121.8 5.1 %gather_fusion.1 = bf16[1024,512]{1,0:T(8,128)(2,1)} fusion(bf16[256,512]{1,0:T(8,128)(2,1)S(1)} %get-tuple-element.11, s32[1024]{0:T(1024)S(1)} %get-tuple-element.12), kind=kCustom, calls=%fused_computation.1 | custom fusion | bytes 2101248 | tf_op jit(solution)/shard_map/gather | solution.py:104
  126.8 2.4 copy.56
  131.5 2.8 gather_fusion.2
  134.4 2.2 bitcast_reduce_fusion
  136.9 98.4 %psum.15 = f32[512,8]{0,1:T(8,128)S(1)} all-reduce(f32[512,8]{0,1:T(8,128)S(1)} %convolution_bitcast_fusion.2), channel_id=1, replica_groups=mesh['rep'=8,'day'=64] {'rep','day'}, use_global_device_ids=true, to_apply=%region_9.10 | all-reduce | flops 4096 | bytes 32768 | tf_op jit(solution)/shard_map/psum | solution.py:112
  236.1 136.0 %all-reduce.2.cloned.1.call-done = f32[512,1536]{1,0:T(8,128)} async-done(((f32[512,1536]{1,0:T(8,128)}), f32[512,1536]{1,0:T(8,128)}) %all-reduce.2.cloned.1.call-update) | async-done | bytes 3145744 | tf_op jit(solution)/shard_map/psum | solution.py:112
  372.1 1.4 constant_dynamic-slice_fusion.1
  (55 shorter events, 10.2 us)
Async XLA Ops:
  7.2 54.0 %copy-start = (bf16[512,1536]{1,0:T(8,128)(2,1)S(1)}, bf16[512,1536]{1,0:T(8,128)(2,1)}, u32[]{:S(2)}) copy-start(bf16[512,1536]{1,0:T(8,128)(2,1)} %param.12) | copy-start | bytes 4718596
  15.9 3.0 copy-start.1
  33.1 0.9 copy-start.4
  34.0 26.8 %all-to-all-start = ((bf16[64,4,512]{2,1,0:T(4,128)(2,1)}), bf16[64,4,512]{2,1,0:T(4,128)(2,1)S(1)}, u32[]{:S(2)}, u32[]{:S(2)}) async-start(bf16[64,4,512]{2,1,0:T(4,128)(2,1)} %reshape.314), calls=%async_computation | async-start | bytes 524288 | tf_op jit(solution)/shard_map/all_to_all | solution.py:92
  48.8 323.3 %all-reduce.2.cloned.1.call-start = ((), (), s32[]{:S(2)}) async-start(), calls=%async_computation.2 | async-start | bytes 6291456 | tf_op jit(solution)/shard_map/psum | solution.py:112
  60.8 4.2 %copy-start.2 = (bf16[64,4,512]{2,1,0:T(4,128)(2,1)}, bf16[64,4,512]{2,1,0:T(4,128)(2,1)S(1)}, u32[]{:S(2)}) copy-start(bf16[64,4,512]{2,1,0:T(4,128)(2,1)S(1)} %all-to-all-done) | copy-start | bytes 786436
  61.2 3.8 %copy-start.6 = (f32[256,512]{1,0:T(8,128)}, f32[256,512]{1,0:T(8,128)S(1)}, u32[]{:S(2)}) copy-start(f32[256,512]{1,0:T(8,128)S(1)} %reshape.324) | copy-start | bytes 1572868
  65.0 3.0 copy-start.11
  68.1 2.8 copy-start.10
  82.2 2.3 copy-start.12
  82.2 2.3 copy-start.13
  82.2 2.4 copy-start.7
  91.3 0.9 copy-start.3
  91.3 1.8 copy-start.8
  94.4 25.4 %copy-start.5 = (f32[256,512]{1,0:T(8,128)S(1)}, f32[256,512]{1,0:T(8,128)}, u32[]{:S(2)}) copy-start(f32[256,512]{1,0:T(8,128)} %copy-done.4) | copy-start | bytes 1572868
  100.2 18.6 %all-to-all-start.1 = ((bf16[64,2,1024]{2,1,0:T(2,128)(2,1)}), bf16[64,2,1024]{2,1,0:T(2,128)(2,1)S(1)}, u32[]{:S(2)}, u32[]{:S(2)}) async-start(bf16[64,2,1024]{2,1,0:T(2,128)(2,1)} %reshape.375), calls=%async_computation.1 | async-start | bytes 524288 | tf_op jit(solution)/shard_map/all_to_all | solution.py:97
  126.8 2.4 copy-start.9
Sparse Core Ops, SparseCore 0:
  91.5 280.5 all-reduce.1
where the time goes:
time: 382 us; the launch traced here: 380 us
  waiting for transfers between devices  158 us (41%)
  blocking collectives  98.4 us (26%)
  local copies, waits for them, and re-layouts  32.1 us (8%)
  matrix products  31.7 us (8%)
  other arithmetic  24.3 us (6%)
  starting transfers between devices  21.1 us (6%)
  between operations  14.3 us (4%)
    psum x1, waiting for transfers between devices, shards(): lax.psum((grad_weight, score_grad), ('rep', 'day'))  136 us
    psum x1, blocking collectives, shards(): lax.psum((grad_weight, score_grad), ('rep', 'day'))  98.4 us
    all_to_all x1, starting transfers between devices, shards(): lax.all_to_all(summary, 'day', split_axis=0, concat_axis=1, tiled=True)  14.8 us
    all_to_all x1, waiting for transfers between devices, shards(): lax.all_to_all(grad_summary, 'day', split_axis=1, concat_axis=0, tiled=True)  12.6 us
    all_to_all x1, waiting for transfers between devices, shards(): lax.all_to_all(summary, 'day', split_axis=0, concat_axis=1, tiled=True)  9.93 us
  transfers between devices with their start and end apart: 3, of which 3 were waited for; matrix products, arithmetic and copies ran while one was open for 8% of the time, Pallas kernels for 0%

commit v1 on v0

v1 whole, which is shorter than its diff:
```python
import functools
import math

import jax
import jax.numpy as jnp
from jax import lax
from jax.experimental import pallas as pl
from jax.experimental.pallas import tpu as pltpu
from jax.sharding import Mesh, PartitionSpec as P

DAY = ("x", "z", "core")
F32 = jnp.float32
BF16 = jnp.bfloat16
BF16_MAX = 3.3895313892515355e38


def iota(shape, dim):
    return lax.broadcasted_iota(jnp.int32, shape, dim)


def one_hot(condition):
    return jnp.where(condition, 1.0, 0.0).astype(BF16)


def dot(a, b, dims):
    return lax.dot_general(a, b, ((dims[0], dims[1]), ((), ())), preferred_element_type=F32)


def nn(a, b):
    return dot(a, b, ((1,), (0,)))


def nt(a, b):
    return dot(a, b, ((1,), (1,)))


def tn(a, b):
    return dot(a, b, ((0,), (0,)))


def split3(x):
    high = jnp.minimum(x, BF16_MAX).astype(BF16)
    rest = x - high.astype(F32)
    middle = rest.astype(BF16)
    low = (rest - middle.astype(F32)).astype(BF16)
    return jnp.concatenate([high.astype(F32), middle.astype(F32), low.astype(F32)], 0).astype(BF16)


def join3(x):
    n = x.shape[0] // 3
    return x[:n] + x[n : 2 * n] + x[2 * n :]


def slot_rows(user_ref, day_ref, users, slots):
    segment = day_ref[...] * users + user_ref[...]
    return one_hot(iota((slots, segment.shape[1]), 0) == segment)


def rows_of(x, width):
    return jnp.concatenate([x[:, i : i + width] for i in range(0, x.shape[1], width)], axis=0)


def lanes_of(x, rows):
    return jnp.concatenate([x[i : i + rows] for i in range(0, x.shape[0], rows)], axis=1)


def pool_kernel(users, slots, user_ref, day_ref, events_ref, score_ref, value_ref, summary_ref, weight_ref):
    width, heads = score_ref.shape
    events = events_ref[...]
    rows = slot_rows(user_ref, day_ref, users, slots)
    eye = one_hot(iota((heads, heads), 0) == iota((heads, heads), 1))
    score_t = nt(eye, score_ref[...]).astype(BF16)
    exponent = jnp.exp(nt(score_t, events))
    denominator = join3(nt(split3(exponent), rows))
    weight = exponent / join3(nn(split3(denominator), rows))
    weight_ref[...] = weight
    expand = one_hot(iota((3 * heads, width), 1) // (width // heads) == iota((3 * heads, width), 0) % heads)
    values = nn(events, value_ref[...])
    weighted = (values * tn(split3(weight), expand)).astype(BF16)
    pooled = nn(rows, weighted)
    summary_ref[...] = lanes_of(pooled.astype(BF16), users)


def centre_kernel(users, slots, user_ref, day_ref, events_ref, value_ref, summary_ref, out_ref):
    rows = slot_rows(user_ref, day_ref, users, slots)
    pooled = rows_of(summary_ref[...], value_ref.shape[0])
    values = nn(events_ref[...], value_ref[...])
    out_ref[...] = (values - tn(rows, pooled)).astype(BF16)


def attention_kernel(heads, loss_scale, x_ref, cot_ref, qkv_weight_ref, grad_ref, normed_ref, grad_qkv_ref):
    width = qkv_weight_ref.shape[0]
    days = cot_ref.shape[0]
    buckets = x_ref.shape[0]
    day_dev = days // buckets
    size = width // heads
    row_day = (iota((days, days), 0) % buckets) * day_dev + iota((days, days), 0) // buckets
    column_day = (iota((days, days), 1) % buckets) * day_dev + iota((days, days), 1) // buckets
    causal = column_day <= row_day
    cot = nn(one_hot(iota((days, days), 1) == row_day), cot_ref[...]).astype(BF16)
    wide = rows_of(x_ref[...], width).astype(F32)
    inverse = lax.rsqrt(jnp.mean(wide * wide, axis=-1, keepdims=True) + 1e-06)
    normed = (wide * inverse).astype(BF16)
    normed_ref[...] = normed
    qkv = nn(normed, qkv_weight_ref[...]).astype(BF16)
    pair = 2 * size
    left = iota((days, pair), 1) < size
    zero = jnp.zeros((days, pair), BF16)
    root = 1.0 / math.sqrt(size)
    parts = ([], [], [])
    for start in range(0, width, pair):
        q, k, v = (qkv[:, i * width + start : i * width + start + pair] for i in range(3))
        c = cot[:, start : start + pair]
        held = ([], [], [], [], [])
        for half in range(2):
            mine = left if half == 0 else ~left
            q1, k1, v1, c1 = (jnp.where(mine, a, zero) for a in (q, k, v, c))
            exponent = jnp.where(causal, jnp.exp(nt(q, k1) * root), 0.0)
            total = jnp.sum(exponent, axis=-1, keepdims=True)
            guard = jnp.where(total > 1.0, 2.0**-64, 1.0)
            attention = (exponent * guard) * (1.0 / (total * guard))
            grad_probs = nt(c, v1) * loss_scale
            inner = jnp.sum(grad_probs * attention, axis=-1, keepdims=True)
            grad_logits = (attention * (grad_probs - inner) * root).astype(BF16)
            for group, item in zip(held, (grad_logits, attention.astype(BF16), q1, k1, c1)):
                group.append(item)
        logits_grad, probs, q2, k2, c2 = held
        parts[0].append(nn(jnp.concatenate(logits_grad, 1), jnp.concatenate(k2, 0)))
        parts[1].append(tn(jnp.concatenate(logits_grad, 0), jnp.concatenate(q2, 0)))
        parts[2].append(tn(jnp.concatenate(probs, 0), jnp.concatenate(c2, 0)) * loss_scale)
    grad_qkv = jnp.concatenate([a.astype(BF16) for part in parts for a in part], axis=1)
    grad_qkv_ref[...] = grad_qkv
    grad_normed = nt(grad_qkv, qkv_weight_ref[...])
    cubed = inverse * inverse * inverse
    grad = (
        cot.astype(F32) * loss_scale
        + inverse * grad_normed
        - wide * cubed * jnp.mean(grad_normed * wide, axis=-1, keepdims=True)
    )
    grad_ref[...] = lanes_of(grad.astype(BF16), buckets)


def outer_kernel(rows, core_ref, normed_ref, grad_qkv_ref, mine_ref, other_ref):
    width, columns = normed_ref.shape[1], grad_qkv_ref.shape[1]
    product = tn(normed_ref[...], grad_qkv_ref[...]).reshape(width // (2 * rows), 2, rows, columns)
    even = product[:, 0].reshape(width // 2, columns).astype(BF16)
    odd = product[:, 1].reshape(width // 2, columns).astype(BF16)
    first = core_ref[0] == 0

    @pl.when(first)
    def _():
        mine_ref[...] = even
        other_ref[...] = odd

    @pl.when(jnp.logical_not(first))
    def _():
        mine_ref[...] = odd
        other_ref[...] = even


def score_kernel(users, slots, user_ref, day_ref, events_ref, centred_ref, weight_ref, grad_ref, out_ref):
    width = events_ref.shape[1]
    heads = weight_ref.shape[0]
    parts, lanes = out_ref.shape
    depth = width // parts
    rows = slot_rows(user_ref, day_ref, users, slots)
    grad = tn(rows, rows_of(grad_ref[...], width))
    terms = (grad * centred_ref[...].astype(F32)).astype(BF16)
    reduce = one_hot(iota((lanes, width), 1) // (width // heads) == iota((lanes, width), 0) % heads)
    weight = jnp.concatenate([weight_ref[...]] * (lanes // heads), axis=0)
    scores = (weight * nt(reduce, terms)).astype(BF16)
    spread = nn(scores, events_ref[...])
    keep = iota((lanes, width), 1) % depth == iota((lanes, width), 0) // heads
    spread = jnp.where(keep, spread, 0.0).astype(BF16)
    pick = one_hot(iota((parts, width), 1) // depth == iota((parts, width), 0))
    out_ref[...] = nt(pick, spread).astype(BF16)


def merge_kernel(weight_ref, score_ref, out_ref):
    copies, depth, columns = out_ref.shape
    lanes = score_ref.shape[1]
    weight = jnp.sum(weight_ref[...].astype(F32), axis=0).astype(BF16)
    score = jnp.sum(score_ref[...].astype(F32), axis=0, keepdims=True)
    keep = iota((depth, lanes), 1) // depth == iota((depth, lanes), 0)
    score = jnp.where(keep, jnp.broadcast_to(score, (depth, lanes)), 0.0).astype(BF16)
    for i in range(copies):
        out_ref[i, :, : columns - lanes] = weight
        out_ref[i, :, columns - lanes :] = score


def final_kernel(x_ref, weight_ref, score_ref):
    columns = weight_ref.shape[1]
    heads = score_ref.shape[1]
    total = jnp.sum(x_ref[...].astype(F32), axis=0)
    weight_ref[...] = total[:, :columns]
    score = total[:, columns:]
    lanes = score.shape[1]
    pick = one_hot(iota((lanes, heads), 0) % heads == iota((lanes, heads), 1))
    score_ref[...] = join3(nn(split3(score), pick))


def call(kernel, outs, args, scalars=0, flops=0):
    vmem = pl.BlockSpec(memory_space=pltpu.VMEM)
    smem = pl.BlockSpec(memory_space=pltpu.SMEM)
    moved = sum(a.size * a.dtype.itemsize for a in args) + sum(math.prod(s) * jnp.dtype(t).itemsize for s, t in outs)
    return pl.pallas_call(
        kernel,
        out_shape=[jax.ShapeDtypeStruct(s, t) for s, t in outs],
        in_specs=[smem] * scalars + [vmem] * (len(args) - scalars),
        out_specs=[vmem] * len(outs),
        compiler_params=pltpu.CompilerParams(vmem_limit_bytes=48 * 2**20),
        cost_estimate=pl.CostEstimate(flops=flops, bytes_accessed=moved, transcendentals=0),
    )(*args)


def shards(sizes, events, event_user, event_day, score_weight, value_weight, qkv_weight, cotangent):
    groups, x_size, z_size, cores = sizes
    buckets = x_size * z_size * cores
    user_dev, days, width = cotangent.shape
    heads = score_weight.shape[1]
    day_dev = days // buckets
    users = user_dev * buckets
    slots = users * day_dev
    count = events.shape[0]
    rows = width // buckets
    loss_scale = 1.0 / math.sqrt(user_dev * buckets * groups * days)
    user_row = event_user.reshape(1, count)
    day_row = event_day.reshape(1, count)

    summary, weight = call(
        functools.partial(pool_kernel, users, slots),
        [((users, day_dev * width), BF16), ((heads, count), F32)],
        (user_row, day_row, events, score_weight, value_weight),
        flops=2 * count * width * (width + slots),
    )
    by_user = lax.all_to_all(summary, DAY, split_axis=0, concat_axis=0, tiled=True)
    (centred,) = call(
        functools.partial(centre_kernel, users, slots),
        [((count, width), BF16)],
        (user_row, day_row, events, value_weight, summary),
        flops=2 * count * width * (width + slots),
    )
    grad_summary, normed, grad_qkv = call(
        functools.partial(attention_kernel, heads, loss_scale),
        [((buckets, day_dev * width), BF16), ((days, width), BF16), ((days, 3 * width), BF16)],
        (by_user, cotangent.reshape(days, width), qkv_weight),
        flops=2 * days * width * (6 * width + 14 * days),
    )
    grad_days = lax.all_to_all(grad_summary, DAY, split_axis=0, concat_axis=0, tiled=True)
    mine, other = call(
        functools.partial(outer_kernel, rows),
        [((width // 2, 3 * width), BF16)] * 2,
        (lax.axis_index("core").reshape(1), normed, grad_qkv),
        scalars=1,
        flops=2 * days * width * 3 * width,
    )
    theirs = lax.ppermute(other, "core", [(i, cores - 1 - i) for i in range(cores)])
    chip = (mine.astype(F32) + theirs.astype(F32)).astype(BF16)
    chip = chip.reshape(x_size * z_size, rows, 3 * width)
    plane = lax.all_to_all(chip, ("x", "z"), split_axis=0, concat_axis=0, tiled=True)
    (score_part,) = call(
        functools.partial(score_kernel, users, slots),
        [((buckets, 128), BF16)],
        (user_row, day_row, events, centred, weight, grad_days),
        flops=2 * count * width * (slots + 256),
    )
    score_rows = lax.all_to_all(score_part, DAY, split_axis=0, concat_axis=0, tiled=True)
    (merged,) = call(
        merge_kernel,
        [((groups, rows, 3 * width + 128), BF16)],
        (plane, score_rows),
    )
    everyone = lax.all_to_all(merged, "rep", split_axis=0, concat_axis=0, tiled=True)
    return tuple(call(final_kernel, [((rows, 3 * width), F32), ((rows, heads), F32)], (everyone,)))


def solution(mesh):
    sizes = (8, 4, 8, 2)
    split = Mesh(mesh.devices.reshape(sizes), ("rep",) + DAY)
    whole = ("rep",) + DAY
    in_specs = (P(whole, None), P(whole), P(whole), P(), P(), P(), P(whole, None, None))
    out_specs = (P(DAY, None), P(DAY, None))
    return jax.shard_map(
        functools.partial(shards, sizes), mesh=split, in_specs=in_specs, out_specs=out_specs, check_vma=False
    )
```

time: 382 us -> 127 us (0.33)
  the two profiles are of different devices: /device:TPU:1 before, /device:TPU:64 now
where the time goes in v1:
time: 127 us; the launch traced here: 126 us
  waiting for transfers between devices  51.1 us (40%)
  starting transfers between devices  32.5 us (26%)
  blocking collectives  16.9 us (13%)
  local copies, waits for them, and re-layouts  11 us (9%)
  Pallas kernels  10.3 us (8%)
  other arithmetic  3.92 us (3%)
    all_to_all x1, waiting for transfers between devices, shards(): lax.all_to_all(chip, ('x', 'z'), split_axis=0, concat_axis=0, tiled=True)  23.4 us
    all_to_all x1, blocking collectives, shards(): lax.all_to_all(merged, 'rep', split_axis=0, concat_axis=0, tiled=True)  16.9 us
    all_to_all x1, starting transfers between devices, shards(): lax.all_to_all(summary, DAY, split_axis=0, concat_axis=0, tiled=True)  13 us
    all_to_all x1, waiting for transfers between devices, shards(): lax.all_to_all(summary, DAY, split_axis=0, concat_axis=0, tiled=True)  11.7 us
    pallas_call x7, Pallas kernels, call(): pl.pallas_call(kernel, out_shape=[jax.ShapeDtypeStruct(s, t) for s, t in...  10.3 us
    unnamed x28, local copies, waits for them, and re-layouts  9.83 us
    all_to_all x1, waiting for transfers between devices, shards(): lax.all_to_all(grad_summary, DAY, split_axis=0, concat_axis=0, tiled=True)  9.7 us
    all_to_all x1, starting transfers between devices, shards(): lax.all_to_all(score_part, DAY, split_axis=0, concat_axis=0, tiled=True)  6.27 us
  transfers between devices with their start and end apart: 5, of which 4 were waited for; matrix products, arithmetic and copies ran while one was open for 5% of the time, Pallas kernels for 2%

profile of v1, /device:TPU:64, one launch (start us, length us, event | category | flops | bytes accessed | tf_op | source)
XLA Modules:
  0.0 126.5 jit_solution(11714946761781699160)
XLA Ops:
  0.6 0.9 copy.14.score_ref
  1.5 1.2 copy-done
  2.7 0.7 copy-done.2
  3.4 0.7 copy-done.4
  4.1 1.0 copy-done.7
  5.1 2.0 %shard_map.86 = (bf16[64,2048]{1,0:T(8,128)(2,1)S(1)}, f32[8,1024]{1,0:T(8,128)S(1)}) custom-call(s32[1,1024]{1,0:T(1,128)S(1)} %bitcast.24, s32[1,1024]{1,0:T(1,128)S(1)} %bitcast.27, bf16[1024,512]{1,0:T(8,128)(2,1)S(1)} %copy-done, bf16[512,8]{1,0:T(8,128)(2,1)S(1)} %copy.14.score_ref, bf16[512,512]{1,0:T(8,128)(2,1)S(1)} %copy-done.7), custom_call_target="tpu_custom_call" | custom-call | flops 805306368 | bytes 1884160 | tf_op jit(solution)/shard_map/pallas_call | solution.py:206
  7.2 0.5 broadcast
  7.7 0.9 reduce
  8.6 0.9 reshape.30
  9.5 13.0 %all-to-all-start = ((bf16[64,2,1024]{2,1,0:T(2,128)(2,1)}), bf16[64,2,1024]{2,1,0:T(2,128)(2,1)S(1)}, u32[]{:S(2)}, u32[]{:S(2)}) async-start(bf16[64,2,1024]{2,1,0:T(2,128)(2,1)} %reshape.30), calls=%async_computation | async-start | bytes 524288 | tf_op jit(solution)/shard_map/all_to_all | solution.py:236
  22.5 11.7 %all-to-all-done = bf16[64,2,1024]{2,1,0:T(2,128)(2,1)S(1)} async-done(((bf16[64,2,1024]{2,1,0:T(2,128)(2,1)}), bf16[64,2,1024]{2,1,0:T(2,128)(2,1)S(1)}, u32[]{:S(2)}, u32[]{:S(2)}) %all-to-all-start) | async-done | bytes 262176 | tf_op jit(solution)/shard_map/all_to_all | solution.py:236
  34.2 0.2 reshape.31
  34.6 3.8 %shard_map.87 = (bf16[64,2048]{1,0:T(8,128)(2,1)S(1)}, bf16[256,512]{1,0:T(8,128)(2,1)S(1)}, bf16[256,1536]{1,0:T(8,128)(2,1)S(1)}) custom-call(bf16[64,2048]{1,0:T(8,128)(2,1)S(1)} %bitcast.19, bf16[256,512]{1,0:T(8,128)(2,1)S(1)} %bitcast.30, bf16[512,1536]{1,0:T(8,128)(2,1)S(1)} %copy-done.6), custom_call_target="tpu_custom_call" | custom-call | flops 1744830464 | bytes 3407872 | tf_op jit(solution)/shard_map/pallas_call | solution.py:206
  38.4 1.7 %shard_map.88 = (bf16[256,1536]{1,0:T(8,128)(2,1)S(1)}, bf16[256,1536]{1,0:T(8,128)(2,1)}) custom-call(s32[1]{0:T(128)} %bitcast.core_ref, bf16[256,512]{1,0:T(8,128)(2,1)S(1)} %get-tuple-element.10.normed_ref, bf16[256,1536]{1,0:T(8,128)(2,1)S(1)} %get-tuple-element.11.grad_qkv_ref), custom_call_target="tpu_custom_call" | custom-call | flops 402653184 | bytes 2621444 | tf_op jit(solution)/shard_map/pallas_call | solution.py:206
  40.1 2.1 %collective-permute-start = (bf16[256,1536]{1,0:T(8,128)(2,1)}, bf16[256,1536]{1,0:T(8,128)(2,1)}, u32[]{:S(2)}, u32[]{:S(2)}) collective-permute-start(bf16[256,1536]{1,0:T(8,128)(2,1)} %get-tuple-element.13), channel_id=1, source_target_pairs={{0,1},{1,0},{2,3},{3,2},{4,5},{5,4},{6,7},{7,6},{8,9},{9,8},{10,11... | collective-permute-start | bytes 2359304 | tf_op jit(solution)/shard_map/ppermute | solution.py:257
  42.2 0.8 reduce.1
  43.0 0.9 reshape.32
  43.9 6.2 %all-to-all-start.2 = ((bf16[64,2,1024]{2,1,0:T(2,128)(2,1)}), bf16[64,2,1024]{2,1,0:T(2,128)(2,1)S(1)}, u32[]{:S(2)}, u32[]{:S(2)}) async-start(bf16[64,2,1024]{2,1,0:T(2,128)(2,1)} %reshape.32), calls=%async_computation.2 | async-start | bytes 524288 | tf_op jit(solution)/shard_map/all_to_all | solution.py:249
  50.1 1.0 copy-done.8
  51.1 1.0 shard_map.89.centred_ref
  52.1 9.7 %all-to-all-done.2 = bf16[64,2,1024]{2,1,0:T(2,128)(2,1)S(1)} async-done(((bf16[64,2,1024]{2,1,0:T(2,128)(2,1)}), bf16[64,2,1024]{2,1,0:T(2,128)(2,1)S(1)}, u32[]{:S(2)}, u32[]{:S(2)}) %all-to-all-start.2) | async-done | bytes 262176 | tf_op jit(solution)/shard_map/all_to_all | solution.py:249
  61.8 0.9 reshape.33
  62.8 1.2 copy.24
  64.0 1.0 shard_map.90
  65.0 0.7 copy.17
  65.7 6.3 %all-to-all-start.3 = ((bf16[64,1,128]{2,1,0:T(2,128)(2,1)}), bf16[64,1,128]{2,1,0:T(2,128)(2,1)S(1)}, u32[]{:S(2)}, u32[]{:S(2)}) async-start(bf16[64,1,128]{2,1,0:T(2,128)(2,1)} %copy.17), calls=%async_computation.3 | async-start | bytes 65536 | tf_op jit(solution)/shard_map/all_to_all | solution.py:267
  71.9 2.2 %fusion = bf16[32,8,1536]{2,1,0:T(8,128)(2,1)} fusion(bf16[256,1536]{1,0:T(8,128)(2,1)} %collective-permute-done, bf16[256,1536]{1,0:T(8,128)(2,1)S(1)} %get-tuple-element.12), kind=kLoop, calls=%fused_computation.1 | loop fusion | flops 1572864 | bytes 2359296 | tf_op jit(solution)/shard_map/reshape | solution.py:259
  74.2 6.2 %all-to-all-done.3 = bf16[64,1,128]{2,1,0:T(2,128)(2,1)S(1)} async-done(((bf16[64,1,128]{2,1,0:T(2,128)(2,1)}), bf16[64,1,128]{2,1,0:T(2,128)(2,1)S(1)}, u32[]{:S(2)}, u32[]{:S(2)}) %all-to-all-start.3) | async-done | bytes 16416 | tf_op jit(solution)/shard_map/all_to_all | solution.py:267
  80.4 5.0 %all-to-all-start.1 = ((bf16[32,8,1536]{2,1,0:T(8,128)(2,1)}), bf16[32,8,1536]{2,1,0:T(8,128)(2,1)S(1)}, u32[]{:S(2)}, u32[]{:S(2)}) async-start(bf16[32,8,1536]{2,1,0:T(8,128)(2,1)} %fusion), calls=%async_computation.1 | async-start | bytes 1572864 | tf_op jit(solution)/shard_map/all_to_all | solution.py:260
  85.4 23.4 %all-to-all-done.1.weight_ref = bf16[32,8,1536]{2,1,0:T(8,128)(2,1)S(1)} async-done(((bf16[32,8,1536]{2,1,0:T(8,128)(2,1)}), bf16[32,8,1536]{2,1,0:T(8,128)(2,1)S(1)}, u32[]{:S(2)}, u32[]{:S(2)}) %all-to-all-start.1) | async-done | bytes 786464 | tf_op jit(solution)/shard_map/all_to_all | solution.py:260
  108.9 16.9 %all_to_all.43.x_ref = bf16[8,8,1664]{2,1,0:T(8,128)(2,1)S(1)} all-to-all(bf16[8,8,1664]{2,1,0:T(8,128)(2,1)S(1)} %shard_map.91), channel_id=1, replica_groups=mesh['rep'=8,'x'=4,'z'=8,'core'=2] {'rep'}, dimensions={0} | all-to-all | bytes 425984 | tf_op jit(solution)/shard_map/all_to_all | solution.py:273
  125.8 0.7 shard_map.92
  (19 shorter events, 0.3 us)
Async XLA Ops:
  1.5 1.2 copy-start
  2.7 0.7 copy-start.2
  3.4 0.7 copy-start.4
  4.1 1.0 copy-start.7
  7.7 26.9 %copy-start.6 = (bf16[512,1536]{1,0:T(8,128)(2,1)S(1)}, bf16[512,1536]{1,0:T(8,128)(2,1)}, u32[]{:S(2)}) copy-start(bf16[512,1536]{1,0:T(8,128)(2,1)} %qkv_weight_ref.1) | copy-start | bytes 4718596
  7.7 26.9 %copy-start.9 = (bf16[1,256,512]{2,1,0:T(8,128)(2,1)S(1)}, bf16[1,256,512]{2,1,0:T(8,128)(2,1)}, u32[]{:S(2)}) copy-start(bf16[1,256,512]{2,1,0:T(8,128)(2,1)} %param.13) | copy-start | bytes 786436
  9.5 24.7 %all-to-all-start = ((bf16[64,2,1024]{2,1,0:T(2,128)(2,1)}), bf16[64,2,1024]{2,1,0:T(2,128)(2,1)S(1)}, u32[]{:S(2)}, u32[]{:S(2)}) async-start(bf16[64,2,1024]{2,1,0:T(2,128)(2,1)} %reshape.30), calls=%async_computation | async-start | bytes 524288 | tf_op jit(solution)/shard_map/all_to_all | solution.py:236
  38.4 11.7 %copy-start.1 = (bf16[1024,512]{1,0:T(8,128)(2,1)S(1)}, bf16[1024,512]{1,0:T(8,128)(2,1)}, u32[]{:S(2)}) copy-start(bf16[1024,512]{1,0:T(8,128)(2,1)} %events_ref.5) | copy-start | bytes 3145732
  38.4 11.7 %copy-start.3 = (s32[1024]{0:T(1024)S(1)}, s32[1024]{0:T(1024)}, u32[]{:S(2)}) copy-start(s32[1024]{0:T(1024)} %param.8) | copy-start | bytes 12292
  38.4 11.7 %copy-start.5 = (s32[1024]{0:T(1024)S(1)}, s32[1024]{0:T(1024)}, u32[]{:S(2)}) copy-start(s32[1024]{0:T(1024)} %param.9) | copy-start | bytes 12292
  40.1 31.8 %collective-permute-start = (bf16[256,1536]{1,0:T(8,128)(2,1)}, bf16[256,1536]{1,0:T(8,128)(2,1)}, u32[]{:S(2)}, u32[]{:S(2)}) collective-permute-start(bf16[256,1536]{1,0:T(8,128)(2,1)} %get-tuple-element.13), channel_id=1, source_target_pairs={{0,1},{1,0},{2,3},{3,2},{4,5},{5,4},{6,7},{7,6},{8,9},{9,8},{10,11... | collective-permute-start | bytes 2359304 | tf_op jit(solution)/shard_map/ppermute | solution.py:257
  43.9 17.9 %all-to-all-start.2 = ((bf16[64,2,1024]{2,1,0:T(2,128)(2,1)}), bf16[64,2,1024]{2,1,0:T(2,128)(2,1)S(1)}, u32[]{:S(2)}, u32[]{:S(2)}) async-start(bf16[64,2,1024]{2,1,0:T(2,128)(2,1)} %reshape.32), calls=%async_computation.2 | async-start | bytes 524288 | tf_op jit(solution)/shard_map/all_to_all | solution.py:249
  50.1 1.0 copy-start.8
  65.7 14.8 %all-to-all-start.3 = ((bf16[64,1,128]{2,1,0:T(2,128)(2,1)}), bf16[64,1,128]{2,1,0:T(2,128)(2,1)S(1)}, u32[]{:S(2)}, u32[]{:S(2)}) async-start(bf16[64,1,128]{2,1,0:T(2,128)(2,1)} %copy.17), calls=%async_computation.3 | async-start | bytes 65536 | tf_op jit(solution)/shard_map/all_to_all | solution.py:267
  80.4 28.4 %all-to-all-start.1 = ((bf16[32,8,1536]{2,1,0:T(8,128)(2,1)}), bf16[32,8,1536]{2,1,0:T(8,128)(2,1)S(1)}, u32[]{:S(2)}, u32[]{:S(2)}) async-start(bf16[32,8,1536]{2,1,0:T(8,128)(2,1)} %fusion), calls=%async_computation.1 | async-start | bytes 1572864 | tf_op jit(solution)/shard_map/all_to_all | solution.py:260

commit v2 on v1

v2 whole, which is shorter than its diff:
```python
import functools
import math

import jax
import jax.numpy as jnp
from jax import lax
from jax.experimental import pallas as pl
from jax.experimental.pallas import tpu as pltpu
from jax.sharding import Mesh, PartitionSpec as P

DAY = ("x", "z", "core")
F32 = jnp.float32
BF16 = jnp.bfloat16
BF16_MAX = 3.3895313892515355e38


def iota(shape, dim):
    return lax.broadcasted_iota(jnp.int32, shape, dim)


def one_hot(condition):
    return jnp.where(condition, 1.0, 0.0).astype(BF16)


def dot(a, b, dims):
    return lax.dot_general(a, b, ((dims[0], dims[1]), ((), ())), preferred_element_type=F32)


def nn(a, b):
    return dot(a, b, ((1,), (0,)))


def nt(a, b):
    return dot(a, b, ((1,), (1,)))


def tn(a, b):
    return dot(a, b, ((0,), (0,)))


def split3(x):
    high = jnp.minimum(x, BF16_MAX).astype(BF16)
    rest = x - high.astype(F32)
    middle = rest.astype(BF16)
    low = (rest - middle.astype(F32)).astype(BF16)
    return jnp.concatenate([high.astype(F32), middle.astype(F32), low.astype(F32)], 0).astype(BF16)


def join3(x):
    n = x.shape[0] // 3
    return x[:n] + x[n : 2 * n] + x[2 * n :]


def slot_rows(user_ref, day_ref, users, slots):
    segment = user_ref[...] * (slots // users) + day_ref[...]
    return one_hot(iota((slots, segment.shape[1]), 0) == segment)


def to_rows(x, width):
    return x.astype(F32).reshape(x.size // width, width).astype(BF16)


def to_blocks(x, blocks):
    return x.reshape(blocks, x.size // (blocks * 128), 128).astype(BF16)


def pool_kernel(
    users, slots, user_ref, day_ref, score_ref, events_ref, value_ref, summary_ref, weight_ref, events_buf, value_buf, sems
):
    width, heads = score_ref.shape
    count = events_ref.shape[0]
    copies = []
    for source, target, parts in ((events_ref, events_buf, 8), (value_ref, value_buf, 4)):
        step = source.shape[0] // parts
        for i in range(parts):
            piece = pl.ds(i * step, step)
            copies.append(pltpu.make_async_copy(source.at[piece, :], target.at[piece, :], sems.at[len(copies)]))
    for copy in copies:
        copy.start()
    rows = slot_rows(user_ref, day_ref, users, slots)
    eye = one_hot(iota((heads, heads), 0) == iota((heads, heads), 1))
    score_t = nt(eye, score_ref[...]).astype(BF16)
    expand = one_hot(iota((3 * heads, width), 1) // (width // heads) == iota((3 * heads, width), 0) % heads)
    for copy in copies[:8]:
        copy.wait()
    events = events_buf[...]
    exponent = jnp.exp(nt(score_t, events))
    denominator = join3(nt(split3(exponent), rows))
    weight = exponent / join3(nn(split3(denominator), rows))
    weight_ref[...] = weight
    for copy in copies[8:]:
        copy.wait()
    values = nn(events, value_buf[...])
    weighted = (values * tn(split3(weight), expand)).astype(BF16)
    summary_ref[...] = to_blocks(nn(rows, weighted), users)


def centre_kernel(users, slots, user_ref, day_ref, events_ref, value_ref, summary_ref, out_ref):
    rows = slot_rows(user_ref, day_ref, users, slots)
    pooled = to_rows(summary_ref[...], value_ref.shape[1])
    values = nn(events_ref[...], value_ref[...])
    out_ref[...] = (values - tn(rows, pooled)).astype(BF16)


def attention_kernel(heads, loss_scale, x_ref, cot_ref, qkv_weight_ref, grad_ref, normed_ref, grad_qkv_ref):
    width = qkv_weight_ref.shape[0]
    days = cot_ref.shape[0]
    buckets = x_ref.shape[0]
    size = width // heads
    causal = iota((days, days), 1) <= iota((days, days), 0)
    cot = cot_ref[...]
    wide = to_rows(x_ref[...], width).astype(F32)
    inverse = lax.rsqrt(jnp.mean(wide * wide, axis=-1, keepdims=True) + 1e-06)
    normed = (wide * inverse).astype(BF16)
    normed_ref[...] = normed
    qkv = nn(normed, qkv_weight_ref[...]).astype(BF16)
    pair = 2 * size
    left = iota((days, pair), 1) < size
    zero = jnp.zeros((days, pair), BF16)
    root = 1.0 / math.sqrt(size)
    parts = ([], [], [])
    for start in range(0, width, pair):
        q, k, v = (qkv[:, i * width + start : i * width + start + pair] for i in range(3))
        c = cot[:, start : start + pair]
        held = ([], [], [], [], [])
        for half in range(2):
            mine = left if half == 0 else ~left
            q1, k1, v1, c1 = (jnp.where(mine, a, zero) for a in (q, k, v, c))
            exponent = jnp.where(causal, jnp.exp(nt(q, k1) * root), 0.0)
            total = jnp.sum(exponent, axis=-1, keepdims=True)
            guard = jnp.where(total > 1.0, 2.0**-64, 1.0)
            attention = (exponent * guard) * (1.0 / (total * guard))
            grad_probs = nt(c, v1) * loss_scale
            inner = jnp.sum(grad_probs * attention, axis=-1, keepdims=True)
            grad_logits = (attention * (grad_probs - inner) * root).astype(BF16)
            for group, item in zip(held, (grad_logits, attention.astype(BF16), q1, k1, c1)):
                group.append(item)
        logits_grad, probs, q2, k2, c2 = held
        parts[0].append(nn(jnp.concatenate(logits_grad, 1), jnp.concatenate(k2, 0)))
        parts[1].append(tn(jnp.concatenate(logits_grad, 0), jnp.concatenate(q2, 0)))
        parts[2].append(tn(jnp.concatenate(probs, 0), jnp.concatenate(c2, 0)) * loss_scale)
    grad_qkv = jnp.concatenate([a.astype(BF16) for part in parts for a in part], axis=1)
    grad_qkv_ref[...] = grad_qkv
    grad_normed = nt(grad_qkv, qkv_weight_ref[...])
    cubed = inverse * inverse * inverse
    grad = (
        cot.astype(F32) * loss_scale
        + inverse * grad_normed
        - wide * cubed * jnp.mean(grad_normed * wide, axis=-1, keepdims=True)
    )
    grad_ref[...] = to_blocks(grad, buckets)


def outer_kernel(rows, core_ref, normed_ref, grad_qkv_ref, mine_ref, other_ref):
    width, columns = normed_ref.shape[1], grad_qkv_ref.shape[1]
    product = tn(normed_ref[...], grad_qkv_ref[...]).reshape(width // (2 * rows), 2, rows, columns)
    even = product[:, 0].reshape(width // 2, columns).astype(BF16)
    odd = product[:, 1].reshape(width // 2, columns).astype(BF16)
    first = core_ref[0] == 0

    @pl.when(first)
    def _():
        mine_ref[...] = even
        other_ref[...] = odd

    @pl.when(jnp.logical_not(first))
    def _():
        mine_ref[...] = odd
        other_ref[...] = even


def fold_kernel(row_ref, mine_ref, theirs_ref, keep_ref, send_ref):
    half = keep_ref.shape[1]
    total = (mine_ref[...].astype(F32) + theirs_ref[...].astype(F32)).astype(BF16)
    first = row_ref[0] == 0

    @pl.when(first)
    def _():
        keep_ref[...] = total[:, :half]
        send_ref[...] = total[:, half:]

    @pl.when(jnp.logical_not(first))
    def _():
        keep_ref[...] = total[:, half:]
        send_ref[...] = total[:, :half]


def score_kernel(
    users, slots, cores, user_ref, day_ref, events_ref, centred_ref, weight_ref, grad_ref, keep_ref, got_ref, out_ref
):
    width = events_ref.shape[1]
    heads = weight_ref.shape[0]
    chips, depth, columns = out_ref.shape
    half = keep_ref.shape[1]
    lanes = columns - half
    weight_sum = keep_ref[...].astype(F32) + got_ref[...].astype(F32)
    out_ref[:, :, :half] = weight_sum.reshape(chips, depth, half).astype(BF16)
    rows = slot_rows(user_ref, day_ref, users, slots)
    grad = tn(rows, to_rows(grad_ref[...], width))
    terms = (grad * centred_ref[...].astype(F32)).astype(BF16)
    reduce = one_hot(iota((lanes, width), 1) // (width // heads) == iota((lanes, width), 0) % heads)
    weight = jnp.concatenate([weight_ref[...]] * (lanes // heads), axis=0)
    scores = (weight * nt(reduce, terms)).astype(BF16)
    spread = nn(scores, events_ref[...])
    keep = (iota((lanes, width), 1) // depth) % cores == iota((lanes, width), 0) // heads
    turned = jnp.transpose(jnp.where(keep, spread, 0.0), (1, 0))
    out_ref[:, :, half:] = jnp.sum(turned.reshape(chips, cores, depth, lanes), axis=1).astype(BF16)


def merge_kernel(x_ref, out_ref):
    total = jnp.sum(x_ref[...].astype(F32), axis=0).astype(BF16)
    for i in range(out_ref.shape[0]):
        out_ref[i] = total


def final_kernel(cores, core_ref, x_ref, weight_ref, score_ref):
    half = weight_ref.shape[1] // 2
    heads = score_ref.shape[1]
    groups = x_ref.shape[0] // cores
    core = core_ref[0]
    mine = [x_ref[cores * r + core].astype(F32) for r in range(groups)]
    weight_ref[:, :half] = sum(m[:, :half] for m in mine[0::2])
    weight_ref[:, half:] = sum(m[:, :half] for m in mine[1::2])
    score = jnp.sum(x_ref[:, :, half:].astype(F32), axis=0)
    lanes = score.shape[1]
    pick = one_hot(iota((lanes, heads), 0) == iota((lanes, heads), 1) + core * heads)
    depth = score.shape[0]
    pieces = nn(split3(score), pick)
    score_ref[...] = pieces[:depth] + pieces[depth : 2 * depth] + pieces[2 * depth :]


def call(kernel, outs, args, scalars=0, flops=0, whole=(), scratch=(), limit=24):
    vmem = pl.BlockSpec(memory_space=pltpu.VMEM)
    smem = pl.BlockSpec(memory_space=pltpu.SMEM)
    anywhere = pl.BlockSpec(memory_space=pl.ANY)
    specs = [smem if i < scalars else anywhere if i in whole else vmem for i in range(len(args))]
    moved = sum(a.size * a.dtype.itemsize for a in args) + sum(math.prod(s) * jnp.dtype(t).itemsize for s, t in outs)
    return pl.pallas_call(
        kernel,
        out_shape=[jax.ShapeDtypeStruct(s, t) for s, t in outs],
        in_specs=specs,
        out_specs=[vmem] * len(outs),
        scratch_shapes=scratch,
        compiler_params=pltpu.CompilerParams(vmem_limit_bytes=limit * 2**20),
        cost_estimate=pl.CostEstimate(flops=flops, bytes_accessed=moved, transcendentals=0),
    )(*args)


def shards(sizes, events, event_user, event_day, score_weight, value_weight, qkv_weight, cotangent):
    groups, x_size, z_size, cores = sizes
    chips = x_size * z_size
    buckets = chips * cores
    user_dev, days, width = cotangent.shape
    heads = score_weight.shape[1]
    day_dev = days // buckets
    users = user_dev * buckets
    slots = users * day_dev
    count = events.shape[0]
    rows = width // buckets
    half = 3 * width // 2
    loss_scale = 1.0 / math.sqrt(user_dev * buckets * groups * days)
    user_row = event_user.reshape(1, count)
    day_row = event_day.reshape(1, count)
    core = lax.axis_index("core").reshape(1)
    parity = (lax.axis_index("rep") % 2).reshape(1)

    block = ((buckets, day_dev * width // 128, 128), BF16)
    summary, weight = call(
        functools.partial(pool_kernel, users, slots),
        [block, ((heads, count), F32)],
        (user_row, day_row, score_weight, events, value_weight),
        flops=2 * count * width * (width + slots),
        whole=(3, 4),
        scratch=[pltpu.VMEM((count, width), BF16), pltpu.VMEM((width, width), BF16), pltpu.SemaphoreType.DMA((12,))],
        limit=60,
    )
    by_user = lax.all_to_all(summary, DAY, split_axis=0, concat_axis=0, tiled=True)
    (centred,) = call(
        functools.partial(centre_kernel, users, slots),
        [((count, width), BF16)],
        (user_row, day_row, events, value_weight, summary),
        flops=2 * count * width * (width + slots),
    )
    grad_summary, normed, grad_qkv = call(
        functools.partial(attention_kernel, heads, loss_scale),
        [block, ((days, width), BF16), ((days, 3 * width), BF16)],
        (by_user, cotangent.reshape(days, width), qkv_weight),
        flops=2 * days * width * (6 * width + 14 * days),
    )
    grad_days = lax.all_to_all(grad_summary, DAY, split_axis=0, concat_axis=0, tiled=True)
    mine, other = call(
        functools.partial(outer_kernel, rows),
        [((width // 2, 3 * width), BF16)] * 2,
        (core, normed, grad_qkv),
        scalars=1,
        flops=2 * days * width * 3 * width,
    )
    theirs = lax.ppermute(other, "core", [(i, cores - 1 - i) for i in range(cores)])
    keep, send = call(fold_kernel, [((width // 2, half), BF16)] * 2, (parity, mine, theirs), scalars=1)
    got = lax.ppermute(send, "rep", [(i, i ^ 1) for i in range(groups)])
    (partial_sums,) = call(
        functools.partial(score_kernel, users, slots, cores),
        [((chips, rows, half + 128), BF16)],
        (user_row, day_row, events, centred, weight, grad_days, keep, got),
        flops=2 * count * width * (slots + 256),
    )
    plane = lax.all_to_all(partial_sums, ("x", "z"), split_axis=0, concat_axis=0, tiled=True)
    (merged,) = call(merge_kernel, [((groups * cores, rows, half + 128), BF16)], (plane,))
    everyone = lax.all_to_all(merged, ("rep", "core"), split_axis=0, concat_axis=0, tiled=True)
    return tuple(
        call(
            functools.partial(final_kernel, cores),
            [((rows, 3 * width), F32), ((rows, heads), F32)],
            (core, everyone),
            scalars=1,
        )
    )


def solution(mesh):
    sizes = (8, 4, 8, 2)
    split = Mesh(mesh.devices.reshape(sizes), ("rep",) + DAY)
    whole = ("rep",) + DAY
    in_specs = (P(whole, None), P(whole), P(whole), P(), P(), P(), P(whole, None, None))
    out_specs = (P(DAY, None), P(DAY, None))
    return jax.shard_map(
        functools.partial(shards, sizes), mesh=split, in_specs=in_specs, out_specs=out_specs, check_vma=False
    )
```

time: 127 us -> 109 us (0.86)
  the two profiles are of different devices: /device:TPU:64 before, /device:TPU:1 now
where the time goes in v2:
time: 109 us; the launch traced here: 108 us
  blocking collectives  44 us (40%)
  starting transfers between devices  26.2 us (24%)
  waiting for transfers between devices  20.1 us (18%)
  Pallas kernels  15.6 us (14%)
  local copies, waits for them, and re-layouts  1.52 us (1%)
    all_to_all x1, blocking collectives, shards(): lax.all_to_all(merged, ('rep', 'core'), split_axis=0, concat_axis=0, tile...  22.4 us
    all_to_all x1, blocking collectives, shards(): lax.all_to_all(partial_sums, ('x', 'z'), split_axis=0, concat_axis=0, til...  21.6 us
    pallas_call x8, Pallas kernels, call(): pl.pallas_call(kernel, out_shape=[jax.ShapeDtypeStruct(s, t) for s, t in...  15.6 us
    all_to_all x1, starting transfers between devices, shards(): lax.all_to_all(summary, DAY, split_axis=0, concat_axis=0, tiled=True)  14.9 us
    all_to_all x1, waiting for transfers between devices, shards(): lax.all_to_all(summary, DAY, split_axis=0, concat_axis=0, tiled=True)  12 us
    all_to_all x1, waiting for transfers between devices, shards(): lax.all_to_all(grad_summary, DAY, split_axis=0, concat_axis=0, tiled=True)  6.42 us
    all_to_all x1, starting transfers between devices, shards(): lax.all_to_all(grad_summary, DAY, split_axis=0, concat_axis=0, tiled=True)  5.68 us
    ppermute x1, starting transfers between devices, shards(): got = lax.ppermute(send, 'rep', [(i, i ^ 1) for i in range(groups)])  3.34 us
  transfers between devices with their start and end apart: 4, of which 3 were waited for; matrix products, arithmetic and copies ran while one was open for 0% of the time, Pallas kernels for 2%

profile of v2, /device:TPU:1, one launch (start us, length us, event | category | flops | bytes accessed | tf_op | source)
XLA Modules:
  0.0 108.3 jit_solution(14116551712478768316)
XLA Ops:
  0.6 1.5 %copy.9.score_ref = bf16[512,8]{1,0:T(8,128)(2,1)} copy(bf16[512,8]{0,1:T(8,128)(2,1)} %param.10) | data formatting | bytes 16384 | tf_op args[3]
  2.1 0.0 copy-start.5
  2.1 0.0 copy-start.7
  2.1 5.3 %shard_map.86 = (bf16[64,16,128]{2,1,0:T(8,128)(2,1)}, f32[8,1024]{1,0:T(8,128)}) custom-call(s32[1,1024]{1,0:T(1,128)} %bitcast.5, s32[1,1024]{1,0:T(1,128)} %bitcast.8, bf16[512,8]{1,0:T(8,128)(2,1)} %copy.9.score_ref, bf16[1024,512]{1,0:T(8,128)(2,1)} %events_ref.5, bf16[512,512]{1,0:T(8,128)(2,1)} %value_ref.3), custom_call_target="tpu_custom_call" | custom-call | flops 805306368 | bytes 1884160 | tf_op jit(solution)/shard_map/pallas_call | solution.py:238
  7.4 14.9 %all-to-all-start = ((bf16[64,16,128]{2,1,0:T(8,128)(2,1)}), bf16[64,16,128]{2,1,0:T(8,128)(2,1)S(1)}, u32[]{:S(2)}, u32[]{:S(2)}) async-start(bf16[64,16,128]{2,1,0:T(8,128)(2,1)} %get-tuple-element.11.summary_ref), calls=%async_computation | async-start | bytes 524288 | tf_op jit(solution)/shard_map/all_to_all | solution.py:277
  22.3 12.0 %all-to-all-done.x_ref = bf16[64,16,128]{2,1,0:T(8,128)(2,1)S(1)} async-done(((bf16[64,16,128]{2,1,0:T(8,128)(2,1)}), bf16[64,16,128]{2,1,0:T(8,128)(2,1)S(1)}, u32[]{:S(2)}, u32[]{:S(2)}) %all-to-all-start) | async-done | bytes 262176 | tf_op jit(solution)/shard_map/all_to_all | solution.py:277
  34.3 0.0 copy-done.5
  34.3 0.0 copy-done.7
  34.3 4.6 %shard_map.88 = (bf16[64,16,128]{2,1,0:T(8,128)(2,1)}, bf16[256,512]{1,0:T(8,128)(2,1)S(1)}, bf16[256,1536]{1,0:T(8,128)(2,1)S(1)}) custom-call(bf16[64,16,128]{2,1,0:T(8,128)(2,1)S(1)} %all-to-all-done.x_ref, bf16[256,512]{1,0:T(8,128)(2,1)S(1)} %bitcast.11, bf16[512,1536]{1,0:T(8,128)(2,1)S(1)} %copy-done.5), custom_call_target="tpu_custom_call" | custom-call | flops 1744830464 | bytes 3407872 | tf_op jit(solution)/shard_map/pallas_call | solution.py:238
  38.8 0.0 copy-start
  38.8 0.0 copy-start.1
  38.9 1.6 %shard_map.89 = (bf16[256,1536]{1,0:T(8,128)(2,1)S(1)}, bf16[256,1536]{1,0:T(8,128)(2,1)}) custom-call(s32[1]{0:T(128)} %bitcast.core_ref, bf16[256,512]{1,0:T(8,128)(2,1)S(1)} %get-tuple-element.14.normed_ref, bf16[256,1536]{1,0:T(8,128)(2,1)S(1)} %get-tuple-element.15.grad_qkv_ref), custom_call_target="tpu_custom_call" | custom-call | flops 402653184 | bytes 2621444 | tf_op jit(solution)/shard_map/pallas_call | solution.py:238
  40.5 2.4 %collective-permute-start = (bf16[256,1536]{1,0:T(8,128)(2,1)}, bf16[256,1536]{1,0:T(8,128)(2,1)S(1)}, u32[]{:S(2)}, u32[]{:S(2)}) collective-permute-start(bf16[256,1536]{1,0:T(8,128)(2,1)} %get-tuple-element.17), channel_id=1, source_target_pairs={{0,1},{1,0},{2,3},{3,2},{4,5},{5,4},{6,7},{7,6},{8,9},{9,8},{10,11... | collective-permute-start | bytes 2359304 | tf_op jit(solution)/shard_map/ppermute | solution.py:298
  42.9 5.7 %all-to-all-start.1 = ((bf16[64,16,128]{2,1,0:T(8,128)(2,1)}), bf16[64,16,128]{2,1,0:T(8,128)(2,1)S(1)}, u32[]{:S(2)}, u32[]{:S(2)}) async-start(bf16[64,16,128]{2,1,0:T(8,128)(2,1)} %get-tuple-element.13), calls=%async_computation.1 | async-start | bytes 524288 | tf_op jit(solution)/shard_map/all_to_all | solution.py:290
  48.6 0.0 copy-start.6
  48.6 0.0 collective-permute-done.theirs_ref
  48.6 1.2 %shard_map.90 = (bf16[256,768]{1,0:T(8,128)(2,1)S(1)}, bf16[256,768]{1,0:T(8,128)(2,1)}) custom-call(s32[1]{0:T(128)} %bitcast.4.row_ref, bf16[256,1536]{1,0:T(8,128)(2,1)S(1)} %get-tuple-element.16.mine_ref, bf16[256,1536]{1,0:T(8,128)(2,1)S(1)} %collective-permute-done.theirs_ref), custom_call_target="tpu_custom_call" | custom-call | bytes 2359300 | tf_op jit(solution)/shard_map/pallas_call | solution.py:238
  49.8 3.3 %collective-permute-start.1 = (bf16[256,768]{1,0:T(8,128)(2,1)}, bf16[256,768]{1,0:T(8,128)(2,1)S(1)}, u32[]{:S(2)}, u32[]{:S(2)}) collective-permute-start(bf16[256,768]{1,0:T(8,128)(2,1)} %get-tuple-element.19), channel_id=1, source_target_pairs={{0,64},{64,0},{128,192},{192,128},{256,320},{320,256},{384,448},{4... | collective-permute-start | bytes 1179656 | tf_op jit(solution)/shard_map/ppermute | solution.py:300
  53.1 0.0 copy-done
  53.1 0.0 copy-done.1
  53.1 0.0 copy-done.3
  53.1 0.0 copy-done.4
  53.1 0.0 copy-done.6
  53.2 1.0 shard_map.87.centred_ref
  54.1 6.4 %all-to-all-done.1.grad_ref = bf16[64,16,128]{2,1,0:T(8,128)(2,1)S(1)} async-done(((bf16[64,16,128]{2,1,0:T(8,128)(2,1)}), bf16[64,16,128]{2,1,0:T(8,128)(2,1)S(1)}, u32[]{:S(2)}, u32[]{:S(2)}) %all-to-all-start.1) | async-done | bytes 262176 | tf_op jit(solution)/shard_map/all_to_all | solution.py:290
  60.6 1.6 %collective-permute-done.1.got_ref = bf16[256,768]{1,0:T(8,128)(2,1)S(1)} collective-permute-done((bf16[256,768]{1,0:T(8,128)(2,1)}, bf16[256,768]{1,0:T(8,128)(2,1)S(1)}, u32[]{:S(2)}, u32[]{:S(2)}) %collective-permute-start.1) | collective-permute-done | bytes 393248 | tf_op jit(solution)/shard_map/ppermute | solution.py:300
  62.2 0.0 copy-done.2
  62.2 1.2 %shard_map.91 = bf16[32,8,896]{2,1,0:T(8,128)(2,1)S(1)} custom-call(s32[1,1024]{1,0:T(1,128)S(1)} %bitcast.7, s32[1,1024]{1,0:T(1,128)S(1)} %bitcast.10, bf16[1024,512]{1,0:T(8,128)(2,1)S(1)} %copy-done, bf16[1024,512]{1,0:T(8,128)(2,1)S(1)} %shard_map.87.centred_ref, f32[8,1024]{1,0:T(8,128)S(1)} %copy-done.2, ...), custom_call_target="tpu_custom_call" | custom-call | flops 536870912 | bytes 3645440 | tf_op jit(solution)/shard_map/pallas_call | solution.py:238
  63.4 21.6 %all_to_all.20.x_ref = bf16[32,8,896]{2,1,0:T(8,128)(2,1)S(1)} all-to-all(bf16[32,8,896]{2,1,0:T(8,128)(2,1)S(1)} %shard_map.91), channel_id=1, replica_groups=mesh['rep'=8,'x'=4,'z'=8,'core'=2] {'x','z'}, dimensions={0} | all-to-all | bytes 917504 | tf_op jit(solution)/shard_map/all_to_all | solution.py:307
  85.1 0.1 shard_map.92
  85.1 22.4 %all_to_all.21.x_ref = bf16[16,8,896]{2,1,0:T(8,128)(2,1)S(1)} all-to-all(bf16[16,8,896]{2,1,0:T(8,128)(2,1)S(1)} %shard_map.92), channel_id=1, replica_groups=mesh['rep'=8,'x'=4,'z'=8,'core'=2] {'rep','core'}, dimensions={0} | all-to-all | bytes 458752 | tf_op jit(solution)/shard_map/all_to_all | solution.py:309
  107.5 0.7 shard_map.93
  (3 shorter events, 0.0 us)
Async XLA Ops:
  2.1 32.2 %copy-start.5 = (bf16[512,1536]{1,0:T(8,128)(2,1)S(1)}, bf16[512,1536]{1,0:T(8,128)(2,1)}, u32[]{:S(2)}) copy-start(bf16[512,1536]{1,0:T(8,128)(2,1)} %qkv_weight_ref.1) | copy-start | bytes 4718596
  2.1 32.2 %copy-start.7 = (bf16[1,256,512]{2,1,0:T(8,128)(2,1)S(1)}, bf16[1,256,512]{2,1,0:T(8,128)(2,1)}, u32[]{:S(2)}) copy-start(bf16[1,256,512]{2,1,0:T(8,128)(2,1)} %param.13) | copy-start | bytes 786436
  7.4 26.9 %all-to-all-start = ((bf16[64,16,128]{2,1,0:T(8,128)(2,1)}), bf16[64,16,128]{2,1,0:T(8,128)(2,1)S(1)}, u32[]{:S(2)}, u32[]{:S(2)}) async-start(bf16[64,16,128]{2,1,0:T(8,128)(2,1)} %get-tuple-element.11.summary_ref), calls=%async_computation | async-start | bytes 524288 | tf_op jit(solution)/shard_map/all_to_all | solution.py:277
  38.8 14.3 %copy-start = (bf16[1024,512]{1,0:T(8,128)(2,1)S(1)}, bf16[1024,512]{1,0:T(8,128)(2,1)}, u32[]{:S(2)}) copy-start(bf16[1024,512]{1,0:T(8,128)(2,1)} %events_ref.5) | copy-start | bytes 3145732
  38.8 14.3 %copy-start.1 = (bf16[64,16,128]{2,1,0:T(8,128)(2,1)S(1)}, bf16[64,16,128]{2,1,0:T(8,128)(2,1)}, u32[]{:S(2)}) copy-start(bf16[64,16,128]{2,1,0:T(8,128)(2,1)} %get-tuple-element.11.summary_ref) | copy-start | bytes 786436
  38.8 14.3 %copy-start.3 = (s32[1024]{0:T(1024)S(1)}, s32[1024]{0:T(1024)}, u32[]{:S(2)}) copy-start(s32[1024]{0:T(1024)} %param.8) | copy-start | bytes 12292
  38.8 14.3 %copy-start.4 = (s32[1024]{0:T(1024)S(1)}, s32[1024]{0:T(1024)}, u32[]{:S(2)}) copy-start(s32[1024]{0:T(1024)} %param.9) | copy-start | bytes 12292
  40.5 8.1 %collective-permute-start = (bf16[256,1536]{1,0:T(8,128)(2,1)}, bf16[256,1536]{1,0:T(8,128)(2,1)S(1)}, u32[]{:S(2)}, u32[]{:S(2)}) collective-permute-start(bf16[256,1536]{1,0:T(8,128)(2,1)} %get-tuple-element.17), channel_id=1, source_target_pairs={{0,1},{1,0},{2,3},{3,2},{4,5},{5,4},{6,7},{7,6},{8,9},{9,8},{10,11... | collective-permute-start | bytes 2359304 | tf_op jit(solution)/shard_map/ppermute | solution.py:298
  42.9 17.7 %all-to-all-start.1 = ((bf16[64,16,128]{2,1,0:T(8,128)(2,1)}), bf16[64,16,128]{2,1,0:T(8,128)(2,1)S(1)}, u32[]{:S(2)}, u32[]{:S(2)}) async-start(bf16[64,16,128]{2,1,0:T(8,128)(2,1)} %get-tuple-element.13), calls=%async_computation.1 | async-start | bytes 524288 | tf_op jit(solution)/shard_map/all_to_all | solution.py:290
  48.6 4.6 %copy-start.6 = (bf16[512,512]{1,0:T(8,128)(2,1)S(1)}, bf16[512,512]{1,0:T(8,128)(2,1)}, u32[]{:S(2)}) copy-start(bf16[512,512]{1,0:T(8,128)(2,1)} %value_ref.3) | copy-start | bytes 1572868
  49.8 12.5 %copy-start.2 = (f32[8,1024]{1,0:T(8,128)S(1)}, f32[8,1024]{1,0:T(8,128)}, u32[]{:S(2)}) copy-start(f32[8,1024]{1,0:T(8,128)} %get-tuple-element.12.weight_ref) | copy-start | bytes 98308
  49.8 12.5 %collective-permute-start.1 = (bf16[256,768]{1,0:T(8,128)(2,1)}, bf16[256,768]{1,0:T(8,128)(2,1)S(1)}, u32[]{:S(2)}, u32[]{:S(2)}) collective-permute-start(bf16[256,768]{1,0:T(8,128)(2,1)} %get-tuple-element.19), channel_id=1, source_target_pairs={{0,64},{64,0},{128,192},{192,128},{256,320},{320,256},{384,448},{4... | collective-permute-start | bytes 1179656 | tf_op jit(solution)/shard_map/ppermute | solution.py:300

commit v3 on v2

--- a/solution.py
+++ b/solution.py
@@ -57,62 +57,75 @@
 
 
 def to_rows(x, width):
-    return x.astype(F32).reshape(x.size // width, width).astype(BF16)
+    blocks, depth, lanes = x.shape
+    parts = width // lanes
+    x = x.astype(F32).reshape(blocks, parts, depth // parts, lanes)
+    return jnp.concatenate([x[:, i].reshape(-1, lanes) for i in range(parts)], axis=1)
 
 
 def to_blocks(x, blocks):
-    return x.reshape(blocks, x.size // (blocks * 128), 128).astype(BF16)
+    parts = x.shape[1] // 128
+    x = x.astype(F32)
+    pieces = [x[:, i * 128 : (i + 1) * 128].reshape(blocks, -1, 128) for i in range(parts)]
+    return jnp.concatenate(pieces, axis=1).astype(BF16)
 
 
 def pool_kernel(
-    users, slots, user_ref, day_ref, score_ref, events_ref, value_ref, summary_ref, weight_ref, events_buf, value_buf, sems
+    users, slots, user_ref, day_ref, score_ref, events_ref, value_ref, summary_ref, weight_ref,
+    events_buf, value_buf, value_sem, event_sems,
 ):
-    width, heads = score_ref.shape
-    count = events_ref.shape[0]
-    copies = []
-    for source, target, parts in ((events_ref, events_buf, 8), (value_ref, value_buf, 4)):
-        step = source.shape[0] // parts
-        for i in range(parts):
-            piece = pl.ds(i * step, step)
-            copies.append(pltpu.make_async_copy(source.at[piece, :], target.at[piece, :], sems.at[len(copies)]))
+    heads, width = score_ref.shape
+    steps = event_sems.shape[0]
+    step = events_ref.shape[0] // steps
+    value_copy = pltpu.make_async_copy(value_ref, value_buf, value_sem)
+    pieces = [pl.ds(i * step, step) for i in range(steps)]
+    copies = [
+        pltpu.make_async_copy(events_ref.at[piece, :], events_buf.at[piece, :], event_sems.at[i])
+        for i, piece in enumerate(pieces)
+    ]
+    value_copy.start()
     for copy in copies:
         copy.start()
     rows = slot_rows(user_ref, day_ref, users, slots)
-    eye = one_hot(iota((heads, heads), 0) == iota((heads, heads), 1))
-    score_t = nt(eye, score_ref[...]).astype(BF16)
     expand = one_hot(iota((3 * heads, width), 1) // (width // heads) == iota((3 * heads, width), 0) % heads)
-    for copy in copies[:8]:
-        copy.wait()
-    events = events_buf[...]
-    exponent = jnp.exp(nt(score_t, events))
+    score = score_ref[...]
+    value_copy.wait()
+    value = value_buf[...]
+    logits, values = [], []
+    for i in range(steps):
+        copies[i].wait()
+        part = events_buf[pieces[i], :]
+        logits.append(nt(score, part))
+        values.append(nn(part, value))
+    exponent = jnp.exp(jnp.concatenate(logits, axis=1))
     denominator = join3(nt(split3(exponent), rows))
     weight = exponent / join3(nn(split3(denominator), rows))
     weight_ref[...] = weight
-    for copy in copies[8:]:
-        copy.wait()
-    values = nn(events, value_buf[...])
-    weighted = (values * tn(split3(weight), expand)).astype(BF16)
+    weighted = (jnp.concatenate(values, axis=0) * tn(split3(weight), expand)).astype(BF16)
     summary_ref[...] = to_blocks(nn(rows, weighted), users)
 
 
 def centre_kernel(users, slots, user_ref, day_ref, events_ref, value_ref, summary_ref, out_ref):
     rows = slot_rows(user_ref, day_ref, users, slots)
-    pooled = to_rows(summary_ref[...], value_ref.shape[1])
+    pooled = to_rows(summary_ref[...], value_ref.shape[1]).astype(BF16)
     values = nn(events_ref[...], value_ref[...])
     out_ref[...] = (values - tn(rows, pooled)).astype(BF16)
 
 
-def attention_kernel(heads, loss_scale, x_ref, cot_ref, qkv_weight_ref, grad_ref, normed_ref, grad_qkv_ref):
+def attention_kernel(heads, loss_scale, x_ref, cot_ref, qkv_weight_ref, grad_ref, pack_ref, pack_buf, sems):
     width = qkv_weight_ref.shape[0]
     days = cot_ref.shape[0]
     buckets = x_ref.shape[0]
     size = width // heads
     causal = iota((days, days), 1) <= iota((days, days), 0)
     cot = cot_ref[...]
-    wide = to_rows(x_ref[...], width).astype(F32)
+    wide = to_rows(x_ref[...], width)
     inverse = lax.rsqrt(jnp.mean(wide * wide, axis=-1, keepdims=True) + 1e-06)
     normed = (wide * inverse).astype(BF16)
-    normed_ref[...] = normed
+    pieces = [pl.ds(i * width, width) for i in range(4)]
+    copies = [pltpu.make_async_copy(pack_buf.at[:, p], pack_ref.at[:, p], sems.at[i]) for i, p in enumerate(pieces)]
+    pack_buf[:, pieces[0]] = normed
+    copies[0].start()
     qkv = nn(normed, qkv_weight_ref[...]).astype(BF16)
     pair = 2 * size
     left = iota((days, pair), 1) < size
@@ -140,7 +153,9 @@
         parts[1].append(tn(jnp.concatenate(logits_grad, 0), jnp.concatenate(q2, 0)))
         parts[2].append(tn(jnp.concatenate(probs, 0), jnp.concatenate(c2, 0)) * loss_scale)
     grad_qkv = jnp.concatenate([a.astype(BF16) for part in parts for a in part], axis=1)
-    grad_qkv_ref[...] = grad_qkv
+    pack_buf[:, width:] = grad_qkv
+    for copy in copies[1:]:
+        copy.start()
     grad_normed = nt(grad_qkv, qkv_weight_ref[...])
     cubed = inverse * inverse * inverse
     grad = (
@@ -149,54 +164,40 @@
         - wide * cubed * jnp.mean(grad_normed * wide, axis=-1, keepdims=True)
     )
     grad_ref[...] = to_blocks(grad, buckets)
-
-
-def outer_kernel(rows, core_ref, normed_ref, grad_qkv_ref, mine_ref, other_ref):
-    width, columns = normed_ref.shape[1], grad_qkv_ref.shape[1]
-    product = tn(normed_ref[...], grad_qkv_ref[...]).reshape(width // (2 * rows), 2, rows, columns)
-    even = product[:, 0].reshape(width // 2, columns).astype(BF16)
-    odd = product[:, 1].reshape(width // 2, columns).astype(BF16)
-    first = core_ref[0] == 0
-
-    @pl.when(first)
-    def _():
-        mine_ref[...] = even
-        other_ref[...] = odd
-
-    @pl.when(jnp.logical_not(first))
-    def _():
-        mine_ref[...] = odd
-        other_ref[...] = even
-
-
-def fold_kernel(row_ref, mine_ref, theirs_ref, keep_ref, send_ref):
-    half = keep_ref.shape[1]
-    total = (mine_ref[...].astype(F32) + theirs_ref[...].astype(F32)).astype(BF16)
-    first = row_ref[0] == 0
-
-    @pl.when(first)
-    def _():
-        keep_ref[...] = total[:, :half]
-        send_ref[...] = total[:, half:]
-
-    @pl.when(jnp.logical_not(first))
-    def _():
-        keep_ref[...] = total[:, half:]
-        send_ref[...] = total[:, :half]
+    for copy in copies:
+        copy.wait()
+
+
+def outer_kernel(depth, core_ref, row_ref, mine_ref, theirs_ref, keep_ref, up_ref, down_ref):
+    quarter = up_ref.shape[1]
+    width = mine_ref.shape[1] - 4 * quarter
+    count = width // 2
+    both = jnp.concatenate([mine_ref[...], theirs_ref[...]], axis=0)
+    column = iota((width, count), 1)
+    pick = one_hot(iota((width, count), 0) == (2 * (column // depth) + core_ref[0]) * depth + column % depth)
+    total = tn(nn(both[:, :width], pick).astype(BF16), both[:, width:]).astype(BF16)
+    first = row_ref[0] & 1 == 0
+    for side, send_ref in ((0, up_ref), (1, down_ref)):
+        low = total[:, 2 * side * quarter : (2 * side + 1) * quarter]
+        high = total[:, (2 * side + 1) * quarter : (2 * side + 2) * quarter]
+        keep_ref[:, side * quarter : (side + 1) * quarter] = jnp.where(first, low, high)
+        send_ref[...] = jnp.where(first, high, low)
 
 
 def score_kernel(
-    users, slots, cores, user_ref, day_ref, events_ref, centred_ref, weight_ref, grad_ref, keep_ref, got_ref, out_ref
+    users, slots, cores, user_ref, day_ref, events_ref, centred_ref, weight_ref, grad_ref, keep_ref, up_ref, down_ref, out_ref
 ):
     width = events_ref.shape[1]
     heads = weight_ref.shape[0]
     chips, depth, columns = out_ref.shape
     half = keep_ref.shape[1]
     lanes = columns - half
-    weight_sum = keep_ref[...].astype(F32) + got_ref[...].astype(F32)
-    out_ref[:, :, :half] = weight_sum.reshape(chips, depth, half).astype(BF16)
+    quarter = half // 2
+    for start, got_ref in ((0, up_ref), (quarter, down_ref)):
+        weight_sum = keep_ref[:, start : start + quarter].astype(F32) + got_ref[...].astype(F32)
+        out_ref[:, :, start : start + quarter] = weight_sum.reshape(chips, depth, quarter).astype(BF16)
     rows = slot_rows(user_ref, day_ref, users, slots)
-    grad = tn(rows, to_rows(grad_ref[...], width))
+    grad = tn(rows, to_rows(grad_ref[...], width).astype(BF16))
     terms = (grad * centred_ref[...].astype(F32)).astype(BF16)
     reduce = one_hot(iota((lanes, width), 1) // (width // heads) == iota((lanes, width), 0) % heads)
     weight = jnp.concatenate([weight_ref[...]] * (lanes // heads), axis=0)
@@ -219,8 +220,11 @@
     groups = x_ref.shape[0] // cores
     core = core_ref[0]
     mine = [x_ref[cores * r + core].astype(F32) for r in range(groups)]
-    weight_ref[:, :half] = sum(m[:, :half] for m in mine[0::2])
-    weight_ref[:, half:] = sum(m[:, :half] for m in mine[1::2])
+    quarter = half // 2
+    for side in range(2):
+        for bit in range(2):
+            held = [m[:, side * quarter : (side + 1) * quarter] for r, m in enumerate(mine) if r % 2 == bit]
+            weight_ref[:, (2 * side + bit) * quarter : (2 * side + bit + 1) * quarter] = sum(held)
     score = jnp.sum(x_ref[:, :, half:].astype(F32), axis=0)
     lanes = score.shape[1]
     pick = one_hot(iota((lanes, heads), 0) == iota((lanes, heads), 1) + core * heads)
@@ -229,17 +233,18 @@
     score_ref[...] = pieces[:depth] + pieces[depth : 2 * depth] + pieces[2 * depth :]
 
 
-def call(kernel, outs, args, scalars=0, flops=0, whole=(), scratch=(), limit=24):
+def call(kernel, outs, args, scalars=0, flops=0, moved=None, whole=(), out_whole=(), scratch=(), limit=24):
     vmem = pl.BlockSpec(memory_space=pltpu.VMEM)
     smem = pl.BlockSpec(memory_space=pltpu.SMEM)
-    anywhere = pl.BlockSpec(memory_space=pl.ANY)
+    anywhere = pl.BlockSpec(memory_space=pltpu.HBM)
     specs = [smem if i < scalars else anywhere if i in whole else vmem for i in range(len(args))]
-    moved = sum(a.size * a.dtype.itemsize for a in args) + sum(math.prod(s) * jnp.dtype(t).itemsize for s, t in outs)
+    if moved is None:
+        moved = sum(a.size * a.dtype.itemsize for a in args) + sum(math.prod(s) * jnp.dtype(t).itemsize for s, t in outs)
     return pl.pallas_call(
         kernel,
-        out_shape=[jax.ShapeDtypeStruct(s, t) for s, t in outs],
+        out_shape=[pltpu.HBM(s, t) if i in out_whole else jax.ShapeDtypeStruct(s, t) for i, (s, t) in enumerate(outs)],
         in_specs=specs,
-        out_specs=[vmem] * len(outs),
+        out_specs=[anywhere if i in out_whole else vmem for i in range(len(outs))],
         scratch_shapes=scratch,
         compiler_params=pltpu.CompilerParams(vmem_limit_bytes=limit * 2**20),
         cost_estimate=pl.CostEstimate(flops=flops, bytes_accessed=moved, transcendentals=0),
@@ -262,16 +267,21 @@
     user_row = event_user.reshape(1, count)
     day_row = event_day.reshape(1, count)
     core = lax.axis_index("core").reshape(1)
-    parity = (lax.axis_index("rep") % 2).reshape(1)
+    row = lax.axis_index("rep").reshape(1)
 
     block = ((buckets, day_dev * width // 128, 128), BF16)
     summary, weight = call(
         functools.partial(pool_kernel, users, slots),
         [block, ((heads, count), F32)],
-        (user_row, day_row, score_weight, events, value_weight),
+        (user_row, day_row, score_weight.T, events, value_weight),
         flops=2 * count * width * (width + slots),
         whole=(3, 4),
-        scratch=[pltpu.VMEM((count, width), BF16), pltpu.VMEM((width, width), BF16), pltpu.SemaphoreType.DMA((12,))],
+        scratch=[
+            pltpu.VMEM((count, width), BF16),
+            pltpu.VMEM((width, width), BF16),
+            pltpu.SemaphoreType.DMA,
+            pltpu.SemaphoreType.DMA((4,)),
+        ],
         limit=60,
     )
     by_user = lax.all_to_all(summary, DAY, split_axis=0, concat_axis=0, tiled=True)
@@ -281,27 +291,29 @@
         (user_row, day_row, events, value_weight, summary),
         flops=2 * count * width * (width + slots),
     )
-    grad_summary, normed, grad_qkv = call(
+    grad_summary, mine = call(
         functools.partial(attention_kernel, heads, loss_scale),
-        [block, ((days, width), BF16), ((days, 3 * width), BF16)],
+        [block, ((days, 4 * width), BF16)],
         (by_user, cotangent.reshape(days, width), qkv_weight),
         flops=2 * days * width * (6 * width + 14 * days),
+        out_whole=(1,),
+        scratch=[pltpu.VMEM((days, 4 * width), BF16), pltpu.SemaphoreType.DMA((4,))],
     )
     grad_days = lax.all_to_all(grad_summary, DAY, split_axis=0, concat_axis=0, tiled=True)
-    mine, other = call(
+    theirs = lax.ppermute(mine, "core", [(i, cores - 1 - i) for i in range(cores)])
+    keep, send_up, send_down = call(
         functools.partial(outer_kernel, rows),
-        [((width // 2, 3 * width), BF16)] * 2,
-        (core, normed, grad_qkv),
-        scalars=1,
-        flops=2 * days * width * 3 * width,
-    )
-    theirs = lax.ppermute(other, "core", [(i, cores - 1 - i) for i in range(cores)])
-    keep, send = call(fold_kernel, [((width // 2, half), BF16)] * 2, (parity, mine, theirs), scalars=1)
-    got = lax.ppermute(send, "rep", [(i, i ^ 1) for i in range(groups)])
+        [((width // 2, half), BF16)] + [((width // 2, half // 2), BF16)] * 2,
+        (core, row, mine, theirs),
+        scalars=2,
+        moved=0,
+    )
+    up = lax.ppermute(send_up, "rep", [(i, i ^ 1) for i in range(groups)])
+    down = lax.ppermute(send_down, "rep", [(i, (((i + 1) ^ 1) - 1) % groups) for i in range(groups)])
     (partial_sums,) = call(
         functools.partial(score_kernel, users, slots, cores),
         [((chips, rows, half + 128), BF16)],
-        (user_row, day_row, events, centred, weight, grad_days, keep, got),
+        (user_row, day_row, events, centred, weight, grad_days, keep, up, down),
         flops=2 * count * width * (slots + 256),
     )
     plane = lax.all_to_all(partial_sums, ("x", "z"), split_axis=0, concat_axis=0, tiled=True)

time: 109 us -> 107 us (0.982)
  blocking collectives: 44 us -> 69.4 us
  waiting for transfers between devices: 20.1 us -> 2.66 us
  starting transfers between devices: 26.2 us -> 16.4 us
    all_to_all x0 -> x1, blocking collectives: none -> 26.8 us  [shards(): lax.all_to_all(summary, DAY, split_axis=0, concat_axis=0, tiled=True)]
    all_to_all x1 -> x0, starting transfers between devices: 14.9 us -> none  [shards(): lax.all_to_all(summary, DAY, split_axis=0, concat_axis=0, tiled=True)]
    all_to_all x1 -> x0, waiting for transfers between devices: 12 us -> none  [shards(): lax.all_to_all(summary, DAY, split_axis=0, concat_axis=0, tiled=True)]
    all_to_all x1, waiting for transfers between devices: 6.42 us -> 0.01 us  [shards(): lax.all_to_all(grad_summary, DAY, split_axis=0, concat_axis=0, tiled=True)]
    ppermute x2 -> x3, starting transfers between devices: 5.71 us -> 10.7 us  [the longest x1 4.85 us: shards(): lax.ppermute(send_down, 'rep', [(i, ((i + 1 ^ 1) - 1) % groups) for i in...]
    all_to_all x1, blocking collectives: 22.4 us -> 20.9 us  [shards(): lax.all_to_all(merged, ('rep', 'core'), split_axis=0, concat_axis=0, tile...]
    ppermute x2 -> x3, waiting for transfers between devices: 1.65 us -> 2.66 us  [the longest x1 2.65 us: shards(): lax.ppermute(send_down, 'rep', [(i, ((i + 1 ^ 1) - 1) % groups) for i in...]
    unnamed x17 -> x18, local copies, waits for them, and re-layouts: 1.52 us -> 2.29 us
  transfers between devices with their start and end apart: 4 -> 4, of which waited for: 3 -> 1; matrix products, arithmetic and copies ran while one was open for 0% -> 0% of each run, Pallas kernels for 2% -> 3%
where the time goes in v3:
time: 107 us
  blocking collectives  69.4 us (65%)
  starting transfers between devices  16.4 us (15%)
  Pallas kernels  15.4 us (14%)
  waiting for transfers between devices  2.66 us (2%)
  local copies, waits for them, and re-layouts  2.29 us (2%)
    all_to_all x1, blocking collectives, shards(): lax.all_to_all(summary, DAY, split_axis=0, concat_axis=0, tiled=True)  26.8 us
    all_to_all x1, blocking collectives, shards(): lax.all_to_all(partial_sums, ('x', 'z'), split_axis=0, concat_axis=0, til...  21.6 us
    all_to_all x1, blocking collectives, shards(): lax.all_to_all(merged, ('rep', 'core'), split_axis=0, concat_axis=0, tile...  20.9 us
    pallas_call x7, Pallas kernels, call(): pl.pallas_call(kernel, out_shape=[pltpu.HBM(s, t) if i in out_whole else...  15.4 us
    all_to_all x1, starting transfers between devices, shards(): lax.all_to_all(grad_summary, DAY, split_axis=0, concat_axis=0, tiled=True)  5.73 us
    ppermute x1, starting transfers between devices, shards(): lax.ppermute(send_down, 'rep', [(i, ((i + 1 ^ 1) - 1) % groups) for i in...  4.85 us
    ppermute x1, starting transfers between devices, shards(): up = lax.ppermute(send_up, 'rep', [(i, i ^ 1) for i in range(groups)])  3.32 us
    ppermute x1, waiting for transfers between devices, shards(): lax.ppermute(send_down, 'rep', [(i, ((i + 1 ^ 1) - 1) % groups) for i in...  2.65 us
  transfers between devices with their start and end apart: 4, of which 1 were waited for; matrix products, arithmetic and copies ran while one was open for 0% of the time, Pallas kernels for 3%

profile of v3, /device:TPU:1, one launch (start us, length us, event | category | flops | bytes accessed | tf_op | source)
XLA Modules:
  0.0 106.9 jit_solution(106898651290052375)
XLA Ops:
  0.6 0.0 copy-start.6
  0.6 0.0 copy-start.8
  0.7 5.6 %shard_map.86 = (bf16[64,16,128]{2,1,0:T(8,128)(2,1)}, f32[8,1024]{1,0:T(8,128)}) custom-call(s32[1,1024]{1,0:T(1,128)} %bitcast.6, s32[1,1024]{1,0:T(1,128)} %bitcast.9, bf16[8,512]{1,0:T(8,128)(2,1)} %bitcast.13, bf16[1024,512]{1,0:T(8,128)(2,1)} %events_ref.5, bf16[512,512]{1,0:T(8,128)(2,1)} %value_ref.3), custom_call_target="tpu_custom_call" | custom-call | flops 805306368 | bytes 1884160 | tf_op jit(solution)/shard_map/pallas_call | solution.py:243
  6.3 26.8 %all_to_all.20.x_ref = bf16[64,16,128]{2,1,0:T(8,128)(2,1)S(1)} all-to-all(bf16[64,16,128]{2,1,0:T(8,128)(2,1)} %get-tuple-element.9.summary_ref), channel_id=1, replica_groups=mesh['rep'=8,'x'=4,'z'=8,'core'=2] {'x','z','core'}, dimensions={0} | all-to-all | bytes 524288 | tf_op jit(solution)/shard_map/all_to_all | solution.py:287
  33.1 0.0 copy-done.6
  33.1 0.0 copy-done.8
  33.1 0.0 copy-start.5
  33.1 5.1 %shard_map.88 = (bf16[64,16,128]{2,1,0:T(8,128)(2,1)}, bf16[256,2048]{1,0:T(8,128)(2,1)}) custom-call(bf16[64,16,128]{2,1,0:T(8,128)(2,1)S(1)} %all_to_all.20.x_ref, bf16[256,512]{1,0:T(8,128)(2,1)S(1)} %bitcast.12, bf16[512,1536]{1,0:T(8,128)(2,1)S(1)} %copy-done.6), custom_call_target="tpu_custom_call" | custom-call | flops 1744830464 | bytes 3407872 | tf_op jit(solution)/shard_map/pallas_call | solution.py:243
  38.2 0.0 copy-start
  38.2 2.5 %collective-permute-start = (bf16[256,2048]{1,0:T(8,128)(2,1)}, bf16[256,2048]{1,0:T(8,128)(2,1)S(1)}, u32[]{:S(2)}, u32[]{:S(2)}) collective-permute-start(bf16[256,2048]{1,0:T(8,128)(2,1)} %get-tuple-element.12.mine_ref), channel_id=1, source_target_pairs={{0,1},{1,0},{2,3},{3,2},{4,5},{5,4},{6,7},{7,6},{8,9},{9,8},{10,11... | collective-permute-start | bytes 3145736 | tf_op jit(solution)/shard_map/ppermute | solution.py:303
  40.7 5.7 %all-to-all-start.1 = ((bf16[64,16,128]{2,1,0:T(8,128)(2,1)}), bf16[64,16,128]{2,1,0:T(8,128)(2,1)S(1)}, u32[]{:S(2)}, u32[]{:S(2)}) async-start(bf16[64,16,128]{2,1,0:T(8,128)(2,1)} %get-tuple-element.11), calls=%async_computation.1 | async-start | bytes 524288 | tf_op jit(solution)/shard_map/all_to_all | solution.py:302
  46.5 0.0 collective-permute-done.theirs_ref
  46.5 0.0 copy-start.1
  46.5 1.2 %copy-done.1 = bf16[256,2048]{1,0:T(8,128)(2,1)S(1)} copy-done((bf16[256,2048]{1,0:T(8,128)(2,1)S(1)}, bf16[256,2048]{1,0:T(8,128)(2,1)}, u32[]{:S(2)}) %copy-start.1) | copy-done | bytes 1048600
  47.7 1.8 %shard_map.89 = (bf16[256,768]{1,0:T(8,128)(2,1)S(1)}, bf16[256,384]{1,0:T(8,128)(2,1)}, bf16[256,384]{1,0:T(8,128)(2,1)}) custom-call(s32[1]{0:T(128)} %bitcast.core_ref, s32[1]{0:T(128)} %bitcast.5.row_ref, bf16[256,2048]{1,0:T(8,128)(2,1)S(1)} %copy-done.1, bf16[256,2048]{1,0:T(8,128)(2,1)S(1)} %collective-permute-done.theirs_ref), custom_call_target="tpu_custom_call" | custom-call | tf_op jit(solution)/shard_map/pallas_call | solution.py:243
  49.5 3.3 %collective-permute-start.1 = (bf16[256,384]{1,0:T(8,128)(2,1)}, bf16[256,384]{1,0:T(8,128)(2,1)S(1)}, u32[]{:S(2)}, u32[]{:S(2)}) collective-permute-start(bf16[256,384]{1,0:T(8,128)(2,1)} %get-tuple-element.14), channel_id=1, source_target_pairs={{0,64},{64,0},{128,192},{192,128},{256,320},{320,256},{384,448},{4... | collective-permute-start | bytes 589832 | tf_op jit(solution)/shard_map/ppermute | solution.py:311
  52.8 4.8 %collective-permute-start.2 = (bf16[256,384]{1,0:T(8,128)(2,1)}, bf16[256,384]{1,0:T(8,128)(2,1)S(1)}, u32[]{:S(2)}, u32[]{:S(2)}) collective-permute-start(bf16[256,384]{1,0:T(8,128)(2,1)} %get-tuple-element.15), channel_id=1, source_target_pairs={{0,448},{64,128},{128,64},{192,256},{256,192},{320,384},{384,320},... | collective-permute-start | bytes 589832 | tf_op jit(solution)/shard_map/ppermute | solution.py:312
  57.7 0.0 copy-done.2
  57.7 0.0 copy-done.4
  57.7 0.0 copy-done.5
  57.7 0.0 copy-done
  57.7 0.0 copy-start.7
  57.7 1.0 copy-done.7
  58.8 1.0 shard_map.87.centred_ref
  59.7 0.0 all-to-all-done.1.grad_ref
  59.7 0.0 collective-permute-done.1.up_ref
  59.8 2.7 %collective-permute-done.2.down_ref = bf16[256,384]{1,0:T(8,128)(2,1)S(1)} collective-permute-done((bf16[256,384]{1,0:T(8,128)(2,1)}, bf16[256,384]{1,0:T(8,128)(2,1)S(1)}, u32[]{:S(2)}, u32[]{:S(2)}) %collective-permute-start.2) | collective-permute-done | bytes 196640 | tf_op jit(solution)/shard_map/ppermute | solution.py:312
  62.4 1.1 %shard_map.90 = bf16[32,8,896]{2,1,0:T(8,128)(2,1)S(1)} custom-call(s32[1,1024]{1,0:T(1,128)S(1)} %bitcast.8, s32[1,1024]{1,0:T(1,128)S(1)} %bitcast.11, bf16[1024,512]{1,0:T(8,128)(2,1)S(1)} %copy-done, bf16[1024,512]{1,0:T(8,128)(2,1)S(1)} %shard_map.87.centred_ref, f32[8,1024]{1,0:T(8,128)S(1)} %copy-done.3, ...), custom_call_target="tpu_custom_call" | custom-call | flops 536870912 | bytes 3645440 | tf_op jit(solution)/shard_map/pallas_call | solution.py:243
  63.5 21.6 %all_to_all.21.x_ref = bf16[32,8,896]{2,1,0:T(8,128)(2,1)S(1)} all-to-all(bf16[32,8,896]{2,1,0:T(8,128)(2,1)S(1)} %shard_map.90), channel_id=1, replica_groups=mesh['rep'=8,'x'=4,'z'=8,'core'=2] {'x','z'}, dimensions={0} | all-to-all | bytes 917504 | tf_op jit(solution)/shard_map/all_to_all | solution.py:319
  85.2 0.1 shard_map.91
  85.2 20.9 %all_to_all.22.x_ref = bf16[16,8,896]{2,1,0:T(8,128)(2,1)S(1)} all-to-all(bf16[16,8,896]{2,1,0:T(8,128)(2,1)S(1)} %shard_map.91), channel_id=1, replica_groups=mesh['rep'=8,'x'=4,'z'=8,'core'=2] {'rep','core'}, dimensions={0} | all-to-all | bytes 458752 | tf_op jit(solution)/shard_map/all_to_all | solution.py:321
  106.2 0.7 shard_map.92
  (4 shorter events, 0.0 us)
Async XLA Ops:
  0.6 32.5 %copy-start.6 = (bf16[512,1536]{1,0:T(8,128)(2,1)S(1)}, bf16[512,1536]{1,0:T(8,128)(2,1)}, u32[]{:S(2)}) copy-start(bf16[512,1536]{1,0:T(8,128)(2,1)} %qkv_weight_ref.1) | copy-start | bytes 4718596
  0.6 32.5 %copy-start.8 = (bf16[1,256,512]{2,1,0:T(8,128)(2,1)S(1)}, bf16[1,256,512]{2,1,0:T(8,128)(2,1)}, u32[]{:S(2)}) copy-start(bf16[1,256,512]{2,1,0:T(8,128)(2,1)} %param.13) | copy-start | bytes 786436
  33.1 24.5 %copy-start.2 = (bf16[64,16,128]{2,1,0:T(8,128)(2,1)S(1)}, bf16[64,16,128]{2,1,0:T(8,128)(2,1)}, u32[]{:S(2)}) copy-start(bf16[64,16,128]{2,1,0:T(8,128)(2,1)} %get-tuple-element.9.summary_ref) | copy-start | bytes 786436
  33.1 24.6 %copy-start.4 = (s32[1024]{0:T(1024)S(1)}, s32[1024]{0:T(1024)}, u32[]{:S(2)}) copy-start(s32[1024]{0:T(1024)} %param.8) | copy-start | bytes 12292
  33.1 24.6 %copy-start.5 = (s32[1024]{0:T(1024)S(1)}, s32[1024]{0:T(1024)}, u32[]{:S(2)}) copy-start(s32[1024]{0:T(1024)} %param.9) | copy-start | bytes 12292
  38.2 19.5 %copy-start = (bf16[1024,512]{1,0:T(8,128)(2,1)S(1)}, bf16[1024,512]{1,0:T(8,128)(2,1)}, u32[]{:S(2)}) copy-start(bf16[1024,512]{1,0:T(8,128)(2,1)} %events_ref.5) | copy-start | bytes 3145732
  38.2 8.2 %collective-permute-start = (bf16[256,2048]{1,0:T(8,128)(2,1)}, bf16[256,2048]{1,0:T(8,128)(2,1)S(1)}, u32[]{:S(2)}, u32[]{:S(2)}) collective-permute-start(bf16[256,2048]{1,0:T(8,128)(2,1)} %get-tuple-element.12.mine_ref), channel_id=1, source_target_pairs={{0,1},{1,0},{2,3},{3,2},{4,5},{5,4},{6,7},{7,6},{8,9},{9,8},{10,11... | collective-permute-start | bytes 3145736 | tf_op jit(solution)/shard_map/ppermute | solution.py:303
  40.7 19.0 %all-to-all-start.1 = ((bf16[64,16,128]{2,1,0:T(8,128)(2,1)}), bf16[64,16,128]{2,1,0:T(8,128)(2,1)S(1)}, u32[]{:S(2)}, u32[]{:S(2)}) async-start(bf16[64,16,128]{2,1,0:T(8,128)(2,1)} %get-tuple-element.11), calls=%async_computation.1 | async-start | bytes 524288 | tf_op jit(solution)/shard_map/all_to_all | solution.py:302
  46.5 1.2 %copy-start.1 = (bf16[256,2048]{1,0:T(8,128)(2,1)S(1)}, bf16[256,2048]{1,0:T(8,128)(2,1)}, u32[]{:S(2)}) copy-start(bf16[256,2048]{1,0:T(8,128)(2,1)} %get-tuple-element.12.mine_ref) | copy-start | bytes 3145732
  49.5 12.9 %copy-start.3 = (f32[8,1024]{1,0:T(8,128)S(1)}, f32[8,1024]{1,0:T(8,128)}, u32[]{:S(2)}) copy-start(f32[8,1024]{1,0:T(8,128)} %get-tuple-element.10.weight_ref) | copy-start | bytes 98308
  49.5 10.3 %collective-permute-start.1 = (bf16[256,384]{1,0:T(8,128)(2,1)}, bf16[256,384]{1,0:T(8,128)(2,1)S(1)}, u32[]{:S(2)}, u32[]{:S(2)}) collective-permute-start(bf16[256,384]{1,0:T(8,128)(2,1)} %get-tuple-element.14), channel_id=1, source_target_pairs={{0,64},{64,0},{128,192},{192,128},{256,320},{320,256},{384,448},{4... | collective-permute-start | bytes 589832 | tf_op jit(solution)/shard_map/ppermute | solution.py:311
  52.8 9.6 %collective-permute-start.2 = (bf16[256,384]{1,0:T(8,128)(2,1)}, bf16[256,384]{1,0:T(8,128)(2,1)S(1)}, u32[]{:S(2)}, u32[]{:S(2)}) collective-permute-start(bf16[256,384]{1,0:T(8,128)(2,1)} %get-tuple-element.15), channel_id=1, source_target_pairs={{0,448},{64,128},{128,64},{192,256},{256,192},{320,384},{384,320},... | collective-permute-start | bytes 589832 | tf_op jit(solution)/shard_map/ppermute | solution.py:312
  57.7 1.0 copy-start.7

commit v4 on v3

--- a/solution.py
+++ b/solution.py
@@ -105,28 +105,32 @@
     summary_ref[...] = to_blocks(nn(rows, weighted), users)
 
 
-def centre_kernel(users, slots, user_ref, day_ref, events_ref, value_ref, summary_ref, out_ref):
+def centre_kernel(users, slots, user_ref, day_ref, events_ref, value_ref, summary_ref, qkv_ref, out_ref, qkv_out, sem):
+    copy = pltpu.make_async_copy(qkv_ref, qkv_out, sem)
+    copy.start()
     rows = slot_rows(user_ref, day_ref, users, slots)
     pooled = to_rows(summary_ref[...], value_ref.shape[1]).astype(BF16)
     values = nn(events_ref[...], value_ref[...])
     out_ref[...] = (values - tn(rows, pooled)).astype(BF16)
-
-
-def attention_kernel(heads, loss_scale, x_ref, cot_ref, qkv_weight_ref, grad_ref, pack_ref, pack_buf, sems):
+    copy.wait()
+
+
+def attention_kernel(heads, loss_scale, core_ref, x_ref, cot_ref, qkv_weight_ref, grad_ref, mine_ref, send_ref, cot_buf, mine_buf, send_buf, sems):
     width = qkv_weight_ref.shape[0]
     days = cot_ref.shape[0]
+    cot_copy = pltpu.make_async_copy(cot_ref, cot_buf, sems.at[2])
+    cot_copy.start()
     buckets = x_ref.shape[0]
     size = width // heads
     causal = iota((days, days), 1) <= iota((days, days), 0)
-    cot = cot_ref[...]
     wide = to_rows(x_ref[...], width)
     inverse = lax.rsqrt(jnp.mean(wide * wide, axis=-1, keepdims=True) + 1e-06)
     normed = (wide * inverse).astype(BF16)
-    pieces = [pl.ds(i * width, width) for i in range(4)]
-    copies = [pltpu.make_async_copy(pack_buf.at[:, p], pack_ref.at[:, p], sems.at[i]) for i, p in enumerate(pieces)]
-    pack_buf[:, pieces[0]] = normed
-    copies[0].start()
+    mine_buf[:, :width] = normed
+    send_buf[:, :width] = normed
     qkv = nn(normed, qkv_weight_ref[...]).astype(BF16)
+    cot_copy.wait()
+    cot = cot_buf[...]
     pair = 2 * size
     left = iota((days, pair), 1) < size
     zero = jnp.zeros((days, pair), BF16)
@@ -153,8 +157,15 @@
         parts[1].append(tn(jnp.concatenate(logits_grad, 0), jnp.concatenate(q2, 0)))
         parts[2].append(tn(jnp.concatenate(probs, 0), jnp.concatenate(c2, 0)) * loss_scale)
     grad_qkv = jnp.concatenate([a.astype(BF16) for part in parts for a in part], axis=1)
-    pack_buf[:, width:] = grad_qkv
-    for copy in copies[1:]:
+    half = 3 * width // 2
+    first = core_ref[0] == 0
+    mine_buf[:, width:] = jnp.where(first, grad_qkv[:, :half], grad_qkv[:, half:])
+    send_buf[:, width:] = jnp.where(first, grad_qkv[:, half:], grad_qkv[:, :half])
+    copies = [
+        pltpu.make_async_copy(send_buf, send_ref, sems.at[0]),
+        pltpu.make_async_copy(mine_buf, mine_ref, sems.at[1]),
+    ]
+    for copy in copies:
         copy.start()
     grad_normed = nt(grad_qkv, qkv_weight_ref[...])
     cubed = inverse * inverse * inverse
@@ -168,81 +179,59 @@
         copy.wait()
 
 
-def outer_kernel(depth, core_ref, row_ref, mine_ref, theirs_ref, keep_ref, up_ref, down_ref):
-    quarter = up_ref.shape[1]
-    width = mine_ref.shape[1] - 4 * quarter
-    count = width // 2
+def outer_kernel(width, mine_ref, theirs_ref, out_ref):
     both = jnp.concatenate([mine_ref[...], theirs_ref[...]], axis=0)
-    column = iota((width, count), 1)
-    pick = one_hot(iota((width, count), 0) == (2 * (column // depth) + core_ref[0]) * depth + column % depth)
-    total = tn(nn(both[:, :width], pick).astype(BF16), both[:, width:]).astype(BF16)
-    first = row_ref[0] & 1 == 0
-    for side, send_ref in ((0, up_ref), (1, down_ref)):
-        low = total[:, 2 * side * quarter : (2 * side + 1) * quarter]
-        high = total[:, (2 * side + 1) * quarter : (2 * side + 2) * quarter]
-        keep_ref[:, side * quarter : (side + 1) * quarter] = jnp.where(first, low, high)
-        send_ref[...] = jnp.where(first, high, low)
-
-
-def score_kernel(
-    users, slots, cores, user_ref, day_ref, events_ref, centred_ref, weight_ref, grad_ref, keep_ref, up_ref, down_ref, out_ref
-):
+    out_ref[...] = tn(both[:, :width], both[:, width:]).reshape(out_ref.shape).astype(BF16)
+
+
+def score_kernel(users, slots, user_ref, day_ref, events_ref, centred_ref, weight_ref, grad_ref, outer_ref, out_ref):
     width = events_ref.shape[1]
     heads = weight_ref.shape[0]
-    chips, depth, columns = out_ref.shape
-    half = keep_ref.shape[1]
-    lanes = columns - half
-    quarter = half // 2
-    for start, got_ref in ((0, up_ref), (quarter, down_ref)):
-        weight_sum = keep_ref[:, start : start + quarter].astype(F32) + got_ref[...].astype(F32)
-        out_ref[:, :, start : start + quarter] = weight_sum.reshape(chips, depth, quarter).astype(BF16)
+    parts, depth, half = outer_ref.shape
+    lanes = out_ref.shape[2] - half
+    out_ref[:, :, :half] = outer_ref[...]
     rows = slot_rows(user_ref, day_ref, users, slots)
     grad = tn(rows, to_rows(grad_ref[...], width).astype(BF16))
     terms = (grad * centred_ref[...].astype(F32)).astype(BF16)
-    reduce = one_hot(iota((lanes, width), 1) // (width // heads) == iota((lanes, width), 0) % heads)
-    weight = jnp.concatenate([weight_ref[...]] * (lanes // heads), axis=0)
-    scores = (weight * nt(reduce, terms)).astype(BF16)
-    spread = nn(scores, events_ref[...])
-    keep = (iota((lanes, width), 1) // depth) % cores == iota((lanes, width), 0) // heads
-    turned = jnp.transpose(jnp.where(keep, spread, 0.0), (1, 0))
-    out_ref[:, :, half:] = jnp.sum(turned.reshape(chips, cores, depth, lanes), axis=1).astype(BF16)
-
-
-def merge_kernel(x_ref, out_ref):
-    total = jnp.sum(x_ref[...].astype(F32), axis=0).astype(BF16)
+    reduce = one_hot(iota((heads, width), 1) // (width // heads) == iota((heads, width), 0))
+    scores = (weight_ref[...] * nt(reduce, terms)).astype(BF16)
+    scores = jnp.concatenate([scores.astype(F32), jnp.zeros((lanes - heads, scores.shape[1]), F32)], axis=0).astype(BF16)
+    turned = jnp.transpose(nn(scores, events_ref[...]), (1, 0))
+    out_ref[:, :, half:] = turned.reshape(parts, depth, lanes).astype(BF16)
+
+
+def merge_kernel(cores, x_ref, out_ref):
+    parts, depth, columns = x_ref.shape
+    half = columns - 128
+    total = jnp.sum(x_ref[...].astype(F32).reshape(parts // cores, cores, depth, columns), axis=0)
+    score = jnp.sum(total[:, :, half:], axis=0)
+    pieces = [total[i, :, :half] for i in range(cores)] + [score]
+    merged = jnp.concatenate(pieces, axis=1).astype(BF16)
     for i in range(out_ref.shape[0]):
-        out_ref[i] = total
-
-
-def final_kernel(cores, core_ref, x_ref, weight_ref, score_ref):
-    half = weight_ref.shape[1] // 2
-    heads = score_ref.shape[1]
-    groups = x_ref.shape[0] // cores
-    core = core_ref[0]
-    mine = [x_ref[cores * r + core].astype(F32) for r in range(groups)]
-    quarter = half // 2
-    for side in range(2):
-        for bit in range(2):
-            held = [m[:, side * quarter : (side + 1) * quarter] for r, m in enumerate(mine) if r % 2 == bit]
-            weight_ref[:, (2 * side + bit) * quarter : (2 * side + bit + 1) * quarter] = sum(held)
-    score = jnp.sum(x_ref[:, :, half:].astype(F32), axis=0)
-    lanes = score.shape[1]
-    pick = one_hot(iota((lanes, heads), 0) == iota((lanes, heads), 1) + core * heads)
-    depth = score.shape[0]
-    pieces = nn(split3(score), pick)
-    score_ref[...] = pieces[:depth] + pieces[depth : 2 * depth] + pieces[2 * depth :]
-
-
-def call(kernel, outs, args, scalars=0, flops=0, moved=None, whole=(), out_whole=(), scratch=(), limit=24):
+        out_ref[i] = merged
+
+
+def final_kernel(x_ref, weight_ref, score_ref):
+    columns = weight_ref.shape[1]
+    total = jnp.sum(x_ref[...].astype(F32), axis=0)
+    weight_ref[...] = total[:, :columns]
+    score_ref[...] = total[:, columns : columns + score_ref.shape[1]]
+
+
+def call(kernel, outs, args, scalars=0, flops=0, moved=None, whole=(), held=(), out_whole=(), out_far=(), out_near=(), scratch=(), limit=24):
     vmem = pl.BlockSpec(memory_space=pltpu.VMEM)
     smem = pl.BlockSpec(memory_space=pltpu.SMEM)
     anywhere = pl.BlockSpec(memory_space=pltpu.HBM)
     specs = [smem if i < scalars else anywhere if i in whole else vmem for i in range(len(args))]
     if moved is None:
         moved = sum(a.size * a.dtype.itemsize for a in args) + sum(math.prod(s) * jnp.dtype(t).itemsize for s, t in outs)
+    args = [pltpu.with_memory_space_constraint(a, pltpu.HBM) if i in whole + held else a for i, a in enumerate(args)]
     return pl.pallas_call(
         kernel,
-        out_shape=[pltpu.HBM(s, t) if i in out_whole else jax.ShapeDtypeStruct(s, t) for i, (s, t) in enumerate(outs)],
+        out_shape=[
+            pltpu.HBM(s, t) if i in out_whole + out_far else pltpu.VMEM(s, t) if i in out_near else jax.ShapeDtypeStruct(s, t)
+            for i, (s, t) in enumerate(outs)
+        ],
         in_specs=specs,
         out_specs=[anywhere if i in out_whole else vmem for i in range(len(outs))],
         scratch_shapes=scratch,
@@ -253,8 +242,7 @@
 
 def shards(sizes, events, event_user, event_day, score_weight, value_weight, qkv_weight, cotangent):
     groups, x_size, z_size, cores = sizes
-    chips = x_size * z_size
-    buckets = chips * cores
+    buckets = x_size * z_size * cores
     user_dev, days, width = cotangent.shape
     heads = score_weight.shape[1]
     day_dev = days // buckets
@@ -267,7 +255,6 @@
     user_row = event_user.reshape(1, count)
     day_row = event_day.reshape(1, count)
     core = lax.axis_index("core").reshape(1)
-    row = lax.axis_index("rep").reshape(1)
 
     block = ((buckets, day_dev * width // 128, 128), BF16)
     summary, weight = call(
@@ -285,48 +272,42 @@
         limit=60,
     )
     by_user = lax.all_to_all(summary, DAY, split_axis=0, concat_axis=0, tiled=True)
-    (centred,) = call(
+    centred, qkv_held = call(
         functools.partial(centre_kernel, users, slots),
-        [((count, width), BF16)],
-        (user_row, day_row, events, value_weight, summary),
+        [((count, width), BF16), (qkv_weight.shape, BF16)],
+        (user_row, day_row, events, value_weight, summary, qkv_weight),
         flops=2 * count * width * (width + slots),
-    )
-    grad_summary, mine = call(
+        whole=(5,),
+        held=(2, 3),
+        out_far=(0,),
+        out_near=(1,),
+        scratch=[pltpu.SemaphoreType.DMA],
+    )
+    grad_summary, mine, send = call(
         functools.partial(attention_kernel, heads, loss_scale),
-        [block, ((days, 4 * width), BF16)],
-        (by_user, cotangent.reshape(days, width), qkv_weight),
+        [block, ((days, width + half), BF16), ((days, width + half), BF16)],
+        (core, by_user, cotangent.reshape(days, width), qkv_held),
+        scalars=1,
+        whole=(2,),
         flops=2 * days * width * (6 * width + 14 * days),
-        out_whole=(1,),
-        scratch=[pltpu.VMEM((days, 4 * width), BF16), pltpu.SemaphoreType.DMA((4,))],
+        out_whole=(1, 2),
+        scratch=[pltpu.VMEM((days, width), BF16)] + [pltpu.VMEM((days, width + half), BF16)] * 2 + [pltpu.SemaphoreType.DMA((3,))],
     )
     grad_days = lax.all_to_all(grad_summary, DAY, split_axis=0, concat_axis=0, tiled=True)
-    theirs = lax.ppermute(mine, "core", [(i, cores - 1 - i) for i in range(cores)])
-    keep, send_up, send_down = call(
-        functools.partial(outer_kernel, rows),
-        [((width // 2, half), BF16)] + [((width // 2, half // 2), BF16)] * 2,
-        (core, row, mine, theirs),
-        scalars=2,
-        moved=0,
-    )
-    up = lax.ppermute(send_up, "rep", [(i, i ^ 1) for i in range(groups)])
-    down = lax.ppermute(send_down, "rep", [(i, (((i + 1) ^ 1) - 1) % groups) for i in range(groups)])
+    theirs = lax.ppermute(send, "core", [(i, cores - 1 - i) for i in range(cores)])
+    (outer,) = call(functools.partial(outer_kernel, width), [((buckets, rows, half), BF16)], (mine, theirs), moved=0, held=(0,))
     (partial_sums,) = call(
-        functools.partial(score_kernel, users, slots, cores),
-        [((chips, rows, half + 128), BF16)],
-        (user_row, day_row, events, centred, weight, grad_days, keep, up, down),
+        functools.partial(score_kernel, users, slots),
+        [((buckets, rows, half + 128), BF16)],
+        (user_row, day_row, events, centred, weight, grad_days, outer),
         flops=2 * count * width * (slots + 256),
     )
-    plane = lax.all_to_all(partial_sums, ("x", "z"), split_axis=0, concat_axis=0, tiled=True)
-    (merged,) = call(merge_kernel, [((groups * cores, rows, half + 128), BF16)], (plane,))
-    everyone = lax.all_to_all(merged, ("rep", "core"), split_axis=0, concat_axis=0, tiled=True)
-    return tuple(
-        call(
-            functools.partial(final_kernel, cores),
-            [((rows, 3 * width), F32), ((rows, heads), F32)],
-            (core, everyone),
-            scalars=1,
-        )
-    )
+    gathered = lax.all_to_all(partial_sums, DAY, split_axis=0, concat_axis=0, tiled=True)
+    (merged,) = call(
+        functools.partial(merge_kernel, cores), [((groups, rows, 3 * width + 128), BF16)], (gathered,)
+    )
+    everyone = lax.all_to_all(merged, "rep", split_axis=0, concat_axis=0, tiled=True)
+    return tuple(call(final_kernel, [((rows, 3 * width), F32), ((rows, heads), F32)], (everyone,)))
 
 
 def solution(mesh):

time: 107 us -> 110 us (1.028)
  blocking collectives: 69.4 us -> 48 us
  waiting for transfers between devices: 2.66 us -> 15.1 us
  starting transfers between devices: 16.4 us -> 23 us
  Pallas kernels: 15.4 us -> 18.9 us
    all_to_all x3 -> x2, blocking collectives: 69.4 us -> 48 us  [the longest x1 31.6 us: shards(): lax.all_to_all(partial_sums, DAY, split_axis=0, concat_axis=0, tiled=True)]
    all_to_all x0 -> x1, starting transfers between devices: none -> 14.9 us  [shards(): lax.all_to_all(summary, DAY, split_axis=0, concat_axis=0, tiled=True)]
    all_to_all x1, waiting for transfers between devices: 0.01 us -> 8.34 us  [shards(): lax.all_to_all(grad_summary, DAY, split_axis=0, concat_axis=0, tiled=True)]
    ppermute x3 -> x1, starting transfers between devices: 10.7 us -> 2.49 us  [shards(): lax.ppermute(send, 'core', [(i, cores - 1 - i) for i in range(cores)])]
    all_to_all x0 -> x1, waiting for transfers between devices: none -> 6.77 us  [shards(): lax.all_to_all(summary, DAY, split_axis=0, concat_axis=0, tiled=True)]
    pallas_call x7, Pallas kernels: 15.4 us -> 18.9 us  [call(): pl.pallas_call(kernel, out_shape=[pltpu.HBM(s, t) if i in out_whole + out...]
    ppermute x3 -> x1, waiting for transfers between devices: 2.66 us -> 0.01 us  [shards(): lax.ppermute(send, 'core', [(i, cores - 1 - i) for i in range(cores)])]
    unnamed x18 -> x16, local copies, waits for them, and re-layouts: 2.29 us -> 2.92 us
  transfers between devices with their start and end apart: 4 -> 3, of which waited for: 1 -> 2; matrix products, arithmetic and copies ran while one was open for 0% -> 0% of each run, Pallas kernels for 3% -> 5%
where the time goes in v4:
time: 110 us; the launch traced here: 109 us
  blocking collectives  48 us (44%)
  starting transfers between devices  23 us (21%)
  Pallas kernels  18.9 us (17%)
  waiting for transfers between devices  15.1 us (14%)
  local copies, waits for them, and re-layouts  2.92 us (3%)
    all_to_all x1, blocking collectives, shards(): lax.all_to_all(partial_sums, DAY, split_axis=0, concat_axis=0, tiled=True)  31.6 us
    pallas_call x7, Pallas kernels, call(): pl.pallas_call(kernel, out_shape=[pltpu.HBM(s, t) if i in out_whole + out...  18.9 us
    all_to_all x1, blocking collectives, shards(): lax.all_to_all(merged, 'rep', split_axis=0, concat_axis=0, tiled=True)  16.5 us
    all_to_all x1, starting transfers between devices, shards(): lax.all_to_all(summary, DAY, split_axis=0, concat_axis=0, tiled=True)  14.9 us
    all_to_all x1, waiting for transfers between devices, shards(): lax.all_to_all(grad_summary, DAY, split_axis=0, concat_axis=0, tiled=True)  8.34 us
    all_to_all x1, waiting for transfers between devices, shards(): lax.all_to_all(summary, DAY, split_axis=0, concat_axis=0, tiled=True)  6.77 us
    all_to_all x1, starting transfers between devices, shards(): lax.all_to_all(grad_summary, DAY, split_axis=0, concat_axis=0, tiled=True)  5.7 us
    unnamed x16, local copies, waits for them, and re-layouts  2.92 us
  transfers between devices with their start and end apart: 3, of which 2 were waited for; matrix products, arithmetic and copies ran while one was open for 0% of the time, Pallas kernels for 5%

profile of v4, /device:TPU:1, one launch (start us, length us, event | category | flops | bytes accessed | tf_op | source)
XLA Modules:
  0.0 108.8 jit_solution(12784582715955819775)
XLA Ops:
  0.6 0.0 copy-start.6
  0.6 0.0 copy-start.7
  0.7 5.5 %shard_map.86 = (bf16[64,16,128]{2,1,0:T(8,128)(2,1)}, f32[8,1024]{1,0:T(8,128)}) custom-call(s32[1,1024]{1,0:T(1,128)} %bitcast.5, s32[1,1024]{1,0:T(1,128)} %bitcast.8, bf16[8,512]{1,0:T(8,128)(2,1)} %bitcast.12, bf16[1024,512]{1,0:T(8,128)(2,1)} %events_ref.5, bf16[512,512]{1,0:T(8,128)(2,1)} %value_ref.3), custom_call_target="tpu_custom_call" | custom-call | flops 805306368 | bytes 1884160 | tf_op jit(solution)/shard_map/pallas_call | solution.py:229
  6.2 14.9 %all-to-all-start = ((bf16[64,16,128]{2,1,0:T(8,128)(2,1)}), bf16[64,16,128]{2,1,0:T(8,128)(2,1)S(1)}, u32[]{:S(2)}, u32[]{:S(2)}) async-start(bf16[64,16,128]{2,1,0:T(8,128)(2,1)} %get-tuple-element.9.summary_ref), calls=%async_computation | async-start | bytes 524288 | tf_op jit(solution)/shard_map/all_to_all | solution.py:274
  21.0 0.0 copy-done.6
  21.0 0.0 copy-done.7
  21.0 0.0 copy-start.2
  21.0 1.0 copy-done.2
  22.0 4.2 %shard_map.87 = (bf16[1024,512]{1,0:T(8,128)(2,1)}, bf16[512,1536]{1,0:T(8,128)(2,1)S(1)}) custom-call(s32[1,1024]{1,0:T(1,128)S(1)} %bitcast.6, s32[1,1024]{1,0:T(1,128)S(1)} %bitcast.9, bf16[1024,512]{1,0:T(8,128)(2,1)} %events_ref.5, bf16[512,512]{1,0:T(8,128)(2,1)} %value_ref.3, bf16[64,16,128]{2,1,0:T(8,128)(2,1)S(1)} %copy-done.2, ...), custom_call_target="tpu_custom_call" | custom-call | flops 805306368 | bytes 6037504 | tf_op jit(solution)/shard_map/pallas_call | solution.py:229
  26.2 6.8 %all-to-all-done.x_ref = bf16[64,16,128]{2,1,0:T(8,128)(2,1)S(1)} async-done(((bf16[64,16,128]{2,1,0:T(8,128)(2,1)}), bf16[64,16,128]{2,1,0:T(8,128)(2,1)S(1)}, u32[]{:S(2)}, u32[]{:S(2)}) %all-to-all-start) | async-done | bytes 262176 | tf_op jit(solution)/shard_map/all_to_all | solution.py:274
  33.0 0.0 copy-start.5
  33.0 5.8 %shard_map.88 = (bf16[64,16,128]{2,1,0:T(8,128)(2,1)}, bf16[256,1280]{1,0:T(8,128)(2,1)}, bf16[256,1280]{1,0:T(8,128)(2,1)}) custom-call(s32[1]{0:T(128)} %bitcast.3.core_ref, bf16[64,16,128]{2,1,0:T(8,128)(2,1)S(1)} %all-to-all-done.x_ref, bf16[256,512]{1,0:T(8,128)(2,1)} %bitcast.11, bf16[512,1536]{1,0:T(8,128)(2,1)S(1)} %get-tuple-element.12.qkv_weight_ref), custom_call_target="tpu_custom_call" | custom-call | flops 1744830464 | bytes 3670020 | tf_op jit(solution)/shard_map/pallas_call | solution.py:229
  38.8 0.0 copy-start
  38.8 0.0 copy-start.1
  38.8 2.5 %collective-permute-start = (bf16[256,1280]{1,0:T(8,128)(2,1)}, bf16[256,1280]{1,0:T(8,128)(2,1)S(1)}, u32[]{:S(2)}, u32[]{:S(2)}) collective-permute-start(bf16[256,1280]{1,0:T(8,128)(2,1)} %get-tuple-element.15), channel_id=1, source_target_pairs={{0,1},{1,0},{2,3},{3,2},{4,5},{5,4},{6,7},{7,6},{8,9},{9,8},{10,11... | collective-permute-start | bytes 1966088 | tf_op jit(solution)/shard_map/ppermute | solution.py:297
  41.3 5.7 %all-to-all-start.1 = ((bf16[64,16,128]{2,1,0:T(8,128)(2,1)}), bf16[64,16,128]{2,1,0:T(8,128)(2,1)S(1)}, u32[]{:S(2)}, u32[]{:S(2)}) async-start(bf16[64,16,128]{2,1,0:T(8,128)(2,1)} %get-tuple-element.13), calls=%async_computation.1 | async-start | bytes 524288 | tf_op jit(solution)/shard_map/all_to_all | solution.py:296
  47.0 0.0 collective-permute-done.theirs_ref
  47.0 0.0 copy-start.3
  47.0 0.8 copy-done.3
  47.9 0.0 copy-start.4
  47.9 1.1 copy-done.4
  49.0 1.7 %shard_map.89.outer_ref = bf16[64,8,768]{2,1,0:T(8,128)(2,1)S(1)} custom-call(bf16[256,1280]{1,0:T(8,128)(2,1)} %get-tuple-element.14.mine_ref, bf16[256,1280]{1,0:T(8,128)(2,1)S(1)} %copy-done.4), custom_call_target="tpu_custom_call" | custom-call | tf_op jit(solution)/shard_map/pallas_call | solution.py:229
  50.7 8.3 %all-to-all-done.1.grad_ref = bf16[64,16,128]{2,1,0:T(8,128)(2,1)S(1)} async-done(((bf16[64,16,128]{2,1,0:T(8,128)(2,1)}), bf16[64,16,128]{2,1,0:T(8,128)(2,1)S(1)}, u32[]{:S(2)}, u32[]{:S(2)}) %all-to-all-start.1) | async-done | bytes 262176 | tf_op jit(solution)/shard_map/all_to_all | solution.py:296
  59.0 0.0 copy-done.5
  59.0 0.0 copy-done
  59.0 0.0 copy-done.1
  59.0 1.0 shard_map.90
  60.0 31.6 %all_to_all.20.x_ref = bf16[64,8,896]{2,1,0:T(8,128)(2,1)S(1)} all-to-all(bf16[64,8,896]{2,1,0:T(8,128)(2,1)S(1)} %shard_map.90), channel_id=1, replica_groups=mesh['rep'=8,'x'=4,'z'=8,'core'=2] {'x','z','core'}, dimensions={0} | all-to-all | bytes 1835008 | tf_op jit(solution)/shard_map/all_to_all | solution.py:305
  91.6 0.1 shard_map.91
  91.7 16.5 %all_to_all.21.x_ref = bf16[8,8,1664]{2,1,0:T(8,128)(2,1)S(1)} all-to-all(bf16[8,8,1664]{2,1,0:T(8,128)(2,1)S(1)} %shard_map.91), channel_id=1, replica_groups=mesh['rep'=8,'x'=4,'z'=8,'core'=2] {'rep'}, dimensions={0} | all-to-all | bytes 425984 | tf_op jit(solution)/shard_map/all_to_all | solution.py:309
  108.2 0.7 shard_map.92
Async XLA Ops:
  0.6 20.4 %copy-start.6 = (s32[1024]{0:T(1024)S(1)}, s32[1024]{0:T(1024)}, u32[]{:S(2)}) copy-start(s32[1024]{0:T(1024)} %param.8) | copy-start | bytes 12292
  0.6 20.4 %copy-start.7 = (s32[1024]{0:T(1024)S(1)}, s32[1024]{0:T(1024)}, u32[]{:S(2)}) copy-start(s32[1024]{0:T(1024)} %param.9) | copy-start | bytes 12292
  6.2 26.9 %all-to-all-start = ((bf16[64,16,128]{2,1,0:T(8,128)(2,1)}), bf16[64,16,128]{2,1,0:T(8,128)(2,1)S(1)}, u32[]{:S(2)}, u32[]{:S(2)}) async-start(bf16[64,16,128]{2,1,0:T(8,128)(2,1)} %get-tuple-element.9.summary_ref), calls=%async_computation | async-start | bytes 524288 | tf_op jit(solution)/shard_map/all_to_all | solution.py:274
  21.0 1.0 copy-start.2
  33.0 26.0 %copy-start.5 = (f32[8,1024]{1,0:T(8,128)S(1)}, f32[8,1024]{1,0:T(8,128)}, u32[]{:S(2)}) copy-start(f32[8,1024]{1,0:T(8,128)} %get-tuple-element.11.weight_ref) | copy-start | bytes 98308
  38.8 20.2 %copy-start = (bf16[1024,512]{1,0:T(8,128)(2,1)S(1)}, bf16[1024,512]{1,0:T(8,128)(2,1)}, u32[]{:S(2)}) copy-start(bf16[1024,512]{1,0:T(8,128)(2,1)} %events_ref.5) | copy-start | bytes 3145732
  38.8 20.2 %copy-start.1 = (bf16[1024,512]{1,0:T(8,128)(2,1)S(1)}, bf16[1024,512]{1,0:T(8,128)(2,1)}, u32[]{:S(2)}) copy-start(bf16[1024,512]{1,0:T(8,128)(2,1)} %get-tuple-element.10.centred_ref) | copy-start | bytes 3145732
  38.8 8.2 %collective-permute-start = (bf16[256,1280]{1,0:T(8,128)(2,1)}, bf16[256,1280]{1,0:T(8,128)(2,1)S(1)}, u32[]{:S(2)}, u32[]{:S(2)}) collective-permute-start(bf16[256,1280]{1,0:T(8,128)(2,1)} %get-tuple-element.15), channel_id=1, source_target_pairs={{0,1},{1,0},{2,3},{3,2},{4,5},{5,4},{6,7},{7,6},{8,9},{9,8},{10,11... | collective-permute-start | bytes 1966088 | tf_op jit(solution)/shard_map/ppermute | solution.py:297
  41.3 17.7 %all-to-all-start.1 = ((bf16[64,16,128]{2,1,0:T(8,128)(2,1)}), bf16[64,16,128]{2,1,0:T(8,128)(2,1)S(1)}, u32[]{:S(2)}, u32[]{:S(2)}) async-start(bf16[64,16,128]{2,1,0:T(8,128)(2,1)} %get-tuple-element.13), calls=%async_computation.1 | async-start | bytes 524288 | tf_op jit(solution)/shard_map/all_to_all | solution.py:296
  47.0 0.8 copy-start.3
  47.9 1.1 copy-start.4

commit v5 on v4

--- a/solution.py
+++ b/solution.py
@@ -70,38 +70,26 @@
     return jnp.concatenate(pieces, axis=1).astype(BF16)
 
 
-def pool_kernel(
-    users, slots, user_ref, day_ref, score_ref, events_ref, value_ref, summary_ref, weight_ref,
-    events_buf, value_buf, value_sem, event_sems,
-):
-    heads, width = score_ref.shape
-    steps = event_sems.shape[0]
-    step = events_ref.shape[0] // steps
-    value_copy = pltpu.make_async_copy(value_ref, value_buf, value_sem)
-    pieces = [pl.ds(i * step, step) for i in range(steps)]
-    copies = [
-        pltpu.make_async_copy(events_ref.at[piece, :], events_buf.at[piece, :], event_sems.at[i])
-        for i, piece in enumerate(pieces)
-    ]
-    value_copy.start()
+def pool_kernel(users, slots, *refs):
+    sources, (summary_ref, weight_ref), held, sems = refs[:5], refs[5:7], refs[7:12], refs[12]
+    copies = [pltpu.make_async_copy(source, target, sems.at[i]) for i, (source, target) in enumerate(zip(sources, held))]
     for copy in copies:
         copy.start()
+    user_ref, day_ref, score_ref, events_ref, value_ref = held
+    heads, width = score_ref.shape
+    expand = one_hot(iota((3 * heads, width), 1) // (width // heads) == iota((3 * heads, width), 0) % heads)
+    copies[0].wait()
+    copies[1].wait()
     rows = slot_rows(user_ref, day_ref, users, slots)
-    expand = one_hot(iota((3 * heads, width), 1) // (width // heads) == iota((3 * heads, width), 0) % heads)
-    score = score_ref[...]
-    value_copy.wait()
-    value = value_buf[...]
-    logits, values = [], []
-    for i in range(steps):
-        copies[i].wait()
-        part = events_buf[pieces[i], :]
-        logits.append(nt(score, part))
-        values.append(nn(part, value))
-    exponent = jnp.exp(jnp.concatenate(logits, axis=1))
+    copies[2].wait()
+    copies[3].wait()
+    exponent = jnp.exp(nt(score_ref[...], events_ref[...]))
     denominator = join3(nt(split3(exponent), rows))
     weight = exponent / join3(nn(split3(denominator), rows))
     weight_ref[...] = weight
-    weighted = (jnp.concatenate(values, axis=0) * tn(split3(weight), expand)).astype(BF16)
+    wide = tn(split3(weight), expand)
+    copies[4].wait()
+    weighted = (nn(events_ref[...], value_ref[...]) * wide).astype(BF16)
     summary_ref[...] = to_blocks(nn(rows, weighted), users)
 
 
@@ -115,10 +103,10 @@
     copy.wait()
 
 
-def attention_kernel(heads, loss_scale, core_ref, x_ref, cot_ref, qkv_weight_ref, grad_ref, mine_ref, send_ref, cot_buf, mine_buf, send_buf, sems):
+def attention_kernel(heads, loss_scale, core_ref, x_ref, cot_ref, qkv_weight_ref, grad_ref, mine_ref, send_ref, cot_buf, mine_buf, sems):
     width = qkv_weight_ref.shape[0]
     days = cot_ref.shape[0]
-    cot_copy = pltpu.make_async_copy(cot_ref, cot_buf, sems.at[2])
+    cot_copy = pltpu.make_async_copy(cot_ref, cot_buf, sems.at[1])
     cot_copy.start()
     buckets = x_ref.shape[0]
     size = width // heads
@@ -127,7 +115,7 @@
     inverse = lax.rsqrt(jnp.mean(wide * wide, axis=-1, keepdims=True) + 1e-06)
     normed = (wide * inverse).astype(BF16)
     mine_buf[:, :width] = normed
-    send_buf[:, :width] = normed
+    send_ref[:, :width] = normed
     qkv = nn(normed, qkv_weight_ref[...]).astype(BF16)
     cot_copy.wait()
     cot = cot_buf[...]
@@ -160,13 +148,9 @@
     half = 3 * width // 2
     first = core_ref[0] == 0
     mine_buf[:, width:] = jnp.where(first, grad_qkv[:, :half], grad_qkv[:, half:])
-    send_buf[:, width:] = jnp.where(first, grad_qkv[:, half:], grad_qkv[:, :half])
-    copies = [
-        pltpu.make_async_copy(send_buf, send_ref, sems.at[0]),
-        pltpu.make_async_copy(mine_buf, mine_ref, sems.at[1]),
-    ]
-    for copy in copies:
-        copy.start()
+    send_ref[:, width:] = jnp.where(first, grad_qkv[:, half:], grad_qkv[:, :half])
+    mine_copy = pltpu.make_async_copy(mine_buf, mine_ref, sems.at[0])
+    mine_copy.start()
     grad_normed = nt(grad_qkv, qkv_weight_ref[...])
     cubed = inverse * inverse * inverse
     grad = (
@@ -175,21 +159,35 @@
         - wide * cubed * jnp.mean(grad_normed * wide, axis=-1, keepdims=True)
     )
     grad_ref[...] = to_blocks(grad, buckets)
-    for copy in copies:
-        copy.wait()
-
-
-def outer_kernel(width, mine_ref, theirs_ref, out_ref):
+    mine_copy.wait()
+
+
+def outer_kernel(width, x_ref, mine_ref, theirs_ref, keep_ref, near_ref, far_ref):
     both = jnp.concatenate([mine_ref[...], theirs_ref[...]], axis=0)
-    out_ref[...] = tn(both[:, :width], both[:, width:]).reshape(out_ref.shape).astype(BF16)
-
-
-def score_kernel(users, slots, user_ref, day_ref, events_ref, centred_ref, weight_ref, grad_ref, outer_ref, out_ref):
+    total = tn(both[:, :width], both[:, width:]).astype(BF16)
+    first = x_ref[0] & 1 == 0
+    start = 0
+    for send_ref in (near_ref, far_ref):
+        parts, depth, part = send_ref.shape
+        low = total[:, 2 * start : 2 * start + part]
+        high = total[:, 2 * start + part : 2 * start + 2 * part]
+        keep_ref[:, :, start : start + part] = jnp.where(first, low, high).reshape(parts, depth, part)
+        send_ref[...] = jnp.where(first, high, low).reshape(parts, depth, part)
+        start += part
+
+
+def score_kernel(
+    users, slots, user_ref, day_ref, events_ref, centred_ref, weight_ref, grad_ref, keep_ref, near_ref, far_ref, out_ref
+):
     width = events_ref.shape[1]
     heads = weight_ref.shape[0]
-    parts, depth, half = outer_ref.shape
+    parts, depth, half = keep_ref.shape
     lanes = out_ref.shape[2] - half
-    out_ref[:, :, :half] = outer_ref[...]
+    start = 0
+    for got_ref in (near_ref, far_ref):
+        lane = slice(start, start + got_ref.shape[2])
+        out_ref[:, :, lane] = (keep_ref[:, :, lane].astype(F32) + got_ref[...].astype(F32)).astype(BF16)
+        start += got_ref.shape[2]
     rows = slot_rows(user_ref, day_ref, users, slots)
     grad = tn(rows, to_rows(grad_ref[...], width).astype(BF16))
     terms = (grad * centred_ref[...].astype(F32)).astype(BF16)
@@ -200,12 +198,17 @@
     out_ref[:, :, half:] = turned.reshape(parts, depth, lanes).astype(BF16)
 
 
-def merge_kernel(cores, x_ref, out_ref):
+def merge_kernel(cores, z_size, near, x_ref, out_ref):
     parts, depth, columns = x_ref.shape
-    half = columns - 128
-    total = jnp.sum(x_ref[...].astype(F32).reshape(parts // cores, cores, depth, columns), axis=0)
-    score = jnp.sum(total[:, :, half:], axis=0)
-    pieces = [total[i, :, :half] for i in range(cores)] + [score]
+    kept = columns - 128
+    pairs = parts // (2 * z_size * cores)
+    x = x_ref[...].astype(F32).reshape(pairs, 2, z_size, cores, depth, columns)
+    total = jnp.sum(jnp.sum(x, axis=0), axis=1)
+    pieces = []
+    for core in range(cores):
+        for lane in (slice(0, near), slice(near, kept)):
+            pieces += [total[0, core, :, lane], total[1, core, :, lane]]
+    pieces.append(jnp.sum(total[:, :, :, kept:], axis=(0, 1)))
     merged = jnp.concatenate(pieces, axis=1).astype(BF16)
     for i in range(out_ref.shape[0]):
         out_ref[i] = merged
@@ -262,12 +265,14 @@
         [block, ((heads, count), F32)],
         (user_row, day_row, score_weight.T, events, value_weight),
         flops=2 * count * width * (width + slots),
-        whole=(3, 4),
+        whole=(0, 1, 2, 3, 4),
         scratch=[
+            pltpu.VMEM((1, count), jnp.int32),
+            pltpu.VMEM((1, count), jnp.int32),
+            pltpu.VMEM((heads, width), BF16),
             pltpu.VMEM((count, width), BF16),
             pltpu.VMEM((width, width), BF16),
-            pltpu.SemaphoreType.DMA,
-            pltpu.SemaphoreType.DMA((4,)),
+            pltpu.SemaphoreType.DMA((5,)),
         ],
         limit=60,
     )
@@ -290,21 +295,33 @@
         scalars=1,
         whole=(2,),
         flops=2 * days * width * (6 * width + 14 * days),
-        out_whole=(1, 2),
-        scratch=[pltpu.VMEM((days, width), BF16)] + [pltpu.VMEM((days, width + half), BF16)] * 2 + [pltpu.SemaphoreType.DMA((3,))],
+        out_whole=(1,),
+        out_near=(2,),
+        scratch=[pltpu.VMEM((days, width), BF16), pltpu.VMEM((days, width + half), BF16), pltpu.SemaphoreType.DMA((2,))],
     )
     grad_days = lax.all_to_all(grad_summary, DAY, split_axis=0, concat_axis=0, tiled=True)
     theirs = lax.ppermute(send, "core", [(i, cores - 1 - i) for i in range(cores)])
-    (outer,) = call(functools.partial(outer_kernel, width), [((buckets, rows, half), BF16)], (mine, theirs), moved=0, held=(0,))
+    x_row = lax.axis_index("x").reshape(1)
+    near, far = width // 2, width // 4
+    keep, send_near, send_far = call(
+        functools.partial(outer_kernel, width),
+        [((buckets, rows, columns), BF16) for columns in (near + far, near, far)],
+        (x_row, mine, theirs),
+        scalars=1,
+        moved=0,
+        held=(1,),
+    )
+    got_near = lax.ppermute(send_near, "x", [(i, i ^ 1) for i in range(x_size)])
+    got_far = lax.ppermute(send_far, "x", [(i, (((i + 1) ^ 1) - 1) % x_size) for i in range(x_size)])
     (partial_sums,) = call(
         functools.partial(score_kernel, users, slots),
-        [((buckets, rows, half + 128), BF16)],
-        (user_row, day_row, events, centred, weight, grad_days, outer),
+        [((buckets, rows, near + far + 128), BF16)],
+        (user_row, day_row, events, centred, weight, grad_days, keep, got_near, got_far),
         flops=2 * count * width * (slots + 256),
     )
     gathered = lax.all_to_all(partial_sums, DAY, split_axis=0, concat_axis=0, tiled=True)
     (merged,) = call(
-        functools.partial(merge_kernel, cores), [((groups, rows, 3 * width + 128), BF16)], (gathered,)
+        functools.partial(merge_kernel, cores, z_size, near), [((groups, rows, 3 * width + 128), BF16)], (gathered,)
     )
     everyone = lax.all_to_all(merged, "rep", split_axis=0, concat_axis=0, tiled=True)
     return tuple(call(final_kernel, [((rows, 3 * width), F32), ((rows, heads), F32)], (everyone,)))

time: 110 us -> 107 us (0.973)
  starting transfers between devices: 23 us -> 30.1 us
  waiting for transfers between devices: 15.1 us -> 10.8 us
  blocking collectives: 48 us -> 43.9 us
  local copies, waits for them, and re-layouts: 2.92 us -> 1 us
    ppermute x0 -> x2, starting transfers between devices: none -> 7.08 us  [the longest x1 3.79 us: shards(): lax.ppermute(send_far, 'x', [(i, ((i + 1 ^ 1) - 1) % x_size) for i in ran...]
    all_to_all x1, waiting for transfers between devices: 8.34 us -> 2.39 us  [shards(): lax.all_to_all(grad_summary, DAY, split_axis=0, concat_axis=0, tiled=True)]
    all_to_all x1, blocking collectives: 31.6 us -> 27.4 us  [shards(): lax.all_to_all(partial_sums, DAY, split_axis=0, concat_axis=0, tiled=True)]
    unnamed x16 -> x12, local copies, waits for them, and re-layouts: 2.92 us -> 1 us
    ppermute x0 -> x2, waiting for transfers between devices: none -> 1.61 us  [the longest x1 1.6 us: shards(): lax.ppermute(send_far, 'x', [(i, ((i + 1 ^ 1) - 1) % x_size) for i in ran...]
  transfers between devices with their start and end apart: 3 -> 5, of which waited for: 2 -> 3; matrix products, arithmetic and copies ran while one was open for 0% -> 0% of each run, Pallas kernels for 5% -> 6%
where the time goes in v5:
time: 107 us; the launch traced here: 105 us
  blocking collectives  43.9 us (41%)
  starting transfers between devices  30.1 us (28%)
  Pallas kernels  18.6 us (17%)
  waiting for transfers between devices  10.8 us (10%)
    all_to_all x1, blocking collectives, shards(): lax.all_to_all(partial_sums, DAY, split_axis=0, concat_axis=0, tiled=True)  27.4 us
    pallas_call x7, Pallas kernels, call(): pl.pallas_call(kernel, out_shape=[pltpu.HBM(s, t) if i in out_whole + out...  18.6 us
    all_to_all x1, blocking collectives, shards(): lax.all_to_all(merged, 'rep', split_axis=0, concat_axis=0, tiled=True)  16.5 us
    all_to_all x1, starting transfers between devices, shards(): lax.all_to_all(summary, DAY, split_axis=0, concat_axis=0, tiled=True)  14.9 us
    all_to_all x1, waiting for transfers between devices, shards(): lax.all_to_all(summary, DAY, split_axis=0, concat_axis=0, tiled=True)  6.78 us
    all_to_all x1, starting transfers between devices, shards(): lax.all_to_all(grad_summary, DAY, split_axis=0, concat_axis=0, tiled=True)  5.71 us
    ppermute x1, starting transfers between devices, shards(): lax.ppermute(send_far, 'x', [(i, ((i + 1 ^ 1) - 1) % x_size) for i in ran...  3.79 us
    ppermute x1, starting transfers between devices, shards(): got_near = lax.ppermute(send_near, 'x', [(i, i ^ 1) for i in range(x_size)])  3.29 us
  transfers between devices with their start and end apart: 5, of which 3 were waited for; matrix products, arithmetic and copies ran while one was open for 0% of the time, Pallas kernels for 6%

profile of v5, /device:TPU:1, one launch (start us, length us, event | category | flops | bytes accessed | tf_op | source)
XLA Modules:
  0.0 105.2 jit_solution(12418820768422300511)
XLA Ops:
  0.6 0.0 copy-start.4
  0.6 0.0 copy-start.5
  0.7 4.2 %shard_map.86 = (bf16[64,16,128]{2,1,0:T(8,128)(2,1)}, f32[8,1024]{1,0:T(8,128)}) custom-call(s32[1,1024]{1,0:T(1,128)} %bitcast.6, s32[1,1024]{1,0:T(1,128)} %bitcast.9, bf16[8,512]{1,0:T(8,128)(2,1)} %bitcast.13, bf16[1024,512]{1,0:T(8,128)(2,1)} %events_ref.3, bf16[512,512]{1,0:T(8,128)(2,1)} %value_ref.1), custom_call_target="tpu_custom_call" | custom-call | flops 805306368 | bytes 1884160 | tf_op jit(solution)/shard_map/pallas_call | solution.py:232
  4.9 14.9 %all-to-all-start = ((bf16[64,16,128]{2,1,0:T(8,128)(2,1)}), bf16[64,16,128]{2,1,0:T(8,128)(2,1)S(1)}, u32[]{:S(2)}, u32[]{:S(2)}) async-start(bf16[64,16,128]{2,1,0:T(8,128)(2,1)} %get-tuple-element.12.summary_ref), calls=%async_computation | async-start | bytes 524288 | tf_op jit(solution)/shard_map/all_to_all | solution.py:279
  19.8 0.0 copy-done.4
  19.8 0.0 copy-done.5
  19.8 0.0 copy-start.2
  19.8 1.0 copy-done.2
  20.8 4.2 %shard_map.87 = (bf16[1024,512]{1,0:T(8,128)(2,1)}, bf16[512,1536]{1,0:T(8,128)(2,1)S(1)}) custom-call(s32[1,1024]{1,0:T(1,128)S(1)} %bitcast.7, s32[1,1024]{1,0:T(1,128)S(1)} %bitcast.10, bf16[1024,512]{1,0:T(8,128)(2,1)} %events_ref.3, bf16[512,512]{1,0:T(8,128)(2,1)} %value_ref.1, bf16[64,16,128]{2,1,0:T(8,128)(2,1)S(1)} %copy-done.2, ...), custom_call_target="tpu_custom_call" | custom-call | flops 805306368 | bytes 6037504 | tf_op jit(solution)/shard_map/pallas_call | solution.py:232
  25.0 6.8 %all-to-all-done.x_ref = bf16[64,16,128]{2,1,0:T(8,128)(2,1)S(1)} async-done(((bf16[64,16,128]{2,1,0:T(8,128)(2,1)}), bf16[64,16,128]{2,1,0:T(8,128)(2,1)S(1)}, u32[]{:S(2)}, u32[]{:S(2)}) %all-to-all-start) | async-done | bytes 262176 | tf_op jit(solution)/shard_map/all_to_all | solution.py:279
  31.7 0.0 copy-start.1
  31.8 5.9 %shard_map.88 = (bf16[64,16,128]{2,1,0:T(8,128)(2,1)}, bf16[256,1280]{1,0:T(8,128)(2,1)}, bf16[256,1280]{1,0:T(8,128)(2,1)}) custom-call(s32[1]{0:T(128)} %bitcast.3.core_ref, bf16[64,16,128]{2,1,0:T(8,128)(2,1)S(1)} %all-to-all-done.x_ref, bf16[256,512]{1,0:T(8,128)(2,1)} %bitcast.12, bf16[512,1536]{1,0:T(8,128)(2,1)S(1)} %get-tuple-element.15.qkv_weight_ref), custom_call_target="tpu_custom_call" | custom-call | flops 1744830464 | bytes 3670020 | tf_op jit(solution)/shard_map/pallas_call | solution.py:232
  37.6 0.0 copy-start
  37.6 0.0 copy-start.3
  37.7 2.5 %collective-permute-start = (bf16[256,1280]{1,0:T(8,128)(2,1)}, bf16[256,1280]{1,0:T(8,128)(2,1)S(1)}, u32[]{:S(2)}, u32[]{:S(2)}) collective-permute-start(bf16[256,1280]{1,0:T(8,128)(2,1)} %get-tuple-element.18), channel_id=1, source_target_pairs={{0,1},{1,0},{2,3},{3,2},{4,5},{5,4},{6,7},{7,6},{8,9},{9,8},{10,11... | collective-permute-start | bytes 1966088 | tf_op jit(solution)/shard_map/ppermute | solution.py:303
  40.2 5.7 %all-to-all-start.1 = ((bf16[64,16,128]{2,1,0:T(8,128)(2,1)}), bf16[64,16,128]{2,1,0:T(8,128)(2,1)S(1)}, u32[]{:S(2)}, u32[]{:S(2)}) async-start(bf16[64,16,128]{2,1,0:T(8,128)(2,1)} %get-tuple-element.16), calls=%async_computation.1 | async-start | bytes 524288 | tf_op jit(solution)/shard_map/all_to_all | solution.py:302
  45.9 0.0 collective-permute-done.theirs_ref
  45.9 2.5 %shard_map.89 = (bf16[64,8,384]{2,1,0:T(8,128)(2,1)S(1)}, bf16[64,8,256]{2,1,0:T(8,128)(2,1)}, bf16[64,8,128]{2,1,0:T(8,128)(2,1)}) custom-call(s32[1]{0:T(128)} %bitcast.5.x_ref, bf16[256,1280]{1,0:T(8,128)(2,1)} %get-tuple-element.17.mine_ref, bf16[256,1280]{1,0:T(8,128)(2,1)S(1)} %collective-permute-done.theirs_ref), custom_call_target="tpu_custom_call" | custom-call | tf_op jit(solution)/shard_map/pallas_call | solution.py:232
  48.4 3.3 %collective-permute-start.1 = (bf16[64,8,256]{2,1,0:T(8,128)(2,1)}, bf16[64,8,256]{2,1,0:T(8,128)(2,1)S(1)}, u32[]{:S(2)}, u32[]{:S(2)}) collective-permute-start(bf16[64,8,256]{2,1,0:T(8,128)(2,1)} %get-tuple-element.20), channel_id=1, source_target_pairs={{0,16},{16,0},{32,48},{48,32},{1,17},{17,1},{33,49},{49,33},{2,18}... | collective-permute-start | bytes 786440 | tf_op jit(solution)/shard_map/ppermute | solution.py:314
  51.7 3.8 %collective-permute-start.2 = (bf16[64,8,128]{2,1,0:T(8,128)(2,1)}, bf16[64,8,128]{2,1,0:T(8,128)(2,1)S(1)}, u32[]{:S(2)}, u32[]{:S(2)}) collective-permute-start(bf16[64,8,128]{2,1,0:T(8,128)(2,1)} %get-tuple-element.21), channel_id=1, source_target_pairs={{0,48},{16,32},{32,16},{48,0},{1,49},{17,33},{33,17},{49,1},{2,50}... | collective-permute-start | bytes 393224 | tf_op jit(solution)/shard_map/ppermute | solution.py:315
  55.5 2.4 %all-to-all-done.1.grad_ref = bf16[64,16,128]{2,1,0:T(8,128)(2,1)S(1)} async-done(((bf16[64,16,128]{2,1,0:T(8,128)(2,1)}), bf16[64,16,128]{2,1,0:T(8,128)(2,1)S(1)}, u32[]{:S(2)}, u32[]{:S(2)}) %all-to-all-start.1) | async-done | bytes 262176 | tf_op jit(solution)/shard_map/all_to_all | solution.py:302
  57.9 1.6 %collective-permute-done.2.far_ref = bf16[64,8,128]{2,1,0:T(8,128)(2,1)S(1)} collective-permute-done((bf16[64,8,128]{2,1,0:T(8,128)(2,1)}, bf16[64,8,128]{2,1,0:T(8,128)(2,1)S(1)}, u32[]{:S(2)}, u32[]{:S(2)}) %collective-permute-start.2) | collective-permute-done | bytes 131104 | tf_op jit(solution)/shard_map/ppermute | solution.py:315
  59.5 0.0 collective-permute-done.1.near_ref
  59.5 0.0 copy-done.1
  59.5 0.0 copy-done
  59.5 0.0 copy-done.3
  59.5 1.0 shard_map.90
  60.5 27.4 %all_to_all.20.x_ref = bf16[64,8,512]{2,1,0:T(8,128)(2,1)S(1)} all-to-all(bf16[64,8,512]{2,1,0:T(8,128)(2,1)S(1)} %shard_map.90), channel_id=1, replica_groups=mesh['rep'=8,'x'=4,'z'=8,'core'=2] {'x','z','core'}, dimensions={0} | all-to-all | bytes 1048576 | tf_op jit(solution)/shard_map/all_to_all | solution.py:322
  87.9 0.1 shard_map.91
  88.0 16.5 %all_to_all.21.x_ref = bf16[8,8,1664]{2,1,0:T(8,128)(2,1)S(1)} all-to-all(bf16[8,8,1664]{2,1,0:T(8,128)(2,1)S(1)} %shard_map.91), channel_id=1, replica_groups=mesh['rep'=8,'x'=4,'z'=8,'core'=2] {'rep'}, dimensions={0} | all-to-all | bytes 425984 | tf_op jit(solution)/shard_map/all_to_all | solution.py:326
  104.5 0.7 shard_map.92
Async XLA Ops:
  0.6 19.1 %copy-start.4 = (s32[1024]{0:T(1024)S(1)}, s32[1024]{0:T(1024)}, u32[]{:S(2)}) copy-start(s32[1024]{0:T(1024)} %param.8) | copy-start | bytes 12292
  0.6 19.1 %copy-start.5 = (s32[1024]{0:T(1024)S(1)}, s32[1024]{0:T(1024)}, u32[]{:S(2)}) copy-start(s32[1024]{0:T(1024)} %param.9) | copy-start | bytes 12292
  4.9 26.9 %all-to-all-start = ((bf16[64,16,128]{2,1,0:T(8,128)(2,1)}), bf16[64,16,128]{2,1,0:T(8,128)(2,1)S(1)}, u32[]{:S(2)}, u32[]{:S(2)}) async-start(bf16[64,16,128]{2,1,0:T(8,128)(2,1)} %get-tuple-element.12.summary_ref), calls=%async_computation | async-start | bytes 524288 | tf_op jit(solution)/shard_map/all_to_all | solution.py:279
  19.8 1.0 copy-start.2
  31.7 27.7 %copy-start.1 = (bf16[1024,512]{1,0:T(8,128)(2,1)S(1)}, bf16[1024,512]{1,0:T(8,128)(2,1)}, u32[]{:S(2)}) copy-start(bf16[1024,512]{1,0:T(8,128)(2,1)} %get-tuple-element.13.centred_ref) | copy-start | bytes 3145732
  37.6 21.9 %copy-start = (bf16[1024,512]{1,0:T(8,128)(2,1)S(1)}, bf16[1024,512]{1,0:T(8,128)(2,1)}, u32[]{:S(2)}) copy-start(bf16[1024,512]{1,0:T(8,128)(2,1)} %events_ref.3) | copy-start | bytes 3145732
  37.6 21.8 %copy-start.3 = (f32[8,1024]{1,0:T(8,128)S(1)}, f32[8,1024]{1,0:T(8,128)}, u32[]{:S(2)}) copy-start(f32[8,1024]{1,0:T(8,128)} %get-tuple-element.14.weight_ref) | copy-start | bytes 98308
  37.7 8.2 %collective-permute-start = (bf16[256,1280]{1,0:T(8,128)(2,1)}, bf16[256,1280]{1,0:T(8,128)(2,1)S(1)}, u32[]{:S(2)}, u32[]{:S(2)}) collective-permute-start(bf16[256,1280]{1,0:T(8,128)(2,1)} %get-tuple-element.18), channel_id=1, source_target_pairs={{0,1},{1,0},{2,3},{3,2},{4,5},{5,4},{6,7},{7,6},{8,9},{9,8},{10,11... | collective-permute-start | bytes 1966088 | tf_op jit(solution)/shard_map/ppermute | solution.py:303
  40.2 17.7 %all-to-all-start.1 = ((bf16[64,16,128]{2,1,0:T(8,128)(2,1)}), bf16[64,16,128]{2,1,0:T(8,128)(2,1)S(1)}, u32[]{:S(2)}, u32[]{:S(2)}) async-start(bf16[64,16,128]{2,1,0:T(8,128)(2,1)} %get-tuple-element.16), calls=%async_computation.1 | async-start | bytes 524288 | tf_op jit(solution)/shard_map/all_to_all | solution.py:302
  48.4 11.1 %collective-permute-start.1 = (bf16[64,8,256]{2,1,0:T(8,128)(2,1)}, bf16[64,8,256]{2,1,0:T(8,128)(2,1)S(1)}, u32[]{:S(2)}, u32[]{:S(2)}) collective-permute-start(bf16[64,8,256]{2,1,0:T(8,128)(2,1)} %get-tuple-element.20), channel_id=1, source_target_pairs={{0,16},{16,0},{32,48},{48,32},{1,17},{17,1},{33,49},{49,33},{2,18}... | collective-permute-start | bytes 786440 | tf_op jit(solution)/shard_map/ppermute | solution.py:314
  51.7 7.8 %collective-permute-start.2 = (bf16[64,8,128]{2,1,0:T(8,128)(2,1)}, bf16[64,8,128]{2,1,0:T(8,128)(2,1)S(1)}, u32[]{:S(2)}, u32[]{:S(2)}) collective-permute-start(bf16[64,8,128]{2,1,0:T(8,128)(2,1)} %get-tuple-element.21), channel_id=1, source_target_pairs={{0,48},{16,32},{32,16},{48,0},{1,49},{17,33},{33,17},{49,1},{2,50}... | collective-permute-start | bytes 393224 | tf_op jit(solution)/shard_map/ppermute | solution.py:315

commit v6 on v5

--- a/solution.py
+++ b/solution.py
@@ -103,10 +103,10 @@
     copy.wait()
 
 
-def attention_kernel(heads, loss_scale, core_ref, x_ref, cot_ref, qkv_weight_ref, grad_ref, mine_ref, send_ref, cot_buf, mine_buf, sems):
+def attention_kernel(heads, loss_scale, core_ref, x_ref, cot_ref, qkv_weight_ref, grad_ref, mine_ref, send_ref, cot_buf, sem):
     width = qkv_weight_ref.shape[0]
     days = cot_ref.shape[0]
-    cot_copy = pltpu.make_async_copy(cot_ref, cot_buf, sems.at[1])
+    cot_copy = pltpu.make_async_copy(cot_ref, cot_buf, sem)
     cot_copy.start()
     buckets = x_ref.shape[0]
     size = width // heads
@@ -114,7 +114,7 @@
     wide = to_rows(x_ref[...], width)
     inverse = lax.rsqrt(jnp.mean(wide * wide, axis=-1, keepdims=True) + 1e-06)
     normed = (wide * inverse).astype(BF16)
-    mine_buf[:, :width] = normed
+    mine_ref[:, :width] = normed
     send_ref[:, :width] = normed
     qkv = nn(normed, qkv_weight_ref[...]).astype(BF16)
     cot_copy.wait()
@@ -147,10 +147,8 @@
     grad_qkv = jnp.concatenate([a.astype(BF16) for part in parts for a in part], axis=1)
     half = 3 * width // 2
     first = core_ref[0] == 0
-    mine_buf[:, width:] = jnp.where(first, grad_qkv[:, :half], grad_qkv[:, half:])
+    mine_ref[:, width:] = jnp.where(first, grad_qkv[:, :half], grad_qkv[:, half:])
     send_ref[:, width:] = jnp.where(first, grad_qkv[:, half:], grad_qkv[:, :half])
-    mine_copy = pltpu.make_async_copy(mine_buf, mine_ref, sems.at[0])
-    mine_copy.start()
     grad_normed = nt(grad_qkv, qkv_weight_ref[...])
     cubed = inverse * inverse * inverse
     grad = (
@@ -159,56 +157,66 @@
         - wide * cubed * jnp.mean(grad_normed * wide, axis=-1, keepdims=True)
     )
     grad_ref[...] = to_blocks(grad, buckets)
-    mine_copy.wait()
-
-
-def outer_kernel(width, x_ref, mine_ref, theirs_ref, keep_ref, near_ref, far_ref):
+
+
+def packed(total, quarter, lane):
+    size = total.shape[0] // 2
+    start = 4 * lane + quarter * (lane // 2)
+    rest = total[:, start : start + lane // 2]
+    return jnp.concatenate([total[:, quarter * lane : (quarter + 1) * lane], jnp.concatenate([rest[:size], rest[size:]], axis=1)], axis=0)
+
+
+def outer_kernel(width, x_ref, mine_ref, theirs_ref, *out_refs):
     both = jnp.concatenate([mine_ref[...], theirs_ref[...]], axis=0)
-    total = tn(both[:, :width], both[:, width:]).astype(BF16)
-    first = x_ref[0] & 1 == 0
-    start = 0
-    for send_ref in (near_ref, far_ref):
-        parts, depth, part = send_ref.shape
-        low = total[:, 2 * start : 2 * start + part]
-        high = total[:, 2 * start + part : 2 * start + 2 * part]
-        keep_ref[:, :, start : start + part] = jnp.where(first, low, high).reshape(parts, depth, part)
-        send_ref[...] = jnp.where(first, high, low).reshape(parts, depth, part)
-        start += part
-
-
-def score_kernel(
-    users, slots, user_ref, day_ref, events_ref, centred_ref, weight_ref, grad_ref, keep_ref, near_ref, far_ref, out_ref
-):
+    total = tn(both[:, :width], both[:, width:])
+    quarters = [packed(total, i, out_refs[0].shape[1]).astype(BF16) for i in range(4)]
+    for here in range(4):
+
+        @pl.when(x_ref[0] == here)
+        def _():
+            for step, out_ref in enumerate(out_refs):
+                out_ref[...] = quarters[(here + step) % 4]
+
+
+def score_kernel(users, slots, user_ref, day_ref, events_ref, centred_ref, weight_ref, grad_ref, out_ref):
     width = events_ref.shape[1]
     heads = weight_ref.shape[0]
-    parts, depth, half = keep_ref.shape
-    lanes = out_ref.shape[2] - half
-    start = 0
-    for got_ref in (near_ref, far_ref):
-        lane = slice(start, start + got_ref.shape[2])
-        out_ref[:, :, lane] = (keep_ref[:, :, lane].astype(F32) + got_ref[...].astype(F32)).astype(BF16)
-        start += got_ref.shape[2]
+    lanes = out_ref.shape[1]
     rows = slot_rows(user_ref, day_ref, users, slots)
     grad = tn(rows, to_rows(grad_ref[...], width).astype(BF16))
     terms = (grad * centred_ref[...].astype(F32)).astype(BF16)
-    reduce = one_hot(iota((heads, width), 1) // (width // heads) == iota((heads, width), 0))
-    scores = (weight_ref[...] * nt(reduce, terms)).astype(BF16)
-    scores = jnp.concatenate([scores.astype(F32), jnp.zeros((lanes - heads, scores.shape[1]), F32)], axis=0).astype(BF16)
-    turned = jnp.transpose(nn(scores, events_ref[...]), (1, 0))
-    out_ref[:, :, half:] = turned.reshape(parts, depth, lanes).astype(BF16)
-
-
-def merge_kernel(cores, z_size, near, x_ref, out_ref):
+    reduce = one_hot(iota((lanes, width), 1) // (width // heads) == iota((lanes, width), 0) - lanes // 2)
+    weight = weight_ref[...]
+    blank = jnp.zeros((lanes // 2, weight.shape[1]), F32)
+    weight = jnp.concatenate([blank, weight, blank[heads:]], axis=0)
+    scores = (weight * nt(reduce, terms)).astype(BF16)
+    out_ref[...] = jnp.transpose(nn(scores, events_ref[...]), (1, 0))
+
+
+def join_kernel(score_ref, own_ref, a_ref, b_ref, c_ref, out_ref):
+    width = score_ref.shape[0]
+    parts, depth, _ = out_ref.shape
+    total = own_ref[...].astype(F32) + a_ref[...].astype(F32) + b_ref[...].astype(F32) + c_ref[...].astype(F32)
+    lanes = total.shape[1]
+    size = lanes // 2
+    out_ref[:, :, :lanes] = total[:width].reshape(parts, depth, lanes).astype(BF16)
+    rest = total[width:]
+    rest = jnp.concatenate([rest[:, :size], rest[:, size:]], axis=0)
+    both = jnp.concatenate([rest, score_ref[:, size:]], axis=1)
+    out_ref[:, :, lanes:] = both.reshape(parts, depth, lanes).astype(BF16)
+
+
+def merge_kernel(cores, x_size, x_ref, out_ref):
     parts, depth, columns = x_ref.shape
-    kept = columns - 128
-    pairs = parts // (2 * z_size * cores)
-    x = x_ref[...].astype(F32).reshape(pairs, 2, z_size, cores, depth, columns)
-    total = jnp.sum(jnp.sum(x, axis=0), axis=1)
+    lanes = columns // 2
+    x = x_ref[...].astype(F32).reshape(x_size, parts // (x_size * cores), cores, depth, columns)
+    total = jnp.sum(x, axis=1)
     pieces = []
     for core in range(cores):
-        for lane in (slice(0, near), slice(near, kept)):
-            pieces += [total[0, core, :, lane], total[1, core, :, lane]]
-    pieces.append(jnp.sum(total[:, :, :, kept:], axis=(0, 1)))
+        pieces += [total[i, core, :, :lanes] for i in range(x_size)]
+        pieces += [total[i, core, :, lanes : lanes + lanes // 2] for i in range(x_size)]
+    score = jnp.sum(total[:, :, :, lanes + lanes // 2 :], axis=(0, 1))
+    pieces += [score, jnp.zeros_like(score)]
     merged = jnp.concatenate(pieces, axis=1).astype(BF16)
     for i in range(out_ref.shape[0]):
         out_ref[i] = merged
@@ -295,34 +303,30 @@
         scalars=1,
         whole=(2,),
         flops=2 * days * width * (6 * width + 14 * days),
-        out_whole=(1,),
-        out_near=(2,),
-        scratch=[pltpu.VMEM((days, width), BF16), pltpu.VMEM((days, width + half), BF16), pltpu.SemaphoreType.DMA((2,))],
+        out_near=(1, 2),
+        scratch=[pltpu.VMEM((days, width), BF16), pltpu.SemaphoreType.DMA],
     )
     grad_days = lax.all_to_all(grad_summary, DAY, split_axis=0, concat_axis=0, tiled=True)
     theirs = lax.ppermute(send, "core", [(i, cores - 1 - i) for i in range(cores)])
     x_row = lax.axis_index("x").reshape(1)
-    near, far = width // 2, width // 4
-    keep, send_near, send_far = call(
+    packs = call(
         functools.partial(outer_kernel, width),
-        [((buckets, rows, columns), BF16) for columns in (near + far, near, far)],
+        [((width + width // 2, 128), BF16)] * x_size,
         (x_row, mine, theirs),
         scalars=1,
         moved=0,
-        held=(1,),
-    )
-    got_near = lax.ppermute(send_near, "x", [(i, i ^ 1) for i in range(x_size)])
-    got_far = lax.ppermute(send_far, "x", [(i, (((i + 1) ^ 1) - 1) % x_size) for i in range(x_size)])
-    (partial_sums,) = call(
+    )
+    got = [lax.ppermute(packs[k], "x", [(i, (i + k) % x_size) for i in range(x_size)]) for k in (2, 1, 3)]
+    (score,) = call(
         functools.partial(score_kernel, users, slots),
-        [((buckets, rows, near + far + 128), BF16)],
-        (user_row, day_row, events, centred, weight, grad_days, keep, got_near, got_far),
+        [((width, 128), F32)],
+        (user_row, day_row, events, centred, weight, grad_days),
+        held=(2, 3),
         flops=2 * count * width * (slots + 256),
     )
+    (partial_sums,) = call(join_kernel, [((buckets, rows, 256), BF16)], (score, packs[0], *got))
     gathered = lax.all_to_all(partial_sums, DAY, split_axis=0, concat_axis=0, tiled=True)
-    (merged,) = call(
-        functools.partial(merge_kernel, cores, z_size, near), [((groups, rows, 3 * width + 128), BF16)], (gathered,)
-    )
+    (merged,) = call(functools.partial(merge_kernel, cores, x_size), [((groups, rows, 3 * width + 128), BF16)], (gathered,))
     everyone = lax.all_to_all(merged, "rep", split_axis=0, concat_axis=0, tiled=True)
     return tuple(call(final_kernel, [((rows, 3 * width), F32), ((rows, heads), F32)], (everyone,)))
 

time: 107 us -> 103 us (0.963)
  blocking collectives: 43.9 us -> 38.3 us
  starting transfers between devices: 30.1 us -> 34.3 us
  waiting for transfers between devices: 10.8 us -> 9.41 us
    all_to_all x1, blocking collectives: 27.4 us -> 22 us  [shards(): lax.all_to_all(partial_sums, DAY, split_axis=0, concat_axis=0, tiled=True)]
    ppermute x2 -> x3, starting transfers between devices: 7.08 us -> 11.4 us  [shards(): lax.ppermute(packs[k], 'x', [(i, (i + k) % x_size) for i in range(x_size)])]
    all_to_all x1, waiting for transfers between devices: 2.39 us -> 0.01 us  [shards(): lax.all_to_all(grad_summary, DAY, split_axis=0, concat_axis=0, tiled=True)]
    ppermute x2 -> x3, waiting for transfers between devices: 1.61 us -> 2.63 us  [shards(): lax.ppermute(packs[k], 'x', [(i, (i + k) % x_size) for i in range(x_size)])]
    pallas_call x7 -> x8, Pallas kernels: 18.6 us -> 17.7 us  [call(): pl.pallas_call(kernel, out_shape=[pltpu.HBM(s, t) if i in out_whole + out...]
  transfers between devices with their start and end apart: 5 -> 6, of which waited for: 3 -> 2; matrix products, arithmetic and copies ran while one was open for 0% -> 0% of each run, Pallas kernels for 6% -> 7%
where the time goes in v6:
time: 103 us; the launch traced here: 102 us
  blocking collectives  38.3 us (37%)
  starting transfers between devices  34.3 us (33%)
  Pallas kernels  17.7 us (17%)
  waiting for transfers between devices  9.41 us (9%)
    all_to_all x1, blocking collectives, shards(): lax.all_to_all(partial_sums, DAY, split_axis=0, concat_axis=0, tiled=True)  22 us
    pallas_call x8, Pallas kernels, call(): pl.pallas_call(kernel, out_shape=[pltpu.HBM(s, t) if i in out_whole + out...  17.7 us
    all_to_all x1, blocking collectives, shards(): lax.all_to_all(merged, 'rep', split_axis=0, concat_axis=0, tiled=True)  16.3 us
    all_to_all x1, starting transfers between devices, shards(): lax.all_to_all(summary, DAY, split_axis=0, concat_axis=0, tiled=True)  14.9 us
    ppermute x3, starting transfers between devices, shards(): lax.ppermute(packs[k], 'x', [(i, (i + k) % x_size) for i in range(x_size)])  11.4 us
    all_to_all x1, waiting for transfers between devices, shards(): lax.all_to_all(summary, DAY, split_axis=0, concat_axis=0, tiled=True)  6.77 us
    all_to_all x1, starting transfers between devices, shards(): lax.all_to_all(grad_summary, DAY, split_axis=0, concat_axis=0, tiled=True)  5.7 us
    ppermute x3, waiting for transfers between devices, shards(): lax.ppermute(packs[k], 'x', [(i, (i + k) % x_size) for i in range(x_size)])  2.63 us
  transfers between devices with their start and end apart: 6, of which 2 were waited for; matrix products, arithmetic and copies ran while one was open for 0% of the time, Pallas kernels for 7%

profile of v6, /device:TPU:1, one launch (start us, length us, event | category | flops | bytes accessed | tf_op | source)
XLA Modules:
  0.0 101.6 jit_solution(6783429683582795932)
XLA Ops:
  0.6 0.0 copy-start.2
  0.6 0.0 copy-start.3
  0.7 4.2 %shard_map.86 = (bf16[64,16,128]{2,1,0:T(8,128)(2,1)}, f32[8,1024]{1,0:T(8,128)}) custom-call(s32[1,1024]{1,0:T(1,128)} %bitcast.6, s32[1,1024]{1,0:T(1,128)} %bitcast.9, bf16[8,512]{1,0:T(8,128)(2,1)} %bitcast.13, bf16[1024,512]{1,0:T(8,128)(2,1)} %events_ref.3, bf16[512,512]{1,0:T(8,128)(2,1)} %value_ref.1), custom_call_target="tpu_custom_call" | custom-call | flops 805306368 | bytes 1884160 | tf_op jit(solution)/shard_map/pallas_call | solution.py:240
  4.9 14.9 %all-to-all-start = ((bf16[64,16,128]{2,1,0:T(8,128)(2,1)}), bf16[64,16,128]{2,1,0:T(8,128)(2,1)S(1)}, u32[]{:S(2)}, u32[]{:S(2)}) async-start(bf16[64,16,128]{2,1,0:T(8,128)(2,1)} %get-tuple-element.13.summary_ref), calls=%async_computation | async-start | bytes 524288 | tf_op jit(solution)/shard_map/all_to_all | solution.py:287
  19.7 0.0 copy-done.2
  19.8 0.0 copy-done.3
  19.8 0.0 copy-start
  19.8 1.0 copy-done
  20.7 4.2 %shard_map.87 = (bf16[1024,512]{1,0:T(8,128)(2,1)}, bf16[512,1536]{1,0:T(8,128)(2,1)S(1)}) custom-call(s32[1,1024]{1,0:T(1,128)S(1)} %bitcast.7, s32[1,1024]{1,0:T(1,128)S(1)} %bitcast.10, bf16[1024,512]{1,0:T(8,128)(2,1)} %events_ref.3, bf16[512,512]{1,0:T(8,128)(2,1)} %value_ref.1, bf16[64,16,128]{2,1,0:T(8,128)(2,1)S(1)} %copy-done, bf16[512,1536]{1,0:T(8,128)(2,1)} %qkv_ref.1), custom_call_target="tpu_custom_call" | custom-call | flops 805306368 | bytes 6037504 | tf_op jit(solution)/shard_map/pallas_call | solution.py:240
  25.0 6.8 %all-to-all-done.x_ref = bf16[64,16,128]{2,1,0:T(8,128)(2,1)S(1)} async-done(((bf16[64,16,128]{2,1,0:T(8,128)(2,1)}), bf16[64,16,128]{2,1,0:T(8,128)(2,1)S(1)}, u32[]{:S(2)}, u32[]{:S(2)}) %all-to-all-start) | async-done | bytes 262176 | tf_op jit(solution)/shard_map/all_to_all | solution.py:287
  31.7 5.0 %shard_map.88 = (bf16[64,16,128]{2,1,0:T(8,128)(2,1)}, bf16[256,1280]{1,0:T(8,128)(2,1)S(1)}, bf16[256,1280]{1,0:T(8,128)(2,1)}) custom-call(s32[1]{0:T(128)} %bitcast.3.core_ref, bf16[64,16,128]{2,1,0:T(8,128)(2,1)S(1)} %all-to-all-done.x_ref, bf16[256,512]{1,0:T(8,128)(2,1)} %bitcast.12, bf16[512,1536]{1,0:T(8,128)(2,1)S(1)} %get-tuple-element.16.qkv_weight_ref), custom_call_target="tpu_custom_call" | custom-call | flops 1744830464 | bytes 3670020 | tf_op jit(solution)/shard_map/pallas_call | solution.py:240
  36.8 0.0 copy-start.1
  36.8 2.4 %collective-permute-start = (bf16[256,1280]{1,0:T(8,128)(2,1)}, bf16[256,1280]{1,0:T(8,128)(2,1)S(1)}, u32[]{:S(2)}, u32[]{:S(2)}) collective-permute-start(bf16[256,1280]{1,0:T(8,128)(2,1)} %get-tuple-element.19), channel_id=1, source_target_pairs={{0,1},{1,0},{2,3},{3,2},{4,5},{5,4},{6,7},{7,6},{8,9},{9,8},{10,11... | collective-permute-start | bytes 1966088 | tf_op jit(solution)/shard_map/ppermute | solution.py:310
  39.1 5.7 %all-to-all-start.1 = ((bf16[64,16,128]{2,1,0:T(8,128)(2,1)}), bf16[64,16,128]{2,1,0:T(8,128)(2,1)S(1)}, u32[]{:S(2)}, u32[]{:S(2)}) async-start(bf16[64,16,128]{2,1,0:T(8,128)(2,1)} %get-tuple-element.17), calls=%async_computation.1 | async-start | bytes 524288 | tf_op jit(solution)/shard_map/all_to_all | solution.py:309
  44.9 0.0 collective-permute-done.theirs_ref
  44.9 0.8 shard_map.90
  45.6 4.9 %collective-permute-start.1 = (bf16[768,128]{1,0:T(8,128)(2,1)S(1)}, bf16[768,128]{1,0:T(8,128)(2,1)S(1)}, u32[]{:S(2)}, u32[]{:S(2)}) collective-permute-start(bf16[768,128]{1,0:T(8,128)(2,1)S(1)} %get-tuple-element.21), channel_id=1, source_target_pairs={{0,32},{16,48},{32,0},{48,16},{1,33},{17,49},{33,1},{49,17},{2,34}... | collective-permute-start | bytes 589832 | tf_op jit(solution)/shard_map/ppermute | solution.py:319
  50.5 2.3 %collective-permute-start.2 = (bf16[768,128]{1,0:T(8,128)(2,1)S(1)}, bf16[768,128]{1,0:T(8,128)(2,1)S(1)}, u32[]{:S(2)}, u32[]{:S(2)}) collective-permute-start(bf16[768,128]{1,0:T(8,128)(2,1)S(1)} %get-tuple-element.22), channel_id=1, source_target_pairs={{0,16},{16,32},{32,48},{48,0},{1,17},{17,33},{33,49},{49,1},{2,18}... | collective-permute-start | bytes 589832 | tf_op jit(solution)/shard_map/ppermute | solution.py:319
  52.9 4.2 %collective-permute-start.3 = (bf16[768,128]{1,0:T(8,128)(2,1)S(1)}, bf16[768,128]{1,0:T(8,128)(2,1)S(1)}, u32[]{:S(2)}, u32[]{:S(2)}) collective-permute-start(bf16[768,128]{1,0:T(8,128)(2,1)S(1)} %get-tuple-element.23), channel_id=1, source_target_pairs={{0,48},{16,0},{32,16},{48,32},{1,49},{17,1},{33,17},{49,33},{2,50}... | collective-permute-start | bytes 589832 | tf_op jit(solution)/shard_map/ppermute | solution.py:319
  57.1 0.0 all-to-all-done.1.grad_ref
  57.1 0.0 copy-done.1
  57.1 2.6 %shard_map.89.score_ref = f32[512,128]{1,0:T(8,128)S(1)} custom-call(s32[1,1024]{1,0:T(1,128)S(1)} %bitcast.8, s32[1,1024]{1,0:T(1,128)S(1)} %bitcast.11, bf16[1024,512]{1,0:T(8,128)(2,1)} %events_ref.3, bf16[1024,512]{1,0:T(8,128)(2,1)} %get-tuple-element.14.centred_ref, f32[8,1024]{1,0:T(8,128)S(1)} %copy-done.1, ...), custom_call_target="tpu_custom_call" | custom-call | flops 536870912 | bytes 2662400 | tf_op jit(solution)/shard_map/pallas_call | solution.py:240
  59.6 0.0 collective-permute-done.1.a_ref
  59.7 2.6 %collective-permute-done.2.b_ref = bf16[768,128]{1,0:T(8,128)(2,1)S(1)} collective-permute-done((bf16[768,128]{1,0:T(8,128)(2,1)S(1)}, bf16[768,128]{1,0:T(8,128)(2,1)S(1)}, u32[]{:S(2)}, u32[]{:S(2)}) %collective-permute-start.2) | collective-permute-done | bytes 196640 | tf_op jit(solution)/shard_map/ppermute | solution.py:319
  62.3 0.0 collective-permute-done.3.c_ref
  62.3 0.2 shard_map.91
  62.5 22.0 %all_to_all.20.x_ref = bf16[64,8,256]{2,1,0:T(8,128)(2,1)S(1)} all-to-all(bf16[64,8,256]{2,1,0:T(8,128)(2,1)S(1)} %shard_map.91), channel_id=1, replica_groups=mesh['rep'=8,'x'=4,'z'=8,'core'=2] {'x','z','core'}, dimensions={0} | all-to-all | bytes 524288 | tf_op jit(solution)/shard_map/all_to_all | solution.py:328
  84.5 0.1 shard_map.92
  84.6 16.3 %all_to_all.21.x_ref = bf16[8,8,1664]{2,1,0:T(8,128)(2,1)S(1)} all-to-all(bf16[8,8,1664]{2,1,0:T(8,128)(2,1)S(1)} %shard_map.92), channel_id=1, replica_groups=mesh['rep'=8,'x'=4,'z'=8,'core'=2] {'rep'}, dimensions={0} | all-to-all | bytes 425984 | tf_op jit(solution)/shard_map/all_to_all | solution.py:330
  100.9 0.7 shard_map.93
Async XLA Ops:
  0.6 19.1 %copy-start.2 = (s32[1024]{0:T(1024)S(1)}, s32[1024]{0:T(1024)}, u32[]{:S(2)}) copy-start(s32[1024]{0:T(1024)} %param.8) | copy-start | bytes 12292
  0.6 19.1 %copy-start.3 = (s32[1024]{0:T(1024)S(1)}, s32[1024]{0:T(1024)}, u32[]{:S(2)}) copy-start(s32[1024]{0:T(1024)} %param.9) | copy-start | bytes 12292
  4.9 26.9 %all-to-all-start = ((bf16[64,16,128]{2,1,0:T(8,128)(2,1)}), bf16[64,16,128]{2,1,0:T(8,128)(2,1)S(1)}, u32[]{:S(2)}, u32[]{:S(2)}) async-start(bf16[64,16,128]{2,1,0:T(8,128)(2,1)} %get-tuple-element.13.summary_ref), calls=%async_computation | async-start | bytes 524288 | tf_op jit(solution)/shard_map/all_to_all | solution.py:287
  19.8 1.0 copy-start
  36.8 20.3 %copy-start.1 = (f32[8,1024]{1,0:T(8,128)S(1)}, f32[8,1024]{1,0:T(8,128)}, u32[]{:S(2)}) copy-start(f32[8,1024]{1,0:T(8,128)} %get-tuple-element.15.weight_ref) | copy-start | bytes 98308
  36.8 8.1 %collective-permute-start = (bf16[256,1280]{1,0:T(8,128)(2,1)}, bf16[256,1280]{1,0:T(8,128)(2,1)S(1)}, u32[]{:S(2)}, u32[]{:S(2)}) collective-permute-start(bf16[256,1280]{1,0:T(8,128)(2,1)} %get-tuple-element.19), channel_id=1, source_target_pairs={{0,1},{1,0},{2,3},{3,2},{4,5},{5,4},{6,7},{7,6},{8,9},{9,8},{10,11... | collective-permute-start | bytes 1966088 | tf_op jit(solution)/shard_map/ppermute | solution.py:310
  39.1 17.9 %all-to-all-start.1 = ((bf16[64,16,128]{2,1,0:T(8,128)(2,1)}), bf16[64,16,128]{2,1,0:T(8,128)(2,1)S(1)}, u32[]{:S(2)}, u32[]{:S(2)}) async-start(bf16[64,16,128]{2,1,0:T(8,128)(2,1)} %get-tuple-element.17), calls=%async_computation.1 | async-start | bytes 524288 | tf_op jit(solution)/shard_map/all_to_all | solution.py:309
  45.6 14.0 %collective-permute-start.1 = (bf16[768,128]{1,0:T(8,128)(2,1)S(1)}, bf16[768,128]{1,0:T(8,128)(2,1)S(1)}, u32[]{:S(2)}, u32[]{:S(2)}) collective-permute-start(bf16[768,128]{1,0:T(8,128)(2,1)S(1)} %get-tuple-element.21), channel_id=1, source_target_pairs={{0,32},{16,48},{32,0},{48,16},{1,33},{17,49},{33,1},{49,17},{2,34}... | collective-permute-start | bytes 589832 | tf_op jit(solution)/shard_map/ppermute | solution.py:319
  50.5 11.7 %collective-permute-start.2 = (bf16[768,128]{1,0:T(8,128)(2,1)S(1)}, bf16[768,128]{1,0:T(8,128)(2,1)S(1)}, u32[]{:S(2)}, u32[]{:S(2)}) collective-permute-start(bf16[768,128]{1,0:T(8,128)(2,1)S(1)} %get-tuple-element.22), channel_id=1, source_target_pairs={{0,16},{16,32},{32,48},{48,0},{1,17},{17,33},{33,49},{49,1},{2,18}... | collective-permute-start | bytes 589832 | tf_op jit(solution)/shard_map/ppermute | solution.py:319
  52.9 9.4 %collective-permute-start.3 = (bf16[768,128]{1,0:T(8,128)(2,1)S(1)}, bf16[768,128]{1,0:T(8,128)(2,1)S(1)}, u32[]{:S(2)}, u32[]{:S(2)}) collective-permute-start(bf16[768,128]{1,0:T(8,128)(2,1)S(1)} %get-tuple-element.23), channel_id=1, source_target_pairs={{0,48},{16,0},{32,16},{48,32},{1,49},{17,1},{33,17},{49,33},{2,50}... | collective-permute-start | bytes 589832 | tf_op jit(solution)/shard_map/ppermute | solution.py:319

commit v7 on v6

--- a/solution.py
+++ b/solution.py
@@ -159,64 +159,48 @@
     grad_ref[...] = to_blocks(grad, buckets)
 
 
-def packed(total, quarter, lane):
-    size = total.shape[0] // 2
-    start = 4 * lane + quarter * (lane // 2)
-    rest = total[:, start : start + lane // 2]
-    return jnp.concatenate([total[:, quarter * lane : (quarter + 1) * lane], jnp.concatenate([rest[:size], rest[size:]], axis=1)], axis=0)
-
-
 def outer_kernel(width, x_ref, mine_ref, theirs_ref, *out_refs):
     both = jnp.concatenate([mine_ref[...], theirs_ref[...]], axis=0)
-    total = tn(both[:, :width], both[:, width:])
-    quarters = [packed(total, i, out_refs[0].shape[1]).astype(BF16) for i in range(4)]
-    for here in range(4):
+    total = tn(both[:, :width], both[:, width:]).astype(BF16)
+    count = len(out_refs)
+    size = width // count
+    for here in range(count):
 
         @pl.when(x_ref[0] == here)
         def _():
             for step, out_ref in enumerate(out_refs):
-                out_ref[...] = quarters[(here + step) % 4]
+                start = (here + step) % count * size
+                out_ref[...] = total[start : start + size]
 
 
 def score_kernel(users, slots, user_ref, day_ref, events_ref, centred_ref, weight_ref, grad_ref, out_ref):
     width = events_ref.shape[1]
-    heads = weight_ref.shape[0]
-    lanes = out_ref.shape[1]
+    planes, heads, lanes = out_ref.shape
     rows = slot_rows(user_ref, day_ref, users, slots)
     grad = tn(rows, to_rows(grad_ref[...], width).astype(BF16))
     terms = (grad * centred_ref[...].astype(F32)).astype(BF16)
-    reduce = one_hot(iota((lanes, width), 1) // (width // heads) == iota((lanes, width), 0) - lanes // 2)
-    weight = weight_ref[...]
-    blank = jnp.zeros((lanes // 2, weight.shape[1]), F32)
-    weight = jnp.concatenate([blank, weight, blank[heads:]], axis=0)
-    scores = (weight * nt(reduce, terms)).astype(BF16)
-    out_ref[...] = jnp.transpose(nn(scores, events_ref[...]), (1, 0))
+    reduce = one_hot(iota((heads, width), 1) // (width // heads) == iota((heads, width), 0))
+    scores = (weight_ref[...] * nt(reduce, terms)).astype(BF16)
+    spread = nn(scores, events_ref[...])
+    for i in range(planes):
+        out_ref[i] = spread[:, i * lanes : (i + 1) * lanes].astype(BF16)
 
 
 def join_kernel(score_ref, own_ref, a_ref, b_ref, c_ref, out_ref):
-    width = score_ref.shape[0]
-    parts, depth, _ = out_ref.shape
+    parts, depth, columns = out_ref.shape
+    lanes = score_ref.shape[2]
     total = own_ref[...].astype(F32) + a_ref[...].astype(F32) + b_ref[...].astype(F32) + c_ref[...].astype(F32)
-    lanes = total.shape[1]
-    size = lanes // 2
-    out_ref[:, :, :lanes] = total[:width].reshape(parts, depth, lanes).astype(BF16)
-    rest = total[width:]
-    rest = jnp.concatenate([rest[:, :size], rest[:, size:]], axis=0)
-    both = jnp.concatenate([rest, score_ref[:, size:]], axis=1)
-    out_ref[:, :, lanes:] = both.reshape(parts, depth, lanes).astype(BF16)
-
-
-def merge_kernel(cores, x_size, x_ref, out_ref):
+    out_ref[:, :, : columns - lanes] = total.reshape(parts, depth, columns - lanes).astype(BF16)
+    score = jnp.sum(score_ref[...].astype(F32), axis=0)
+    blank = jnp.zeros((lanes - score.shape[0], lanes), F32)
+    turned = jnp.transpose(jnp.concatenate([score, blank], axis=0), (1, 0))
+    out_ref[:, :, columns - lanes :] = turned.reshape(parts, depth, lanes).astype(BF16)
+
+
+def merge_kernel(cores, half, x_ref, out_ref):
     parts, depth, columns = x_ref.shape
-    lanes = columns // 2
-    x = x_ref[...].astype(F32).reshape(x_size, parts // (x_size * cores), cores, depth, columns)
-    total = jnp.sum(x, axis=1)
-    pieces = []
-    for core in range(cores):
-        pieces += [total[i, core, :, :lanes] for i in range(x_size)]
-        pieces += [total[i, core, :, lanes : lanes + lanes // 2] for i in range(x_size)]
-    score = jnp.sum(total[:, :, :, lanes + lanes // 2 :], axis=(0, 1))
-    pieces += [score, jnp.zeros_like(score)]
+    total = jnp.sum(x_ref[...].astype(F32).reshape(parts // cores, cores, depth, columns), axis=0)
+    pieces = [total[core, :, :half] for core in range(cores)] + [jnp.sum(total[:, :, half:], axis=0)]
     merged = jnp.concatenate(pieces, axis=1).astype(BF16)
     for i in range(out_ref.shape[0]):
         out_ref[i] = merged
@@ -309,9 +293,10 @@
     grad_days = lax.all_to_all(grad_summary, DAY, split_axis=0, concat_axis=0, tiled=True)
     theirs = lax.ppermute(send, "core", [(i, cores - 1 - i) for i in range(cores)])
     x_row = lax.axis_index("x").reshape(1)
+    plane = width // x_size
     packs = call(
         functools.partial(outer_kernel, width),
-        [((width + width // 2, 128), BF16)] * x_size,
+        [((plane, half), BF16)] * x_size,
         (x_row, mine, theirs),
         scalars=1,
         moved=0,
@@ -319,14 +304,19 @@
     got = [lax.ppermute(packs[k], "x", [(i, (i + k) % x_size) for i in range(x_size)]) for k in (2, 1, 3)]
     (score,) = call(
         functools.partial(score_kernel, users, slots),
-        [((width, 128), F32)],
+        [((x_size, heads, plane), BF16)],
         (user_row, day_row, events, centred, weight, grad_days),
         held=(2, 3),
         flops=2 * count * width * (slots + 256),
     )
-    (partial_sums,) = call(join_kernel, [((buckets, rows, 256), BF16)], (score, packs[0], *got))
-    gathered = lax.all_to_all(partial_sums, DAY, split_axis=0, concat_axis=0, tiled=True)
-    (merged,) = call(functools.partial(merge_kernel, cores, x_size), [((groups, rows, 3 * width + 128), BF16)], (gathered,))
+    score_rows = lax.all_to_all(score, "x", split_axis=0, concat_axis=0, tiled=True)
+    (partial_sums,) = call(
+        join_kernel, [((z_size * cores, rows, half + plane), BF16)], (score_rows, packs[0], *got)
+    )
+    gathered = lax.all_to_all(partial_sums, ("z", "core"), split_axis=0, concat_axis=0, tiled=True)
+    (merged,) = call(
+        functools.partial(merge_kernel, cores, half), [((groups, rows, 3 * width + plane), BF16)], (gathered,)
+    )
     everyone = lax.all_to_all(merged, "rep", split_axis=0, concat_axis=0, tiled=True)
     return tuple(call(final_kernel, [((rows, 3 * width), F32), ((rows, heads), F32)], (everyone,)))
 

time: 103 us -> 105 us (1.019); the launches traced: 102 us -> 105 us
  blocking collectives: 38.3 us -> 44.4 us
  waiting for transfers between devices: 9.41 us -> 6.79 us
    all_to_all x1 -> x2, blocking collectives: 22 us -> 26.4 us  [the longest x1 18.8 us: shards(): lax.all_to_all(partial_sums, ('z', 'core'), split_axis=0, concat_axis=0,...]
    ppermute x3, waiting for transfers between devices: 2.63 us -> 0.01 us  [shards(): lax.ppermute(packs[k], 'x', [(i, (i + k) % x_size) for i in range(x_size)])]
    all_to_all x1, blocking collectives: 16.3 us -> 18 us  [shards(): lax.all_to_all(merged, 'rep', split_axis=0, concat_axis=0, tiled=True)]
  transfers between devices with their start and end apart: 6 -> 6, of which waited for: 2 -> 1; matrix products, arithmetic and copies ran while one was open for 0% -> 0% of each run, Pallas kernels for 7% -> 7%
where the time goes in v7:
time: 105 us
  blocking collectives  44.4 us (42%)
  starting transfers between devices  34.3 us (33%)
  Pallas kernels  17.4 us (17%)
  waiting for transfers between devices  6.79 us (6%)
    all_to_all x1, blocking collectives, shards(): lax.all_to_all(partial_sums, ('z', 'core'), split_axis=0, concat_axis=0,...  18.8 us
    all_to_all x1, blocking collectives, shards(): lax.all_to_all(merged, 'rep', split_axis=0, concat_axis=0, tiled=True)  18 us
    pallas_call x8, Pallas kernels, call(): pl.pallas_call(kernel, out_shape=[pltpu.HBM(s, t) if i in out_whole + out...  17.4 us
    all_to_all x1, starting transfers between devices, shards(): lax.all_to_all(summary, DAY, split_axis=0, concat_axis=0, tiled=True)  14.9 us
    ppermute x3, starting transfers between devices, shards(): lax.ppermute(packs[k], 'x', [(i, (i + k) % x_size) for i in range(x_size)])  11.4 us
    all_to_all x1, blocking collectives, shards(): lax.all_to_all(score, 'x', split_axis=0, concat_axis=0, tiled=True)  7.61 us
    all_to_all x1, waiting for transfers between devices, shards(): lax.all_to_all(summary, DAY, split_axis=0, concat_axis=0, tiled=True)  6.77 us
    all_to_all x1, starting transfers between devices, shards(): lax.all_to_all(grad_summary, DAY, split_axis=0, concat_axis=0, tiled=True)  5.7 us
  transfers between devices with their start and end apart: 6, of which 1 were waited for; matrix products, arithmetic and copies ran while one was open for 0% of the time, Pallas kernels for 7%

profile of v7, /device:TPU:1, one launch (start us, length us, event | category | flops | bytes accessed | tf_op | source)
XLA Modules:
  0.0 104.6 jit_solution(6384591462994013972)
XLA Ops:
  0.6 0.0 copy-start.2
  0.6 0.0 copy-start.3
  0.7 4.2 %shard_map.86 = (bf16[64,16,128]{2,1,0:T(8,128)(2,1)}, f32[8,1024]{1,0:T(8,128)}) custom-call(s32[1,1024]{1,0:T(1,128)} %bitcast.6, s32[1,1024]{1,0:T(1,128)} %bitcast.9, bf16[8,512]{1,0:T(8,128)(2,1)} %bitcast.13, bf16[1024,512]{1,0:T(8,128)(2,1)} %events_ref.3, bf16[512,512]{1,0:T(8,128)(2,1)} %value_ref.1), custom_call_target="tpu_custom_call" | custom-call | flops 805306368 | bytes 1884160 | tf_op jit(solution)/shard_map/pallas_call | solution.py:224
  4.9 14.9 %all-to-all-start = ((bf16[64,16,128]{2,1,0:T(8,128)(2,1)}), bf16[64,16,128]{2,1,0:T(8,128)(2,1)S(1)}, u32[]{:S(2)}, u32[]{:S(2)}) async-start(bf16[64,16,128]{2,1,0:T(8,128)(2,1)} %get-tuple-element.13.summary_ref), calls=%async_computation | async-start | bytes 524288 | tf_op jit(solution)/shard_map/all_to_all | solution.py:271
  19.7 0.0 copy-done.2
  19.8 0.0 copy-done.3
  19.8 0.0 copy-start
  19.8 1.0 copy-done
  20.7 4.2 %shard_map.87 = (bf16[1024,512]{1,0:T(8,128)(2,1)}, bf16[512,1536]{1,0:T(8,128)(2,1)S(1)}) custom-call(s32[1,1024]{1,0:T(1,128)S(1)} %bitcast.7, s32[1,1024]{1,0:T(1,128)S(1)} %bitcast.10, bf16[1024,512]{1,0:T(8,128)(2,1)} %events_ref.3, bf16[512,512]{1,0:T(8,128)(2,1)} %value_ref.1, bf16[64,16,128]{2,1,0:T(8,128)(2,1)S(1)} %copy-done, bf16[512,1536]{1,0:T(8,128)(2,1)} %qkv_ref.1), custom_call_target="tpu_custom_call" | custom-call | flops 805306368 | bytes 6037504 | tf_op jit(solution)/shard_map/pallas_call | solution.py:224
  25.0 6.8 %all-to-all-done.x_ref = bf16[64,16,128]{2,1,0:T(8,128)(2,1)S(1)} async-done(((bf16[64,16,128]{2,1,0:T(8,128)(2,1)}), bf16[64,16,128]{2,1,0:T(8,128)(2,1)S(1)}, u32[]{:S(2)}, u32[]{:S(2)}) %all-to-all-start) | async-done | bytes 262176 | tf_op jit(solution)/shard_map/all_to_all | solution.py:271
  31.7 5.0 %shard_map.88 = (bf16[64,16,128]{2,1,0:T(8,128)(2,1)}, bf16[256,1280]{1,0:T(8,128)(2,1)S(1)}, bf16[256,1280]{1,0:T(8,128)(2,1)}) custom-call(s32[1]{0:T(128)} %bitcast.3.core_ref, bf16[64,16,128]{2,1,0:T(8,128)(2,1)S(1)} %all-to-all-done.x_ref, bf16[256,512]{1,0:T(8,128)(2,1)} %bitcast.12, bf16[512,1536]{1,0:T(8,128)(2,1)S(1)} %get-tuple-element.16.qkv_weight_ref), custom_call_target="tpu_custom_call" | custom-call | flops 1744830464 | bytes 3670020 | tf_op jit(solution)/shard_map/pallas_call | solution.py:224
  36.8 0.0 copy-start.1
  36.8 2.4 %collective-permute-start = (bf16[256,1280]{1,0:T(8,128)(2,1)}, bf16[256,1280]{1,0:T(8,128)(2,1)S(1)}, u32[]{:S(2)}, u32[]{:S(2)}) collective-permute-start(bf16[256,1280]{1,0:T(8,128)(2,1)} %get-tuple-element.19), channel_id=1, source_target_pairs={{0,1},{1,0},{2,3},{3,2},{4,5},{5,4},{6,7},{7,6},{8,9},{9,8},{10,11... | collective-permute-start | bytes 1966088 | tf_op jit(solution)/shard_map/ppermute | solution.py:294
  39.1 5.7 %all-to-all-start.1 = ((bf16[64,16,128]{2,1,0:T(8,128)(2,1)}), bf16[64,16,128]{2,1,0:T(8,128)(2,1)S(1)}, u32[]{:S(2)}, u32[]{:S(2)}) async-start(bf16[64,16,128]{2,1,0:T(8,128)(2,1)} %get-tuple-element.17), calls=%async_computation.1 | async-start | bytes 524288 | tf_op jit(solution)/shard_map/all_to_all | solution.py:293
  44.9 0.0 collective-permute-done.theirs_ref
  44.9 0.7 shard_map.90
  45.6 4.9 %collective-permute-start.1 = (bf16[128,768]{1,0:T(8,128)(2,1)S(1)}, bf16[128,768]{1,0:T(8,128)(2,1)S(1)}, u32[]{:S(2)}, u32[]{:S(2)}) collective-permute-start(bf16[128,768]{1,0:T(8,128)(2,1)S(1)} %get-tuple-element.21), channel_id=1, source_target_pairs={{0,32},{16,48},{32,0},{48,16},{1,33},{17,49},{33,1},{49,17},{2,34}... | collective-permute-start | bytes 589832 | tf_op jit(solution)/shard_map/ppermute | solution.py:304
  50.5 2.3 %collective-permute-start.2 = (bf16[128,768]{1,0:T(8,128)(2,1)S(1)}, bf16[128,768]{1,0:T(8,128)(2,1)S(1)}, u32[]{:S(2)}, u32[]{:S(2)}) collective-permute-start(bf16[128,768]{1,0:T(8,128)(2,1)S(1)} %get-tuple-element.22), channel_id=1, source_target_pairs={{0,16},{16,32},{32,48},{48,0},{1,17},{17,33},{33,49},{49,1},{2,18}... | collective-permute-start | bytes 589832 | tf_op jit(solution)/shard_map/ppermute | solution.py:304
  52.8 4.2 %collective-permute-start.3 = (bf16[128,768]{1,0:T(8,128)(2,1)S(1)}, bf16[128,768]{1,0:T(8,128)(2,1)S(1)}, u32[]{:S(2)}, u32[]{:S(2)}) collective-permute-start(bf16[128,768]{1,0:T(8,128)(2,1)S(1)} %get-tuple-element.23), channel_id=1, source_target_pairs={{0,48},{16,0},{32,16},{48,32},{1,49},{17,1},{33,17},{49,33},{2,50}... | collective-permute-start | bytes 589832 | tf_op jit(solution)/shard_map/ppermute | solution.py:304
  57.0 0.0 all-to-all-done.1.grad_ref
  57.0 0.0 copy-done.1
  57.0 2.4 %shard_map.89 = bf16[4,8,128]{2,1,0:T(8,128)(2,1)S(1)} custom-call(s32[1,1024]{1,0:T(1,128)S(1)} %bitcast.8, s32[1,1024]{1,0:T(1,128)S(1)} %bitcast.11, bf16[1024,512]{1,0:T(8,128)(2,1)} %events_ref.3, bf16[1024,512]{1,0:T(8,128)(2,1)} %get-tuple-element.14.centred_ref, f32[8,1024]{1,0:T(8,128)S(1)} %copy-done.1, ...), custom_call_target="tpu_custom_call" | custom-call | flops 536870912 | bytes 2408448 | tf_op jit(solution)/shard_map/pallas_call | solution.py:224
  59.4 7.6 %all_to_all.25.score_ref = bf16[4,8,128]{2,1,0:T(8,128)(2,1)S(1)} all-to-all(bf16[4,8,128]{2,1,0:T(8,128)(2,1)S(1)} %shard_map.89), channel_id=1, replica_groups=mesh['rep'=8,'x'=4,'z'=8,'core'=2] {'x'}, dimensions={0} | all-to-all | bytes 16384 | tf_op jit(solution)/shard_map/all_to_all | solution.py:312
  67.0 0.0 collective-permute-done.1.a_ref
  67.0 0.0 collective-permute-done.2.b_ref
  67.0 0.0 collective-permute-done.3.c_ref
  67.0 0.2 shard_map.91
  67.2 18.8 %all_to_all.26.x_ref = bf16[16,8,896]{2,1,0:T(8,128)(2,1)S(1)} all-to-all(bf16[16,8,896]{2,1,0:T(8,128)(2,1)S(1)} %shard_map.91), channel_id=1, replica_groups=mesh['rep'=8,'x'=4,'z'=8,'core'=2] {'z','core'}, dimensions={0} | all-to-all | bytes 458752 | tf_op jit(solution)/shard_map/all_to_all | solution.py:316
  86.0 18.0 %all_to_all.27.x_ref = bf16[8,8,1664]{2,1,0:T(8,128)(2,1)S(1)} all-to-all(bf16[8,8,1664]{2,1,0:T(8,128)(2,1)S(1)} %shard_map.92), channel_id=1, replica_groups=mesh['rep'=8,'x'=4,'z'=8,'core'=2] {'rep'}, dimensions={0} | all-to-all | bytes 425984 | tf_op jit(solution)/shard_map/all_to_all | solution.py:320
  104.0 0.7 shard_map.93
  (1 shorter events, 0.0 us)
Async XLA Ops:
  0.6 19.1 %copy-start.2 = (s32[1024]{0:T(1024)S(1)}, s32[1024]{0:T(1024)}, u32[]{:S(2)}) copy-start(s32[1024]{0:T(1024)} %param.8) | copy-start | bytes 12292
  0.6 19.1 %copy-start.3 = (s32[1024]{0:T(1024)S(1)}, s32[1024]{0:T(1024)}, u32[]{:S(2)}) copy-start(s32[1024]{0:T(1024)} %param.9) | copy-start | bytes 12292
  4.9 26.9 %all-to-all-start = ((bf16[64,16,128]{2,1,0:T(8,128)(2,1)}), bf16[64,16,128]{2,1,0:T(8,128)(2,1)S(1)}, u32[]{:S(2)}, u32[]{:S(2)}) async-start(bf16[64,16,128]{2,1,0:T(8,128)(2,1)} %get-tuple-element.13.summary_ref), calls=%async_computation | async-start | bytes 524288 | tf_op jit(solution)/shard_map/all_to_all | solution.py:271
  19.8 1.0 copy-start
  36.8 20.2 %copy-start.1 = (f32[8,1024]{1,0:T(8,128)S(1)}, f32[8,1024]{1,0:T(8,128)}, u32[]{:S(2)}) copy-start(f32[8,1024]{1,0:T(8,128)} %get-tuple-element.15.weight_ref) | copy-start | bytes 98308
  36.8 8.1 %collective-permute-start = (bf16[256,1280]{1,0:T(8,128)(2,1)}, bf16[256,1280]{1,0:T(8,128)(2,1)S(1)}, u32[]{:S(2)}, u32[]{:S(2)}) collective-permute-start(bf16[256,1280]{1,0:T(8,128)(2,1)} %get-tuple-element.19), channel_id=1, source_target_pairs={{0,1},{1,0},{2,3},{3,2},{4,5},{5,4},{6,7},{7,6},{8,9},{9,8},{10,11... | collective-permute-start | bytes 1966088 | tf_op jit(solution)/shard_map/ppermute | solution.py:294
  39.1 17.9 %all-to-all-start.1 = ((bf16[64,16,128]{2,1,0:T(8,128)(2,1)}), bf16[64,16,128]{2,1,0:T(8,128)(2,1)S(1)}, u32[]{:S(2)}, u32[]{:S(2)}) async-start(bf16[64,16,128]{2,1,0:T(8,128)(2,1)} %get-tuple-element.17), calls=%async_computation.1 | async-start | bytes 524288 | tf_op jit(solution)/shard_map/all_to_all | solution.py:293
  45.6 21.4 %collective-permute-start.1 = (bf16[128,768]{1,0:T(8,128)(2,1)S(1)}, bf16[128,768]{1,0:T(8,128)(2,1)S(1)}, u32[]{:S(2)}, u32[]{:S(2)}) collective-permute-start(bf16[128,768]{1,0:T(8,128)(2,1)S(1)} %get-tuple-element.21), channel_id=1, source_target_pairs={{0,32},{16,48},{32,0},{48,16},{1,33},{17,49},{33,1},{49,17},{2,34}... | collective-permute-start | bytes 589832 | tf_op jit(solution)/shard_map/ppermute | solution.py:304
  50.5 16.5 %collective-permute-start.2 = (bf16[128,768]{1,0:T(8,128)(2,1)S(1)}, bf16[128,768]{1,0:T(8,128)(2,1)S(1)}, u32[]{:S(2)}, u32[]{:S(2)}) collective-permute-start(bf16[128,768]{1,0:T(8,128)(2,1)S(1)} %get-tuple-element.22), channel_id=1, source_target_pairs={{0,16},{16,32},{32,48},{48,0},{1,17},{17,33},{33,49},{49,1},{2,18}... | collective-permute-start | bytes 589832 | tf_op jit(solution)/shard_map/ppermute | solution.py:304
  52.8 14.2 %collective-permute-start.3 = (bf16[128,768]{1,0:T(8,128)(2,1)S(1)}, bf16[128,768]{1,0:T(8,128)(2,1)S(1)}, u32[]{:S(2)}, u32[]{:S(2)}) collective-permute-start(bf16[128,768]{1,0:T(8,128)(2,1)S(1)} %get-tuple-element.23), channel_id=1, source_target_pairs={{0,48},{16,0},{32,16},{48,32},{1,49},{17,1},{33,17},{49,33},{2,50}... | collective-permute-start | bytes 589832 | tf_op jit(solution)/shard_map/ppermute | solution.py:304

commit v8 on v6

--- a/solution.py
+++ b/solution.py
@@ -166,16 +166,16 @@
     return jnp.concatenate([total[:, quarter * lane : (quarter + 1) * lane], jnp.concatenate([rest[:size], rest[size:]], axis=1)], axis=0)
 
 
-def outer_kernel(width, x_ref, mine_ref, theirs_ref, *out_refs):
+def outer_kernel(width, place_ref, mine_ref, theirs_ref, *out_refs):
     both = jnp.concatenate([mine_ref[...], theirs_ref[...]], axis=0)
     total = tn(both[:, :width], both[:, width:])
     quarters = [packed(total, i, out_refs[0].shape[1]).astype(BF16) for i in range(4)]
     for here in range(4):
 
-        @pl.when(x_ref[0] == here)
+        @pl.when(place_ref[0] == here)
         def _():
             for step, out_ref in enumerate(out_refs):
-                out_ref[...] = quarters[(here + step) % 4]
+                out_ref[...] = quarters[here ^ step]
 
 
 def score_kernel(users, slots, user_ref, day_ref, events_ref, centred_ref, weight_ref, grad_ref, out_ref):
@@ -206,15 +206,15 @@
     out_ref[:, :, lanes:] = both.reshape(parts, depth, lanes).astype(BF16)
 
 
-def merge_kernel(cores, x_size, x_ref, out_ref):
+def merge_kernel(cores, z_size, x_ref, out_ref):
     parts, depth, columns = x_ref.shape
     lanes = columns // 2
-    x = x_ref[...].astype(F32).reshape(x_size, parts // (x_size * cores), cores, depth, columns)
-    total = jnp.sum(x, axis=1)
+    x = x_ref[...].astype(F32).reshape(parts // (2 * z_size * cores), 2, z_size, cores, depth, columns)
+    total = jnp.sum(jnp.sum(x, axis=0), axis=1)
     pieces = []
     for core in range(cores):
-        pieces += [total[i, core, :, :lanes] for i in range(x_size)]
-        pieces += [total[i, core, :, lanes : lanes + lanes // 2] for i in range(x_size)]
+        pieces += [total[i, core, :, :lanes] for i in range(2)]
+        pieces += [total[i, core, :, lanes : lanes + lanes // 2] for i in range(2)]
     score = jnp.sum(total[:, :, :, lanes + lanes // 2 :], axis=(0, 1))
     pieces += [score, jnp.zeros_like(score)]
     merged = jnp.concatenate(pieces, axis=1).astype(BF16)
@@ -222,11 +222,19 @@
         out_ref[i] = merged
 
 
-def final_kernel(x_ref, weight_ref, score_ref):
-    columns = weight_ref.shape[1]
-    total = jnp.sum(x_ref[...].astype(F32), axis=0)
-    weight_ref[...] = total[:, :columns]
-    score_ref[...] = total[:, columns : columns + score_ref.shape[1]]
+def final_kernel(cores, x_ref, weight_ref, score_ref):
+    groups, depth, columns = x_ref.shape
+    total = jnp.sum(x_ref[...].astype(F32).reshape(groups // 2, 2, depth, columns), axis=0)
+    half = weight_ref.shape[1] // cores
+    held = half // 2
+    near, far = 2 * half // 3, half // 3
+    for core in range(cores):
+        for side in range(2):
+            start = core * half + side * (near // 2)
+            weight_ref[:, start : start + near // 2] = total[side, :, core * held : core * held + near // 2]
+            start = core * half + near + side * (far // 2)
+            weight_ref[:, start : start + far // 2] = total[side, :, core * held + near // 2 : (core + 1) * held]
+    score_ref[...] = jnp.sum(total, axis=0)[:, cores * held : cores * held + score_ref.shape[1]]
 
 
 def call(kernel, outs, args, scalars=0, flops=0, moved=None, whole=(), held=(), out_whole=(), out_far=(), out_near=(), scratch=(), limit=24):
@@ -308,15 +316,20 @@
     )
     grad_days = lax.all_to_all(grad_summary, DAY, split_axis=0, concat_axis=0, tiled=True)
     theirs = lax.ppermute(send, "core", [(i, cores - 1 - i) for i in range(cores)])
-    x_row = lax.axis_index("x").reshape(1)
+    place = ((lax.axis_index("rep") & 1) * 2 + (lax.axis_index("x") & 1)).reshape(1)
     packs = call(
         functools.partial(outer_kernel, width),
-        [((width + width // 2, 128), BF16)] * x_size,
-        (x_row, mine, theirs),
+        [((width + width // 2, 128), BF16)] * 4,
+        (place, mine, theirs),
         scalars=1,
         moved=0,
     )
-    got = [lax.ppermute(packs[k], "x", [(i, (i + k) % x_size) for i in range(x_size)]) for k in (2, 1, 3)]
+    square = [(i, (i // x_size ^ 1) * x_size + (i % x_size ^ 1)) for i in range(groups * x_size)]
+    got = [
+        lax.ppermute(packs[3], ("rep", "x"), square),
+        lax.ppermute(packs[2], "rep", [(i, i ^ 1) for i in range(groups)]),
+        lax.ppermute(packs[1], "x", [(i, i ^ 1) for i in range(x_size)]),
+    ]
     (score,) = call(
         functools.partial(score_kernel, users, slots),
         [((width, 128), F32)],
@@ -326,9 +339,13 @@
     )
     (partial_sums,) = call(join_kernel, [((buckets, rows, 256), BF16)], (score, packs[0], *got))
     gathered = lax.all_to_all(partial_sums, DAY, split_axis=0, concat_axis=0, tiled=True)
-    (merged,) = call(functools.partial(merge_kernel, cores, x_size), [((groups, rows, 3 * width + 128), BF16)], (gathered,))
+    (merged,) = call(
+        functools.partial(merge_kernel, cores, z_size), [((groups, rows, half + 128), BF16)], (gathered,)
+    )
     everyone = lax.all_to_all(merged, "rep", split_axis=0, concat_axis=0, tiled=True)
-    return tuple(call(final_kernel, [((rows, 3 * width), F32), ((rows, heads), F32)], (everyone,)))
+    return tuple(
+        call(functools.partial(final_kernel, cores), [((rows, 3 * width), F32), ((rows, heads), F32)], (everyone,))
+    )
 
 
 def solution(mesh):

time: 103 us -> 99.1 us (0.962)
  starting transfers between devices: 34.3 us -> 31.3 us
  blocking collectives: 38.3 us -> 36.7 us
  waiting for transfers between devices: 9.41 us -> 10.5 us
    ppermute x3, starting transfers between devices: 11.4 us -> 8.42 us  [the longest x1 4.31 us: shards(): lax.ppermute(packs[3], ('rep', 'x'), square)]
    all_to_all x1, waiting for transfers between devices: 0.01 us -> 2.77 us  [shards(): lax.all_to_all(grad_summary, DAY, split_axis=0, concat_axis=0, tiled=True)]
    all_to_all x1, blocking collectives: 16.3 us -> 14.2 us  [shards(): lax.all_to_all(merged, 'rep', split_axis=0, concat_axis=0, tiled=True)]
    ppermute x3, waiting for transfers between devices: 2.63 us -> 0.96 us  [the longest x1 0.73 us: shards(): lax.ppermute(packs[2], 'rep', [(i, i ^ 1) for i in range(groups)])]
  transfers between devices with their start and end apart: 6 -> 6, of which waited for: 2 -> 4; matrix products, arithmetic and copies ran while one was open for 0% -> 0% of each run, Pallas kernels for 7% -> 8%
where the time goes in v8:
time: 99.1 us; the launch traced here: 98 us
  blocking collectives  36.7 us (37%)
  starting transfers between devices  31.3 us (32%)
  Pallas kernels  17.7 us (18%)
  waiting for transfers between devices  10.5 us (11%)
    all_to_all x1, blocking collectives, shards(): lax.all_to_all(partial_sums, DAY, split_axis=0, concat_axis=0, tiled=True)  22.5 us
    pallas_call x8, Pallas kernels, call(): pl.pallas_call(kernel, out_shape=[pltpu.HBM(s, t) if i in out_whole + out...  17.7 us
    all_to_all x1, starting transfers between devices, shards(): lax.all_to_all(summary, DAY, split_axis=0, concat_axis=0, tiled=True)  14.9 us
    all_to_all x1, blocking collectives, shards(): lax.all_to_all(merged, 'rep', split_axis=0, concat_axis=0, tiled=True)  14.2 us
    all_to_all x1, waiting for transfers between devices, shards(): lax.all_to_all(summary, DAY, split_axis=0, concat_axis=0, tiled=True)  6.77 us
    all_to_all x1, starting transfers between devices, shards(): lax.all_to_all(grad_summary, DAY, split_axis=0, concat_axis=0, tiled=True)  5.7 us
    ppermute x1, starting transfers between devices, shards(): lax.ppermute(packs[3], ('rep', 'x'), square)  4.31 us
    all_to_all x1, waiting for transfers between devices, shards(): lax.all_to_all(grad_summary, DAY, split_axis=0, concat_axis=0, tiled=True)  2.77 us
  transfers between devices with their start and end apart: 6, of which 4 were waited for; matrix products, arithmetic and copies ran while one was open for 0% of the time, Pallas kernels for 8%

profile of v8, /device:TPU:1, one launch (start us, length us, event | category | flops | bytes accessed | tf_op | source)
XLA Modules:
  0.0 98.0 jit_solution(6144068219485833763)
XLA Ops:
  0.6 0.0 copy-start.2
  0.6 0.0 copy-start.3
  0.7 4.2 %shard_map.86 = (bf16[64,16,128]{2,1,0:T(8,128)(2,1)}, f32[8,1024]{1,0:T(8,128)}) custom-call(s32[1,1024]{1,0:T(1,128)} %bitcast.6, s32[1,1024]{1,0:T(1,128)} %bitcast.9, bf16[8,512]{1,0:T(8,128)(2,1)} %bitcast.13, bf16[1024,512]{1,0:T(8,128)(2,1)} %events_ref.3, bf16[512,512]{1,0:T(8,128)(2,1)} %value_ref.1), custom_call_target="tpu_custom_call" | custom-call | flops 805306368 | bytes 1884160 | tf_op jit(solution)/shard_map/pallas_call | solution.py:248
  4.9 14.9 %all-to-all-start = ((bf16[64,16,128]{2,1,0:T(8,128)(2,1)}), bf16[64,16,128]{2,1,0:T(8,128)(2,1)S(1)}, u32[]{:S(2)}, u32[]{:S(2)}) async-start(bf16[64,16,128]{2,1,0:T(8,128)(2,1)} %get-tuple-element.13.summary_ref), calls=%async_computation | async-start | bytes 524288 | tf_op jit(solution)/shard_map/all_to_all | solution.py:295
  19.7 0.0 copy-done.2
  19.8 0.0 copy-done.3
  19.8 0.0 copy-start
  19.8 1.0 copy-done
  20.7 4.2 %shard_map.87 = (bf16[1024,512]{1,0:T(8,128)(2,1)}, bf16[512,1536]{1,0:T(8,128)(2,1)S(1)}) custom-call(s32[1,1024]{1,0:T(1,128)S(1)} %bitcast.7, s32[1,1024]{1,0:T(1,128)S(1)} %bitcast.10, bf16[1024,512]{1,0:T(8,128)(2,1)} %events_ref.3, bf16[512,512]{1,0:T(8,128)(2,1)} %value_ref.1, bf16[64,16,128]{2,1,0:T(8,128)(2,1)S(1)} %copy-done, bf16[512,1536]{1,0:T(8,128)(2,1)} %qkv_ref.1), custom_call_target="tpu_custom_call" | custom-call | flops 805306368 | bytes 6037504 | tf_op jit(solution)/shard_map/pallas_call | solution.py:248
  25.0 6.8 %all-to-all-done.x_ref = bf16[64,16,128]{2,1,0:T(8,128)(2,1)S(1)} async-done(((bf16[64,16,128]{2,1,0:T(8,128)(2,1)}), bf16[64,16,128]{2,1,0:T(8,128)(2,1)S(1)}, u32[]{:S(2)}, u32[]{:S(2)}) %all-to-all-start) | async-done | bytes 262176 | tf_op jit(solution)/shard_map/all_to_all | solution.py:295
  31.7 5.0 %shard_map.88 = (bf16[64,16,128]{2,1,0:T(8,128)(2,1)}, bf16[256,1280]{1,0:T(8,128)(2,1)S(1)}, bf16[256,1280]{1,0:T(8,128)(2,1)}) custom-call(s32[1]{0:T(128)} %bitcast.3.core_ref, bf16[64,16,128]{2,1,0:T(8,128)(2,1)S(1)} %all-to-all-done.x_ref, bf16[256,512]{1,0:T(8,128)(2,1)} %bitcast.12, bf16[512,1536]{1,0:T(8,128)(2,1)S(1)} %get-tuple-element.16.qkv_weight_ref), custom_call_target="tpu_custom_call" | custom-call | flops 1744830464 | bytes 3670020 | tf_op jit(solution)/shard_map/pallas_call | solution.py:248
  36.8 0.0 copy-start.1
  36.8 2.4 %collective-permute-start = (bf16[256,1280]{1,0:T(8,128)(2,1)}, bf16[256,1280]{1,0:T(8,128)(2,1)S(1)}, u32[]{:S(2)}, u32[]{:S(2)}) collective-permute-start(bf16[256,1280]{1,0:T(8,128)(2,1)} %get-tuple-element.19), channel_id=1, source_target_pairs={{0,1},{1,0},{2,3},{3,2},{4,5},{5,4},{6,7},{7,6},{8,9},{9,8},{10,11... | collective-permute-start | bytes 1966088 | tf_op jit(solution)/shard_map/ppermute | solution.py:318
  39.1 5.7 %all-to-all-start.1 = ((bf16[64,16,128]{2,1,0:T(8,128)(2,1)}), bf16[64,16,128]{2,1,0:T(8,128)(2,1)S(1)}, u32[]{:S(2)}, u32[]{:S(2)}) async-start(bf16[64,16,128]{2,1,0:T(8,128)(2,1)} %get-tuple-element.17), calls=%async_computation.1 | async-start | bytes 524288 | tf_op jit(solution)/shard_map/all_to_all | solution.py:317
  44.9 0.0 collective-permute-done.theirs_ref
  44.9 0.8 shard_map.90
  45.6 4.3 %collective-permute-start.1 = (bf16[768,128]{1,0:T(8,128)(2,1)S(1)}, bf16[768,128]{1,0:T(8,128)(2,1)S(1)}, u32[]{:S(2)}, u32[]{:S(2)}) collective-permute-start(bf16[768,128]{1,0:T(8,128)(2,1)S(1)} %get-tuple-element.21), channel_id=1, source_target_pairs={{0,80},{16,64},{32,112},{48,96},{64,16},{80,0},{96,48},{112,32},{1... | collective-permute-start | bytes 589832 | tf_op jit(solution)/shard_map/ppermute | solution.py:329
  50.0 2.1 %collective-permute-start.2 = (bf16[768,128]{1,0:T(8,128)(2,1)S(1)}, bf16[768,128]{1,0:T(8,128)(2,1)S(1)}, u32[]{:S(2)}, u32[]{:S(2)}) collective-permute-start(bf16[768,128]{1,0:T(8,128)(2,1)S(1)} %get-tuple-element.22), channel_id=1, source_target_pairs={{0,64},{64,0},{128,192},{192,128},{256,320},{320,256},{384,448},{4... | collective-permute-start | bytes 589832 | tf_op jit(solution)/shard_map/ppermute | solution.py:330
  52.0 2.0 %collective-permute-start.3 = (bf16[768,128]{1,0:T(8,128)(2,1)S(1)}, bf16[768,128]{1,0:T(8,128)(2,1)S(1)}, u32[]{:S(2)}, u32[]{:S(2)}) collective-permute-start(bf16[768,128]{1,0:T(8,128)(2,1)S(1)} %get-tuple-element.23), channel_id=1, source_target_pairs={{0,16},{16,0},{32,48},{48,32},{1,17},{17,1},{33,49},{49,33},{2,18}... | collective-permute-start | bytes 589832 | tf_op jit(solution)/shard_map/ppermute | solution.py:331
  54.1 2.8 %all-to-all-done.1.grad_ref = bf16[64,16,128]{2,1,0:T(8,128)(2,1)S(1)} async-done(((bf16[64,16,128]{2,1,0:T(8,128)(2,1)}), bf16[64,16,128]{2,1,0:T(8,128)(2,1)S(1)}, u32[]{:S(2)}, u32[]{:S(2)}) %all-to-all-start.1) | async-done | bytes 262176 | tf_op jit(solution)/shard_map/all_to_all | solution.py:317
  56.9 0.0 copy-done.1
  56.9 2.6 %shard_map.89.score_ref = f32[512,128]{1,0:T(8,128)S(1)} custom-call(s32[1,1024]{1,0:T(1,128)S(1)} %bitcast.8, s32[1,1024]{1,0:T(1,128)S(1)} %bitcast.11, bf16[1024,512]{1,0:T(8,128)(2,1)} %events_ref.3, bf16[1024,512]{1,0:T(8,128)(2,1)} %get-tuple-element.14.centred_ref, f32[8,1024]{1,0:T(8,128)S(1)} %copy-done.1, ...), custom_call_target="tpu_custom_call" | custom-call | flops 536870912 | bytes 2662400 | tf_op jit(solution)/shard_map/pallas_call | solution.py:248
  59.4 0.0 collective-permute-done.1.a_ref
  59.4 0.7 collective-permute-done.2.b_ref
  60.2 0.2 collective-permute-done.3.c_ref
  60.4 0.2 shard_map.91
  60.6 22.5 %all_to_all.20.x_ref = bf16[64,8,256]{2,1,0:T(8,128)(2,1)S(1)} all-to-all(bf16[64,8,256]{2,1,0:T(8,128)(2,1)S(1)} %shard_map.91), channel_id=1, replica_groups=mesh['rep'=8,'x'=4,'z'=8,'core'=2] {'x','z','core'}, dimensions={0} | all-to-all | bytes 524288 | tf_op jit(solution)/shard_map/all_to_all | solution.py:341
  83.1 0.1 shard_map.92
  83.2 14.2 %all_to_all.21.x_ref = bf16[8,8,896]{2,1,0:T(8,128)(2,1)S(1)} all-to-all(bf16[8,8,896]{2,1,0:T(8,128)(2,1)S(1)} %shard_map.92), channel_id=1, replica_groups=mesh['rep'=8,'x'=4,'z'=8,'core'=2] {'rep'}, dimensions={0} | all-to-all | bytes 229376 | tf_op jit(solution)/shard_map/all_to_all | solution.py:345
  97.4 0.6 shard_map.93
Async XLA Ops:
  0.6 19.1 %copy-start.2 = (s32[1024]{0:T(1024)S(1)}, s32[1024]{0:T(1024)}, u32[]{:S(2)}) copy-start(s32[1024]{0:T(1024)} %param.8) | copy-start | bytes 12292
  0.6 19.1 %copy-start.3 = (s32[1024]{0:T(1024)S(1)}, s32[1024]{0:T(1024)}, u32[]{:S(2)}) copy-start(s32[1024]{0:T(1024)} %param.9) | copy-start | bytes 12292
  4.9 26.9 %all-to-all-start = ((bf16[64,16,128]{2,1,0:T(8,128)(2,1)}), bf16[64,16,128]{2,1,0:T(8,128)(2,1)S(1)}, u32[]{:S(2)}, u32[]{:S(2)}) async-start(bf16[64,16,128]{2,1,0:T(8,128)(2,1)} %get-tuple-element.13.summary_ref), calls=%async_computation | async-start | bytes 524288 | tf_op jit(solution)/shard_map/all_to_all | solution.py:295
  19.8 1.0 %copy-start = (bf16[64,16,128]{2,1,0:T(8,128)(2,1)S(1)}, bf16[64,16,128]{2,1,0:T(8,128)(2,1)}, u32[]{:S(2)}) copy-start(bf16[64,16,128]{2,1,0:T(8,128)(2,1)} %get-tuple-element.13.summary_ref) | copy-start | bytes 786436
  36.8 20.1 %copy-start.1 = (f32[8,1024]{1,0:T(8,128)S(1)}, f32[8,1024]{1,0:T(8,128)}, u32[]{:S(2)}) copy-start(f32[8,1024]{1,0:T(8,128)} %get-tuple-element.15.weight_ref) | copy-start | bytes 98308
  36.8 8.1 %collective-permute-start = (bf16[256,1280]{1,0:T(8,128)(2,1)}, bf16[256,1280]{1,0:T(8,128)(2,1)S(1)}, u32[]{:S(2)}, u32[]{:S(2)}) collective-permute-start(bf16[256,1280]{1,0:T(8,128)(2,1)} %get-tuple-element.19), channel_id=1, source_target_pairs={{0,1},{1,0},{2,3},{3,2},{4,5},{5,4},{6,7},{7,6},{8,9},{9,8},{10,11... | collective-permute-start | bytes 1966088 | tf_op jit(solution)/shard_map/ppermute | solution.py:318
  39.1 17.7 %all-to-all-start.1 = ((bf16[64,16,128]{2,1,0:T(8,128)(2,1)}), bf16[64,16,128]{2,1,0:T(8,128)(2,1)S(1)}, u32[]{:S(2)}, u32[]{:S(2)}) async-start(bf16[64,16,128]{2,1,0:T(8,128)(2,1)} %get-tuple-element.17), calls=%async_computation.1 | async-start | bytes 524288 | tf_op jit(solution)/shard_map/all_to_all | solution.py:317
  45.6 13.8 %collective-permute-start.1 = (bf16[768,128]{1,0:T(8,128)(2,1)S(1)}, bf16[768,128]{1,0:T(8,128)(2,1)S(1)}, u32[]{:S(2)}, u32[]{:S(2)}) collective-permute-start(bf16[768,128]{1,0:T(8,128)(2,1)S(1)} %get-tuple-element.21), channel_id=1, source_target_pairs={{0,80},{16,64},{32,112},{48,96},{64,16},{80,0},{96,48},{112,32},{1... | collective-permute-start | bytes 589832 | tf_op jit(solution)/shard_map/ppermute | solution.py:329
  50.0 10.2 %collective-permute-start.2 = (bf16[768,128]{1,0:T(8,128)(2,1)S(1)}, bf16[768,128]{1,0:T(8,128)(2,1)S(1)}, u32[]{:S(2)}, u32[]{:S(2)}) collective-permute-start(bf16[768,128]{1,0:T(8,128)(2,1)S(1)} %get-tuple-element.22), channel_id=1, source_target_pairs={{0,64},{64,0},{128,192},{192,128},{256,320},{320,256},{384,448},{4... | collective-permute-start | bytes 589832 | tf_op jit(solution)/shard_map/ppermute | solution.py:330
  52.0 8.3 %collective-permute-start.3 = (bf16[768,128]{1,0:T(8,128)(2,1)S(1)}, bf16[768,128]{1,0:T(8,128)(2,1)S(1)}, u32[]{:S(2)}, u32[]{:S(2)}) collective-permute-start(bf16[768,128]{1,0:T(8,128)(2,1)S(1)} %get-tuple-element.23), channel_id=1, source_target_pairs={{0,16},{16,0},{32,48},{48,32},{1,17},{17,1},{33,49},{49,33},{2,18}... | collective-permute-start | bytes 589832 | tf_op jit(solution)/shard_map/ppermute | solution.py:331

commit v9 on v8

--- a/solution.py
+++ b/solution.py
@@ -327,8 +327,8 @@
     square = [(i, (i // x_size ^ 1) * x_size + (i % x_size ^ 1)) for i in range(groups * x_size)]
     got = [
         lax.ppermute(packs[3], ("rep", "x"), square),
-        lax.ppermute(packs[2], "rep", [(i, i ^ 1) for i in range(groups)]),
-        lax.ppermute(packs[1], "x", [(i, i ^ 1) for i in range(x_size)]),
+        lax.ppermute(packs[2], "rep", [(i, (((i + 1) ^ 1) - 1) % groups) for i in range(groups)]),
+        lax.ppermute(packs[1], "x", [(i, (((i + 1) ^ 1) - 1) % x_size) for i in range(x_size)]),
     ]
     (score,) = call(
         functools.partial(score_kernel, users, slots),

time: 99.1 us -> 98.6 us (level)
  starting transfers between devices: 31.3 us -> 35.9 us
  blocking collectives: 36.7 us -> 33.1 us
  waiting for transfers between devices: 10.5 us -> 8.96 us
    ppermute x2, starting transfers between devices: 4.11 us -> 8.67 us  [the longest x1 4.87 us: shards(): lax.ppermute(packs[2], 'rep', [(i, ((i + 1 ^ 1) - 1) % groups) for i in r...]
    all_to_all x1, blocking collectives: 14.2 us -> 10.6 us  [shards(): lax.all_to_all(merged, 'rep', split_axis=0, concat_axis=0, tiled=True)]
    all_to_all x1, waiting for transfers between devices: 2.77 us -> 0.01 us  [shards(): lax.all_to_all(grad_summary, DAY, split_axis=0, concat_axis=0, tiled=True)]
    ppermute x2, waiting for transfers between devices: 0.96 us -> 2.17 us  [the longest x1 2.17 us: shards(): lax.ppermute(packs[1], 'x', [(i, ((i + 1 ^ 1) - 1) % x_size) for i in ran...]
  transfers between devices with their start and end apart: 6 -> 6, of which waited for: 4 -> 2; matrix products, arithmetic and copies ran while one was open for 0% -> 0% of each run, Pallas kernels for 8% -> 8%
where the time goes in v9:
time: 98.6 us; the launch traced here: 97.5 us
  starting transfers between devices  35.9 us (36%)
  blocking collectives  33.1 us (34%)
  Pallas kernels  17.7 us (18%)
  waiting for transfers between devices  8.96 us (9%)
  local copies, waits for them, and re-layouts  0.99 us (1%)
    all_to_all x1, blocking collectives, shards(): lax.all_to_all(partial_sums, DAY, split_axis=0, concat_axis=0, tiled=True)  22.5 us
    pallas_call x8, Pallas kernels, call(): pl.pallas_call(kernel, out_shape=[pltpu.HBM(s, t) if i in out_whole + out...  17.7 us
    all_to_all x1, starting transfers between devices, shards(): lax.all_to_all(summary, DAY, split_axis=0, concat_axis=0, tiled=True)  14.9 us
    all_to_all x1, blocking collectives, shards(): lax.all_to_all(merged, 'rep', split_axis=0, concat_axis=0, tiled=True)  10.6 us
    all_to_all x1, waiting for transfers between devices, shards(): lax.all_to_all(summary, DAY, split_axis=0, concat_axis=0, tiled=True)  6.77 us
    all_to_all x1, starting transfers between devices, shards(): lax.all_to_all(grad_summary, DAY, split_axis=0, concat_axis=0, tiled=True)  5.7 us
    ppermute x1, starting transfers between devices, shards(): lax.ppermute(packs[2], 'rep', [(i, ((i + 1 ^ 1) - 1) % groups) for i in r...  4.87 us
    ppermute x1, starting transfers between devices, shards(): lax.ppermute(packs[3], ('rep', 'x'), square)  4.31 us
  transfers between devices with their start and end apart: 6, of which 2 were waited for; matrix products, arithmetic and copies ran while one was open for 0% of the time, Pallas kernels for 8%

profile of v9, /device:TPU:1, one launch (start us, length us, event | category | flops | bytes accessed | tf_op | source)
XLA Modules:
  0.0 97.5 jit_solution(17833937203396637933)
XLA Ops:
  0.6 0.0 copy-start.2
  0.6 0.0 copy-start.3
  0.7 4.2 %shard_map.86 = (bf16[64,16,128]{2,1,0:T(8,128)(2,1)}, f32[8,1024]{1,0:T(8,128)}) custom-call(s32[1,1024]{1,0:T(1,128)} %bitcast.6, s32[1,1024]{1,0:T(1,128)} %bitcast.9, bf16[8,512]{1,0:T(8,128)(2,1)} %bitcast.13, bf16[1024,512]{1,0:T(8,128)(2,1)} %events_ref.3, bf16[512,512]{1,0:T(8,128)(2,1)} %value_ref.1), custom_call_target="tpu_custom_call" | custom-call | flops 805306368 | bytes 1884160 | tf_op jit(solution)/shard_map/pallas_call | solution.py:248
  4.9 14.9 %all-to-all-start = ((bf16[64,16,128]{2,1,0:T(8,128)(2,1)}), bf16[64,16,128]{2,1,0:T(8,128)(2,1)S(1)}, u32[]{:S(2)}, u32[]{:S(2)}) async-start(bf16[64,16,128]{2,1,0:T(8,128)(2,1)} %get-tuple-element.13.summary_ref), calls=%async_computation | async-start | bytes 524288 | tf_op jit(solution)/shard_map/all_to_all | solution.py:295
  19.7 0.0 copy-done.2
  19.8 0.0 copy-done.3
  19.8 0.0 copy-start
  19.8 1.0 copy-done
  20.7 4.2 %shard_map.87 = (bf16[1024,512]{1,0:T(8,128)(2,1)}, bf16[512,1536]{1,0:T(8,128)(2,1)S(1)}) custom-call(s32[1,1024]{1,0:T(1,128)S(1)} %bitcast.7, s32[1,1024]{1,0:T(1,128)S(1)} %bitcast.10, bf16[1024,512]{1,0:T(8,128)(2,1)} %events_ref.3, bf16[512,512]{1,0:T(8,128)(2,1)} %value_ref.1, bf16[64,16,128]{2,1,0:T(8,128)(2,1)S(1)} %copy-done, bf16[512,1536]{1,0:T(8,128)(2,1)} %qkv_ref.1), custom_call_target="tpu_custom_call" | custom-call | flops 805306368 | bytes 6037504 | tf_op jit(solution)/shard_map/pallas_call | solution.py:248
  25.0 6.8 %all-to-all-done.x_ref = bf16[64,16,128]{2,1,0:T(8,128)(2,1)S(1)} async-done(((bf16[64,16,128]{2,1,0:T(8,128)(2,1)}), bf16[64,16,128]{2,1,0:T(8,128)(2,1)S(1)}, u32[]{:S(2)}, u32[]{:S(2)}) %all-to-all-start) | async-done | bytes 262176 | tf_op jit(solution)/shard_map/all_to_all | solution.py:295
  31.7 5.0 %shard_map.88 = (bf16[64,16,128]{2,1,0:T(8,128)(2,1)}, bf16[256,1280]{1,0:T(8,128)(2,1)S(1)}, bf16[256,1280]{1,0:T(8,128)(2,1)}) custom-call(s32[1]{0:T(128)} %bitcast.3.core_ref, bf16[64,16,128]{2,1,0:T(8,128)(2,1)S(1)} %all-to-all-done.x_ref, bf16[256,512]{1,0:T(8,128)(2,1)} %bitcast.12, bf16[512,1536]{1,0:T(8,128)(2,1)S(1)} %get-tuple-element.16.qkv_weight_ref), custom_call_target="tpu_custom_call" | custom-call | flops 1744830464 | bytes 3670020 | tf_op jit(solution)/shard_map/pallas_call | solution.py:248
  36.8 0.0 copy-start.1
  36.8 2.4 %collective-permute-start = (bf16[256,1280]{1,0:T(8,128)(2,1)}, bf16[256,1280]{1,0:T(8,128)(2,1)S(1)}, u32[]{:S(2)}, u32[]{:S(2)}) collective-permute-start(bf16[256,1280]{1,0:T(8,128)(2,1)} %get-tuple-element.19), channel_id=1, source_target_pairs={{0,1},{1,0},{2,3},{3,2},{4,5},{5,4},{6,7},{7,6},{8,9},{9,8},{10,11... | collective-permute-start | bytes 1966088 | tf_op jit(solution)/shard_map/ppermute | solution.py:318
  39.1 5.7 %all-to-all-start.1 = ((bf16[64,16,128]{2,1,0:T(8,128)(2,1)}), bf16[64,16,128]{2,1,0:T(8,128)(2,1)S(1)}, u32[]{:S(2)}, u32[]{:S(2)}) async-start(bf16[64,16,128]{2,1,0:T(8,128)(2,1)} %get-tuple-element.17), calls=%async_computation.1 | async-start | bytes 524288 | tf_op jit(solution)/shard_map/all_to_all | solution.py:317
  44.9 0.0 collective-permute-done.theirs_ref
  44.9 0.8 shard_map.90
  45.6 4.3 %collective-permute-start.1 = (bf16[768,128]{1,0:T(8,128)(2,1)S(1)}, bf16[768,128]{1,0:T(8,128)(2,1)S(1)}, u32[]{:S(2)}, u32[]{:S(2)}) collective-permute-start(bf16[768,128]{1,0:T(8,128)(2,1)S(1)} %get-tuple-element.21), channel_id=1, source_target_pairs={{0,80},{16,64},{32,112},{48,96},{64,16},{80,0},{96,48},{112,32},{1... | collective-permute-start | bytes 589832 | tf_op jit(solution)/shard_map/ppermute | solution.py:329
  50.0 4.9 %collective-permute-start.2 = (bf16[768,128]{1,0:T(8,128)(2,1)S(1)}, bf16[768,128]{1,0:T(8,128)(2,1)S(1)}, u32[]{:S(2)}, u32[]{:S(2)}) collective-permute-start(bf16[768,128]{1,0:T(8,128)(2,1)S(1)} %get-tuple-element.22), channel_id=1, source_target_pairs={{0,448},{64,128},{128,64},{192,256},{256,192},{320,384},{384,320},... | collective-permute-start | bytes 589832 | tf_op jit(solution)/shard_map/ppermute | solution.py:330
  54.8 3.8 %collective-permute-start.3 = (bf16[768,128]{1,0:T(8,128)(2,1)S(1)}, bf16[768,128]{1,0:T(8,128)(2,1)S(1)}, u32[]{:S(2)}, u32[]{:S(2)}) collective-permute-start(bf16[768,128]{1,0:T(8,128)(2,1)S(1)} %get-tuple-element.23), channel_id=1, source_target_pairs={{0,48},{16,32},{32,16},{48,0},{1,49},{17,33},{33,17},{49,1},{2,50}... | collective-permute-start | bytes 589832 | tf_op jit(solution)/shard_map/ppermute | solution.py:331
  58.6 0.0 all-to-all-done.1.grad_ref
  58.6 0.0 copy-done.1
  58.7 2.6 %shard_map.89.score_ref = f32[512,128]{1,0:T(8,128)S(1)} custom-call(s32[1,1024]{1,0:T(1,128)S(1)} %bitcast.8, s32[1,1024]{1,0:T(1,128)S(1)} %bitcast.11, bf16[1024,512]{1,0:T(8,128)(2,1)} %events_ref.3, bf16[1024,512]{1,0:T(8,128)(2,1)} %get-tuple-element.14.centred_ref, f32[8,1024]{1,0:T(8,128)S(1)} %copy-done.1, ...), custom_call_target="tpu_custom_call" | custom-call | flops 536870912 | bytes 2662400 | tf_op jit(solution)/shard_map/pallas_call | solution.py:248
  61.2 0.0 collective-permute-done.1.a_ref
  61.2 0.0 collective-permute-done.2.b_ref
  61.3 2.2 %collective-permute-done.3.c_ref = bf16[768,128]{1,0:T(8,128)(2,1)S(1)} collective-permute-done((bf16[768,128]{1,0:T(8,128)(2,1)S(1)}, bf16[768,128]{1,0:T(8,128)(2,1)S(1)}, u32[]{:S(2)}, u32[]{:S(2)}) %collective-permute-start.3) | collective-permute-done | bytes 196640 | tf_op jit(solution)/shard_map/ppermute | solution.py:331
  63.4 0.2 shard_map.91
  63.6 22.5 %all_to_all.20.x_ref = bf16[64,8,256]{2,1,0:T(8,128)(2,1)S(1)} all-to-all(bf16[64,8,256]{2,1,0:T(8,128)(2,1)S(1)} %shard_map.91), channel_id=1, replica_groups=mesh['rep'=8,'x'=4,'z'=8,'core'=2] {'x','z','core'}, dimensions={0} | all-to-all | bytes 524288 | tf_op jit(solution)/shard_map/all_to_all | solution.py:341
  86.1 0.1 shard_map.92
  86.2 10.6 %all_to_all.21.x_ref = bf16[8,8,896]{2,1,0:T(8,128)(2,1)S(1)} all-to-all(bf16[8,8,896]{2,1,0:T(8,128)(2,1)S(1)} %shard_map.92), channel_id=1, replica_groups=mesh['rep'=8,'x'=4,'z'=8,'core'=2] {'rep'}, dimensions={0} | all-to-all | bytes 229376 | tf_op jit(solution)/shard_map/all_to_all | solution.py:345
  96.9 0.6 shard_map.93
Async XLA Ops:
  0.6 19.1 %copy-start.2 = (s32[1024]{0:T(1024)S(1)}, s32[1024]{0:T(1024)}, u32[]{:S(2)}) copy-start(s32[1024]{0:T(1024)} %param.8) | copy-start | bytes 12292
  0.6 19.1 %copy-start.3 = (s32[1024]{0:T(1024)S(1)}, s32[1024]{0:T(1024)}, u32[]{:S(2)}) copy-start(s32[1024]{0:T(1024)} %param.9) | copy-start | bytes 12292
  4.9 26.9 %all-to-all-start = ((bf16[64,16,128]{2,1,0:T(8,128)(2,1)}), bf16[64,16,128]{2,1,0:T(8,128)(2,1)S(1)}, u32[]{:S(2)}, u32[]{:S(2)}) async-start(bf16[64,16,128]{2,1,0:T(8,128)(2,1)} %get-tuple-element.13.summary_ref), calls=%async_computation | async-start | bytes 524288 | tf_op jit(solution)/shard_map/all_to_all | solution.py:295
  19.8 1.0 %copy-start = (bf16[64,16,128]{2,1,0:T(8,128)(2,1)S(1)}, bf16[64,16,128]{2,1,0:T(8,128)(2,1)}, u32[]{:S(2)}) copy-start(bf16[64,16,128]{2,1,0:T(8,128)(2,1)} %get-tuple-element.13.summary_ref) | copy-start | bytes 786436
  36.8 21.9 %copy-start.1 = (f32[8,1024]{1,0:T(8,128)S(1)}, f32[8,1024]{1,0:T(8,128)}, u32[]{:S(2)}) copy-start(f32[8,1024]{1,0:T(8,128)} %get-tuple-element.15.weight_ref) | copy-start | bytes 98308
  36.8 8.1 %collective-permute-start = (bf16[256,1280]{1,0:T(8,128)(2,1)}, bf16[256,1280]{1,0:T(8,128)(2,1)S(1)}, u32[]{:S(2)}, u32[]{:S(2)}) collective-permute-start(bf16[256,1280]{1,0:T(8,128)(2,1)} %get-tuple-element.19), channel_id=1, source_target_pairs={{0,1},{1,0},{2,3},{3,2},{4,5},{5,4},{6,7},{7,6},{8,9},{9,8},{10,11... | collective-permute-start | bytes 1966088 | tf_op jit(solution)/shard_map/ppermute | solution.py:318
  39.1 19.5 %all-to-all-start.1 = ((bf16[64,16,128]{2,1,0:T(8,128)(2,1)}), bf16[64,16,128]{2,1,0:T(8,128)(2,1)S(1)}, u32[]{:S(2)}, u32[]{:S(2)}) async-start(bf16[64,16,128]{2,1,0:T(8,128)(2,1)} %get-tuple-element.17), calls=%async_computation.1 | async-start | bytes 524288 | tf_op jit(solution)/shard_map/all_to_all | solution.py:317
  45.6 15.6 %collective-permute-start.1 = (bf16[768,128]{1,0:T(8,128)(2,1)S(1)}, bf16[768,128]{1,0:T(8,128)(2,1)S(1)}, u32[]{:S(2)}, u32[]{:S(2)}) collective-permute-start(bf16[768,128]{1,0:T(8,128)(2,1)S(1)} %get-tuple-element.21), channel_id=1, source_target_pairs={{0,80},{16,64},{32,112},{48,96},{64,16},{80,0},{96,48},{112,32},{1... | collective-permute-start | bytes 589832 | tf_op jit(solution)/shard_map/ppermute | solution.py:329
  50.0 11.3 %collective-permute-start.2 = (bf16[768,128]{1,0:T(8,128)(2,1)S(1)}, bf16[768,128]{1,0:T(8,128)(2,1)S(1)}, u32[]{:S(2)}, u32[]{:S(2)}) collective-permute-start(bf16[768,128]{1,0:T(8,128)(2,1)S(1)} %get-tuple-element.22), channel_id=1, source_target_pairs={{0,448},{64,128},{128,64},{192,256},{256,192},{320,384},{384,320},... | collective-permute-start | bytes 589832 | tf_op jit(solution)/shard_map/ppermute | solution.py:330
  54.8 8.6 %collective-permute-start.3 = (bf16[768,128]{1,0:T(8,128)(2,1)S(1)}, bf16[768,128]{1,0:T(8,128)(2,1)S(1)}, u32[]{:S(2)}, u32[]{:S(2)}) collective-permute-start(bf16[768,128]{1,0:T(8,128)(2,1)S(1)} %get-tuple-element.23), channel_id=1, source_target_pairs={{0,48},{16,32},{32,16},{48,0},{1,49},{17,33},{33,17},{49,1},{2,50}... | collective-permute-start | bytes 589832 | tf_op jit(solution)/shard_map/ppermute | solution.py:331

commit v10 on v9

--- a/solution.py
+++ b/solution.py
@@ -110,40 +110,43 @@
     cot_copy.start()
     buckets = x_ref.shape[0]
     size = width // heads
-    causal = iota((days, days), 1) <= iota((days, days), 0)
+    causal = iota((days, days), 0) <= iota((days, days), 1)
     wide = to_rows(x_ref[...], width)
     inverse = lax.rsqrt(jnp.mean(wide * wide, axis=-1, keepdims=True) + 1e-06)
     normed = (wide * inverse).astype(BF16)
     mine_ref[:, :width] = normed
     send_ref[:, :width] = normed
     qkv = nn(normed, qkv_weight_ref[...]).astype(BF16)
-    cot_copy.wait()
-    cot = cot_buf[...]
     pair = 2 * size
     left = iota((days, pair), 1) < size
     zero = jnp.zeros((days, pair), BF16)
     root = 1.0 / math.sqrt(size)
     parts = ([], [], [])
-    for start in range(0, width, pair):
-        q, k, v = (qkv[:, i * width + start : i * width + start + pair] for i in range(3))
-        c = cot[:, start : start + pair]
-        held = ([], [], [], [], [])
-        for half in range(2):
-            mine = left if half == 0 else ~left
-            q1, k1, v1, c1 = (jnp.where(mine, a, zero) for a in (q, k, v, c))
-            exponent = jnp.where(causal, jnp.exp(nt(q, k1) * root), 0.0)
-            total = jnp.sum(exponent, axis=-1, keepdims=True)
-            guard = jnp.where(total > 1.0, 2.0**-64, 1.0)
-            attention = (exponent * guard) * (1.0 / (total * guard))
-            grad_probs = nt(c, v1) * loss_scale
-            inner = jnp.sum(grad_probs * attention, axis=-1, keepdims=True)
-            grad_logits = (attention * (grad_probs - inner) * root).astype(BF16)
-            for group, item in zip(held, (grad_logits, attention.astype(BF16), q1, k1, c1)):
-                group.append(item)
-        logits_grad, probs, q2, k2, c2 = held
-        parts[0].append(nn(jnp.concatenate(logits_grad, 1), jnp.concatenate(k2, 0)))
-        parts[1].append(tn(jnp.concatenate(logits_grad, 0), jnp.concatenate(q2, 0)))
-        parts[2].append(tn(jnp.concatenate(probs, 0), jnp.concatenate(c2, 0)) * loss_scale)
+    starts = range(0, width, pair)
+    rows = [[qkv[:, i * width + start : i * width + start + pair] for start in starts] for i in range(3)]
+    halves = [(i, mine) for i in range(len(starts)) for mine in (left, ~left)]
+    queries, keys, values = ([jnp.where(mine, a[i], zero) for i, mine in halves] for a in rows)
+    logits = [nt(keys[n] * root, rows[0][i]) for n, (i, _) in enumerate(halves)]
+    cot_copy.wait()
+    cot = cot_buf[...]
+    cots = [cot[:, start : start + pair] for start in starts]
+    grad_probs = [nt(values[n], cots[i]) for n, (i, _) in enumerate(halves)]
+    probs, logits_grad = [], []
+    for n in range(len(halves)):
+        exponent = jnp.where(causal, jnp.exp(logits[n]), 0.0)
+        total = jnp.sum(exponent, axis=0, keepdims=True)
+        guard = jnp.where(total > 1.0, 2.0**-64, 1.0)
+        attention = (exponent * guard) * (1.0 / (total * guard))
+        inner = jnp.sum(grad_probs[n] * attention, axis=0, keepdims=True)
+        probs.append(attention.astype(BF16))
+        logits_grad.append((attention * (grad_probs[n] - inner) * (loss_scale * root)).astype(BF16))
+    for i, c in enumerate(cots):
+        pick = slice(2 * i, 2 * i + 2)
+        masked = [jnp.where(mine, c, zero) for mine in (left, ~left)]
+        wide_grad = jnp.concatenate(logits_grad[pick], 1)
+        parts[0].append(tn(jnp.concatenate(logits_grad[pick], 0), jnp.concatenate(keys[pick], 0)))
+        parts[1].append(nn(wide_grad, jnp.concatenate(queries[pick], 0)))
+        parts[2].append(nn(jnp.concatenate(probs[pick], 1), jnp.concatenate(masked, 0)) * loss_scale)
     grad_qkv = jnp.concatenate([a.astype(BF16) for part in parts for a in part], axis=1)
     half = 3 * width // 2
     first = core_ref[0] == 0

time: 98.6 us -> 97.7 us (level)
  no operation moved by 1% of the time
where the time goes in v10:
time: 97.7 us; the launch traced here: 96.6 us
  starting transfers between devices  35.9 us (37%)
  blocking collectives  33.1 us (34%)
  Pallas kernels  16.8 us (17%)
  waiting for transfers between devices  8.96 us (9%)
  local copies, waits for them, and re-layouts  0.99 us (1%)
    all_to_all x1, blocking collectives, shards(): lax.all_to_all(partial_sums, DAY, split_axis=0, concat_axis=0, tiled=True)  22.5 us
    pallas_call x8, Pallas kernels, call(): pl.pallas_call(kernel, out_shape=[pltpu.HBM(s, t) if i in out_whole + out...  16.8 us
    all_to_all x1, starting transfers between devices, shards(): lax.all_to_all(summary, DAY, split_axis=0, concat_axis=0, tiled=True)  14.9 us
    all_to_all x1, blocking collectives, shards(): lax.all_to_all(merged, 'rep', split_axis=0, concat_axis=0, tiled=True)  10.7 us
    all_to_all x1, waiting for transfers between devices, shards(): lax.all_to_all(summary, DAY, split_axis=0, concat_axis=0, tiled=True)  6.77 us
    all_to_all x1, starting transfers between devices, shards(): lax.all_to_all(grad_summary, DAY, split_axis=0, concat_axis=0, tiled=True)  5.7 us
    ppermute x1, starting transfers between devices, shards(): lax.ppermute(packs[2], 'rep', [(i, ((i + 1 ^ 1) - 1) % groups) for i in r...  4.87 us
    ppermute x1, starting transfers between devices, shards(): lax.ppermute(packs[3], ('rep', 'x'), square)  4.31 us
  transfers between devices with their start and end apart: 6, of which 2 were waited for; matrix products, arithmetic and copies ran while one was open for 0% of the time, Pallas kernels for 8%

profile of v10, /device:TPU:1, one launch (start us, length us, event | category | flops | bytes accessed | tf_op | source)
XLA Modules:
  0.0 96.6 jit_solution(8726055548223196966)
XLA Ops:
  0.6 0.0 copy-start.2
  0.6 0.0 copy-start.3
  0.7 4.2 %shard_map.86 = (bf16[64,16,128]{2,1,0:T(8,128)(2,1)}, f32[8,1024]{1,0:T(8,128)}) custom-call(s32[1,1024]{1,0:T(1,128)} %bitcast.6, s32[1,1024]{1,0:T(1,128)} %bitcast.9, bf16[8,512]{1,0:T(8,128)(2,1)} %bitcast.13, bf16[1024,512]{1,0:T(8,128)(2,1)} %events_ref.3, bf16[512,512]{1,0:T(8,128)(2,1)} %value_ref.1), custom_call_target="tpu_custom_call" | custom-call | flops 805306368 | bytes 1884160 | tf_op jit(solution)/shard_map/pallas_call | solution.py:251
  4.9 14.9 %all-to-all-start = ((bf16[64,16,128]{2,1,0:T(8,128)(2,1)}), bf16[64,16,128]{2,1,0:T(8,128)(2,1)S(1)}, u32[]{:S(2)}, u32[]{:S(2)}) async-start(bf16[64,16,128]{2,1,0:T(8,128)(2,1)} %get-tuple-element.13.summary_ref), calls=%async_computation | async-start | bytes 524288 | tf_op jit(solution)/shard_map/all_to_all | solution.py:298
  19.7 0.0 copy-done.2
  19.8 0.0 copy-done.3
  19.8 0.0 copy-start
  19.8 1.0 %copy-done = bf16[64,16,128]{2,1,0:T(8,128)(2,1)S(1)} copy-done((bf16[64,16,128]{2,1,0:T(8,128)(2,1)S(1)}, bf16[64,16,128]{2,1,0:T(8,128)(2,1)}, u32[]{:S(2)}) %copy-start) | copy-done | bytes 262168
  20.7 4.2 %shard_map.87 = (bf16[1024,512]{1,0:T(8,128)(2,1)}, bf16[512,1536]{1,0:T(8,128)(2,1)S(1)}) custom-call(s32[1,1024]{1,0:T(1,128)S(1)} %bitcast.7, s32[1,1024]{1,0:T(1,128)S(1)} %bitcast.10, bf16[1024,512]{1,0:T(8,128)(2,1)} %events_ref.3, bf16[512,512]{1,0:T(8,128)(2,1)} %value_ref.1, bf16[64,16,128]{2,1,0:T(8,128)(2,1)S(1)} %copy-done, bf16[512,1536]{1,0:T(8,128)(2,1)} %qkv_ref.1), custom_call_target="tpu_custom_call" | custom-call | flops 805306368 | bytes 6037504 | tf_op jit(solution)/shard_map/pallas_call | solution.py:251
  25.0 6.8 %all-to-all-done.x_ref = bf16[64,16,128]{2,1,0:T(8,128)(2,1)S(1)} async-done(((bf16[64,16,128]{2,1,0:T(8,128)(2,1)}), bf16[64,16,128]{2,1,0:T(8,128)(2,1)S(1)}, u32[]{:S(2)}, u32[]{:S(2)}) %all-to-all-start) | async-done | bytes 262176 | tf_op jit(solution)/shard_map/all_to_all | solution.py:298
  31.7 4.1 %shard_map.88 = (bf16[64,16,128]{2,1,0:T(8,128)(2,1)}, bf16[256,1280]{1,0:T(8,128)(2,1)S(1)}, bf16[256,1280]{1,0:T(8,128)(2,1)}) custom-call(s32[1]{0:T(128)} %bitcast.3.core_ref, bf16[64,16,128]{2,1,0:T(8,128)(2,1)S(1)} %all-to-all-done.x_ref, bf16[256,512]{1,0:T(8,128)(2,1)} %bitcast.12, bf16[512,1536]{1,0:T(8,128)(2,1)S(1)} %get-tuple-element.16.qkv_weight_ref), custom_call_target="tpu_custom_call" | custom-call | flops 1744830464 | bytes 3670020 | tf_op jit(solution)/shard_map/pallas_call | solution.py:251
  35.8 0.0 copy-start.1
  35.8 2.4 %collective-permute-start = (bf16[256,1280]{1,0:T(8,128)(2,1)}, bf16[256,1280]{1,0:T(8,128)(2,1)S(1)}, u32[]{:S(2)}, u32[]{:S(2)}) collective-permute-start(bf16[256,1280]{1,0:T(8,128)(2,1)} %get-tuple-element.19), channel_id=1, source_target_pairs={{0,1},{1,0},{2,3},{3,2},{4,5},{5,4},{6,7},{7,6},{8,9},{9,8},{10,11... | collective-permute-start | bytes 1966088 | tf_op jit(solution)/shard_map/ppermute | solution.py:321
  38.2 5.7 %all-to-all-start.1 = ((bf16[64,16,128]{2,1,0:T(8,128)(2,1)}), bf16[64,16,128]{2,1,0:T(8,128)(2,1)S(1)}, u32[]{:S(2)}, u32[]{:S(2)}) async-start(bf16[64,16,128]{2,1,0:T(8,128)(2,1)} %get-tuple-element.17), calls=%async_computation.1 | async-start | bytes 524288 | tf_op jit(solution)/shard_map/all_to_all | solution.py:320
  43.9 0.0 collective-permute-done.theirs_ref
  43.9 0.8 shard_map.90
  44.7 4.3 %collective-permute-start.1 = (bf16[768,128]{1,0:T(8,128)(2,1)S(1)}, bf16[768,128]{1,0:T(8,128)(2,1)S(1)}, u32[]{:S(2)}, u32[]{:S(2)}) collective-permute-start(bf16[768,128]{1,0:T(8,128)(2,1)S(1)} %get-tuple-element.21), channel_id=1, source_target_pairs={{0,80},{16,64},{32,112},{48,96},{64,16},{80,0},{96,48},{112,32},{1... | collective-permute-start | bytes 589832 | tf_op jit(solution)/shard_map/ppermute | solution.py:332
  49.0 4.9 %collective-permute-start.2 = (bf16[768,128]{1,0:T(8,128)(2,1)S(1)}, bf16[768,128]{1,0:T(8,128)(2,1)S(1)}, u32[]{:S(2)}, u32[]{:S(2)}) collective-permute-start(bf16[768,128]{1,0:T(8,128)(2,1)S(1)} %get-tuple-element.22), channel_id=1, source_target_pairs={{0,448},{64,128},{128,64},{192,256},{256,192},{320,384},{384,320},... | collective-permute-start | bytes 589832 | tf_op jit(solution)/shard_map/ppermute | solution.py:333
  53.9 3.8 %collective-permute-start.3 = (bf16[768,128]{1,0:T(8,128)(2,1)S(1)}, bf16[768,128]{1,0:T(8,128)(2,1)S(1)}, u32[]{:S(2)}, u32[]{:S(2)}) collective-permute-start(bf16[768,128]{1,0:T(8,128)(2,1)S(1)} %get-tuple-element.23), channel_id=1, source_target_pairs={{0,48},{16,32},{32,16},{48,0},{1,49},{17,33},{33,17},{49,1},{2,50}... | collective-permute-start | bytes 589832 | tf_op jit(solution)/shard_map/ppermute | solution.py:334
  57.7 0.0 all-to-all-done.1.grad_ref
  57.7 0.0 copy-done.1
  57.7 2.6 %shard_map.89.score_ref = f32[512,128]{1,0:T(8,128)S(1)} custom-call(s32[1,1024]{1,0:T(1,128)S(1)} %bitcast.8, s32[1,1024]{1,0:T(1,128)S(1)} %bitcast.11, bf16[1024,512]{1,0:T(8,128)(2,1)} %events_ref.3, bf16[1024,512]{1,0:T(8,128)(2,1)} %get-tuple-element.14.centred_ref, f32[8,1024]{1,0:T(8,128)S(1)} %copy-done.1, ...), custom_call_target="tpu_custom_call" | custom-call | flops 536870912 | bytes 2662400 | tf_op jit(solution)/shard_map/pallas_call | solution.py:251
  60.3 0.0 collective-permute-done.1.a_ref
  60.3 0.0 collective-permute-done.2.b_ref
  60.3 2.2 %collective-permute-done.3.c_ref = bf16[768,128]{1,0:T(8,128)(2,1)S(1)} collective-permute-done((bf16[768,128]{1,0:T(8,128)(2,1)S(1)}, bf16[768,128]{1,0:T(8,128)(2,1)S(1)}, u32[]{:S(2)}, u32[]{:S(2)}) %collective-permute-start.3) | collective-permute-done | bytes 196640 | tf_op jit(solution)/shard_map/ppermute | solution.py:334
  62.5 0.2 shard_map.91
  62.7 22.5 %all_to_all.20.x_ref = bf16[64,8,256]{2,1,0:T(8,128)(2,1)S(1)} all-to-all(bf16[64,8,256]{2,1,0:T(8,128)(2,1)S(1)} %shard_map.91), channel_id=1, replica_groups=mesh['rep'=8,'x'=4,'z'=8,'core'=2] {'x','z','core'}, dimensions={0} | all-to-all | bytes 524288 | tf_op jit(solution)/shard_map/all_to_all | solution.py:344
  85.2 0.1 shard_map.92
  85.3 10.7 %all_to_all.21.x_ref = bf16[8,8,896]{2,1,0:T(8,128)(2,1)S(1)} all-to-all(bf16[8,8,896]{2,1,0:T(8,128)(2,1)S(1)} %shard_map.92), channel_id=1, replica_groups=mesh['rep'=8,'x'=4,'z'=8,'core'=2] {'rep'}, dimensions={0} | all-to-all | bytes 229376 | tf_op jit(solution)/shard_map/all_to_all | solution.py:348
  95.9 0.6 shard_map.93
Async XLA Ops:
  0.6 19.1 %copy-start.2 = (s32[1024]{0:T(1024)S(1)}, s32[1024]{0:T(1024)}, u32[]{:S(2)}) copy-start(s32[1024]{0:T(1024)} %param.8) | copy-start | bytes 12292
  0.6 19.1 %copy-start.3 = (s32[1024]{0:T(1024)S(1)}, s32[1024]{0:T(1024)}, u32[]{:S(2)}) copy-start(s32[1024]{0:T(1024)} %param.9) | copy-start | bytes 12292
  4.9 26.9 %all-to-all-start = ((bf16[64,16,128]{2,1,0:T(8,128)(2,1)}), bf16[64,16,128]{2,1,0:T(8,128)(2,1)S(1)}, u32[]{:S(2)}, u32[]{:S(2)}) async-start(bf16[64,16,128]{2,1,0:T(8,128)(2,1)} %get-tuple-element.13.summary_ref), calls=%async_computation | async-start | bytes 524288 | tf_op jit(solution)/shard_map/all_to_all | solution.py:298
  19.8 1.0 %copy-start = (bf16[64,16,128]{2,1,0:T(8,128)(2,1)S(1)}, bf16[64,16,128]{2,1,0:T(8,128)(2,1)}, u32[]{:S(2)}) copy-start(bf16[64,16,128]{2,1,0:T(8,128)(2,1)} %get-tuple-element.13.summary_ref) | copy-start | bytes 786436
  35.8 21.9 %copy-start.1 = (f32[8,1024]{1,0:T(8,128)S(1)}, f32[8,1024]{1,0:T(8,128)}, u32[]{:S(2)}) copy-start(f32[8,1024]{1,0:T(8,128)} %get-tuple-element.15.weight_ref) | copy-start | bytes 98308
  35.8 8.1 %collective-permute-start = (bf16[256,1280]{1,0:T(8,128)(2,1)}, bf16[256,1280]{1,0:T(8,128)(2,1)S(1)}, u32[]{:S(2)}, u32[]{:S(2)}) collective-permute-start(bf16[256,1280]{1,0:T(8,128)(2,1)} %get-tuple-element.19), channel_id=1, source_target_pairs={{0,1},{1,0},{2,3},{3,2},{4,5},{5,4},{6,7},{7,6},{8,9},{9,8},{10,11... | collective-permute-start | bytes 1966088 | tf_op jit(solution)/shard_map/ppermute | solution.py:321
  38.2 19.5 %all-to-all-start.1 = ((bf16[64,16,128]{2,1,0:T(8,128)(2,1)}), bf16[64,16,128]{2,1,0:T(8,128)(2,1)S(1)}, u32[]{:S(2)}, u32[]{:S(2)}) async-start(bf16[64,16,128]{2,1,0:T(8,128)(2,1)} %get-tuple-element.17), calls=%async_computation.1 | async-start | bytes 524288 | tf_op jit(solution)/shard_map/all_to_all | solution.py:320
  44.7 15.6 %collective-permute-start.1 = (bf16[768,128]{1,0:T(8,128)(2,1)S(1)}, bf16[768,128]{1,0:T(8,128)(2,1)S(1)}, u32[]{:S(2)}, u32[]{:S(2)}) collective-permute-start(bf16[768,128]{1,0:T(8,128)(2,1)S(1)} %get-tuple-element.21), channel_id=1, source_target_pairs={{0,80},{16,64},{32,112},{48,96},{64,16},{80,0},{96,48},{112,32},{1... | collective-permute-start | bytes 589832 | tf_op jit(solution)/shard_map/ppermute | solution.py:332
  49.0 11.3 %collective-permute-start.2 = (bf16[768,128]{1,0:T(8,128)(2,1)S(1)}, bf16[768,128]{1,0:T(8,128)(2,1)S(1)}, u32[]{:S(2)}, u32[]{:S(2)}) collective-permute-start(bf16[768,128]{1,0:T(8,128)(2,1)S(1)} %get-tuple-element.22), channel_id=1, source_target_pairs={{0,448},{64,128},{128,64},{192,256},{256,192},{320,384},{384,320},... | collective-permute-start | bytes 589832 | tf_op jit(solution)/shard_map/ppermute | solution.py:333
  53.9 8.6 %collective-permute-start.3 = (bf16[768,128]{1,0:T(8,128)(2,1)S(1)}, bf16[768,128]{1,0:T(8,128)(2,1)S(1)}, u32[]{:S(2)}, u32[]{:S(2)}) collective-permute-start(bf16[768,128]{1,0:T(8,128)(2,1)S(1)} %get-tuple-element.23), channel_id=1, source_target_pairs={{0,48},{16,32},{32,16},{48,0},{1,49},{17,33},{33,17},{49,1},{2,50}... | collective-permute-start | bytes 589832 | tf_op jit(solution)/shard_map/ppermute | solution.py:334

commit v11 on v10

--- a/solution.py
+++ b/solution.py
@@ -1,4 +1,5 @@
 import functools
+import itertools
 import math
 
 import jax
@@ -262,6 +263,18 @@
     )(*args)
 
 
+def neighbours(sizes, far):
+    pairs = []
+    for place in itertools.product(*map(range, sizes)):
+        skip = int(place[-1] == far)
+        there = [((i + skip ^ 1) - skip) % n for i, n in zip(place[:-1], sizes)] + [place[-1]]
+        flat = [0, 0]
+        for i, j, n in zip(place, there, sizes):
+            flat = [flat[0] * n + i, flat[1] * n + j]
+        pairs.append(tuple(flat))
+    return pairs
+
+
 def shards(sizes, events, event_user, event_day, score_weight, value_weight, qkv_weight, cotangent):
     groups, x_size, z_size, cores = sizes
     buckets = x_size * z_size * cores
@@ -327,11 +340,13 @@
         scalars=1,
         moved=0,
     )
-    square = [(i, (i // x_size ^ 1) * x_size + (i % x_size ^ 1)) for i in range(groups * x_size)]
     got = [
-        lax.ppermute(packs[3], ("rep", "x"), square),
-        lax.ppermute(packs[2], "rep", [(i, (((i + 1) ^ 1) - 1) % groups) for i in range(groups)]),
-        lax.ppermute(packs[1], "x", [(i, (((i + 1) ^ 1) - 1) % x_size) for i in range(x_size)]),
+        lax.ppermute(packs[step], axes, neighbours(sizes_of, far))
+        for step, axes, sizes_of, far in (
+            (3, ("rep", "x", "core"), (groups, x_size, cores), 0),
+            (1, ("x", "core"), (x_size, cores), 1),
+            (2, ("rep", "core"), (groups, cores), 1),
+        )
     ]
     (score,) = call(
         functools.partial(score_kernel, users, slots),

time: 97.7 us -> 96.3 us (0.986)
  waiting for transfers between devices: 8.96 us -> 7.21 us
    ppermute x3, waiting for transfers between devices: 2.18 us -> 0.43 us  [shards(): lax.ppermute(packs[step], axes, neighbours(sizes_of, far))]
where the time goes in v11:
time: 96.3 us; the launch traced here: 95.2 us
  starting transfers between devices  35.9 us (37%)
  blocking collectives  33.5 us (35%)
  Pallas kernels  16.8 us (17%)
  waiting for transfers between devices  7.21 us (7%)
  local copies, waits for them, and re-layouts  0.99 us (1%)
    all_to_all x1, blocking collectives, shards(): lax.all_to_all(partial_sums, DAY, split_axis=0, concat_axis=0, tiled=True)  22.2 us
    pallas_call x8, Pallas kernels, call(): pl.pallas_call(kernel, out_shape=[pltpu.HBM(s, t) if i in out_whole + out...  16.8 us
    all_to_all x1, starting transfers between devices, shards(): lax.all_to_all(summary, DAY, split_axis=0, concat_axis=0, tiled=True)  14.9 us
    ppermute x3, starting transfers between devices, shards(): lax.ppermute(packs[step], axes, neighbours(sizes_of, far))  13 us
    all_to_all x1, blocking collectives, shards(): lax.all_to_all(merged, 'rep', split_axis=0, concat_axis=0, tiled=True)  11.3 us
    all_to_all x1, waiting for transfers between devices, shards(): lax.all_to_all(summary, DAY, split_axis=0, concat_axis=0, tiled=True)  6.77 us
    all_to_all x1, starting transfers between devices, shards(): lax.all_to_all(grad_summary, DAY, split_axis=0, concat_axis=0, tiled=True)  5.7 us
    ppermute x1, starting transfers between devices, shards(): lax.ppermute(send, 'core', [(i, cores - 1 - i) for i in range(cores)])  2.36 us
  transfers between devices with their start and end apart: 6, of which 2 were waited for; matrix products, arithmetic and copies ran while one was open for 0% of the time, Pallas kernels for 8%

profile of v11, /device:TPU:1, one launch (start us, length us, event | category | flops | bytes accessed | tf_op | source)
XLA Modules:
  0.0 95.2 jit_solution(17461188520822656542)
XLA Ops:
  0.6 0.0 copy-start.2
  0.6 0.0 copy-start.3
  0.7 4.2 %shard_map.86 = (bf16[64,16,128]{2,1,0:T(8,128)(2,1)}, f32[8,1024]{1,0:T(8,128)}) custom-call(s32[1,1024]{1,0:T(1,128)} %bitcast.6, s32[1,1024]{1,0:T(1,128)} %bitcast.9, bf16[8,512]{1,0:T(8,128)(2,1)} %bitcast.13, bf16[1024,512]{1,0:T(8,128)(2,1)} %events_ref.3, bf16[512,512]{1,0:T(8,128)(2,1)} %value_ref.1), custom_call_target="tpu_custom_call" | custom-call | flops 805306368 | bytes 1884160 | tf_op jit(solution)/shard_map/pallas_call | solution.py:252
  4.9 14.9 %all-to-all-start = ((bf16[64,16,128]{2,1,0:T(8,128)(2,1)}), bf16[64,16,128]{2,1,0:T(8,128)(2,1)S(1)}, u32[]{:S(2)}, u32[]{:S(2)}) async-start(bf16[64,16,128]{2,1,0:T(8,128)(2,1)} %get-tuple-element.13.summary_ref), calls=%async_computation | async-start | bytes 524288 | tf_op jit(solution)/shard_map/all_to_all | solution.py:311
  19.7 0.0 copy-done.2
  19.8 0.0 copy-done.3
  19.8 0.0 copy-start
  19.8 1.0 %copy-done = bf16[64,16,128]{2,1,0:T(8,128)(2,1)S(1)} copy-done((bf16[64,16,128]{2,1,0:T(8,128)(2,1)S(1)}, bf16[64,16,128]{2,1,0:T(8,128)(2,1)}, u32[]{:S(2)}) %copy-start) | copy-done | bytes 262168
  20.7 4.2 %shard_map.87 = (bf16[1024,512]{1,0:T(8,128)(2,1)}, bf16[512,1536]{1,0:T(8,128)(2,1)S(1)}) custom-call(s32[1,1024]{1,0:T(1,128)S(1)} %bitcast.7, s32[1,1024]{1,0:T(1,128)S(1)} %bitcast.10, bf16[1024,512]{1,0:T(8,128)(2,1)} %events_ref.3, bf16[512,512]{1,0:T(8,128)(2,1)} %value_ref.1, bf16[64,16,128]{2,1,0:T(8,128)(2,1)S(1)} %copy-done, bf16[512,1536]{1,0:T(8,128)(2,1)} %qkv_ref.1), custom_call_target="tpu_custom_call" | custom-call | flops 805306368 | bytes 6037504 | tf_op jit(solution)/shard_map/pallas_call | solution.py:252
  25.0 6.8 %all-to-all-done.x_ref = bf16[64,16,128]{2,1,0:T(8,128)(2,1)S(1)} async-done(((bf16[64,16,128]{2,1,0:T(8,128)(2,1)}), bf16[64,16,128]{2,1,0:T(8,128)(2,1)S(1)}, u32[]{:S(2)}, u32[]{:S(2)}) %all-to-all-start) | async-done | bytes 262176 | tf_op jit(solution)/shard_map/all_to_all | solution.py:311
  31.7 4.1 %shard_map.88 = (bf16[64,16,128]{2,1,0:T(8,128)(2,1)}, bf16[256,1280]{1,0:T(8,128)(2,1)S(1)}, bf16[256,1280]{1,0:T(8,128)(2,1)}) custom-call(s32[1]{0:T(128)} %bitcast.3.core_ref, bf16[64,16,128]{2,1,0:T(8,128)(2,1)S(1)} %all-to-all-done.x_ref, bf16[256,512]{1,0:T(8,128)(2,1)} %bitcast.12, bf16[512,1536]{1,0:T(8,128)(2,1)S(1)} %get-tuple-element.16.qkv_weight_ref), custom_call_target="tpu_custom_call" | custom-call | flops 1744830464 | bytes 3670020 | tf_op jit(solution)/shard_map/pallas_call | solution.py:252
  35.8 0.0 copy-start.1
  35.8 2.4 %collective-permute-start = (bf16[256,1280]{1,0:T(8,128)(2,1)}, bf16[256,1280]{1,0:T(8,128)(2,1)S(1)}, u32[]{:S(2)}, u32[]{:S(2)}) collective-permute-start(bf16[256,1280]{1,0:T(8,128)(2,1)} %get-tuple-element.19), channel_id=1, source_target_pairs={{0,1},{1,0},{2,3},{3,2},{4,5},{5,4},{6,7},{7,6},{8,9},{9,8},{10,11... | collective-permute-start | bytes 1966088 | tf_op jit(solution)/shard_map/ppermute | solution.py:334
  38.2 5.7 %all-to-all-start.1 = ((bf16[64,16,128]{2,1,0:T(8,128)(2,1)}), bf16[64,16,128]{2,1,0:T(8,128)(2,1)S(1)}, u32[]{:S(2)}, u32[]{:S(2)}) async-start(bf16[64,16,128]{2,1,0:T(8,128)(2,1)} %get-tuple-element.17), calls=%async_computation.1 | async-start | bytes 524288 | tf_op jit(solution)/shard_map/all_to_all | solution.py:333
  43.9 0.0 collective-permute-done.theirs_ref
  43.9 0.8 shard_map.90
  44.7 4.3 %collective-permute-start.1 = (bf16[768,128]{1,0:T(8,128)(2,1)S(1)}, bf16[768,128]{1,0:T(8,128)(2,1)S(1)}, u32[]{:S(2)}, u32[]{:S(2)}) collective-permute-start(bf16[768,128]{1,0:T(8,128)(2,1)S(1)} %get-tuple-element.21), channel_id=1, source_target_pairs={{0,496},{1,81},{16,480},{17,65},{32,464},{33,113},{48,448},{49,97}... | collective-permute-start | bytes 589832 | tf_op jit(solution)/shard_map/ppermute | solution.py:344
  49.0 3.8 %collective-permute-start.2 = (bf16[768,128]{1,0:T(8,128)(2,1)S(1)}, bf16[768,128]{1,0:T(8,128)(2,1)S(1)}, u32[]{:S(2)}, u32[]{:S(2)}) collective-permute-start(bf16[768,128]{1,0:T(8,128)(2,1)S(1)} %get-tuple-element.22), channel_id=1, source_target_pairs={{0,16},{1,49},{16,0},{17,33},{32,48},{33,17},{48,32},{49,1},{2,18}... | collective-permute-start | bytes 589832 | tf_op jit(solution)/shard_map/ppermute | solution.py:344
  52.8 4.9 %collective-permute-start.3 = (bf16[768,128]{1,0:T(8,128)(2,1)S(1)}, bf16[768,128]{1,0:T(8,128)(2,1)S(1)}, u32[]{:S(2)}, u32[]{:S(2)}) collective-permute-start(bf16[768,128]{1,0:T(8,128)(2,1)S(1)} %get-tuple-element.23), channel_id=1, source_target_pairs={{0,64},{1,449},{64,0},{65,129},{128,192},{129,65},{192,128},{193,2... | collective-permute-start | bytes 589832 | tf_op jit(solution)/shard_map/ppermute | solution.py:344
  57.7 0.0 all-to-all-done.1.grad_ref
  57.7 0.0 copy-done.1
  57.7 2.6 %shard_map.89.score_ref = f32[512,128]{1,0:T(8,128)S(1)} custom-call(s32[1,1024]{1,0:T(1,128)S(1)} %bitcast.8, s32[1,1024]{1,0:T(1,128)S(1)} %bitcast.11, bf16[1024,512]{1,0:T(8,128)(2,1)} %events_ref.3, bf16[1024,512]{1,0:T(8,128)(2,1)} %get-tuple-element.14.centred_ref, f32[8,1024]{1,0:T(8,128)S(1)} %copy-done.1, ...), custom_call_target="tpu_custom_call" | custom-call | flops 536870912 | bytes 2662400 | tf_op jit(solution)/shard_map/pallas_call | solution.py:252
  60.3 0.0 collective-permute-done.1.a_ref
  60.3 0.0 collective-permute-done.2.b_ref
  60.3 0.4 collective-permute-done.3.c_ref
  60.7 0.2 shard_map.91
  60.9 22.2 %all_to_all.20.x_ref = bf16[64,8,256]{2,1,0:T(8,128)(2,1)S(1)} all-to-all(bf16[64,8,256]{2,1,0:T(8,128)(2,1)S(1)} %shard_map.91), channel_id=1, replica_groups=mesh['rep'=8,'x'=4,'z'=8,'core'=2] {'x','z','core'}, dimensions={0} | all-to-all | bytes 524288 | tf_op jit(solution)/shard_map/all_to_all | solution.py:359
  83.2 0.1 shard_map.92
  83.3 11.3 %all_to_all.21.x_ref = bf16[8,8,896]{2,1,0:T(8,128)(2,1)S(1)} all-to-all(bf16[8,8,896]{2,1,0:T(8,128)(2,1)S(1)} %shard_map.92), channel_id=1, replica_groups=mesh['rep'=8,'x'=4,'z'=8,'core'=2] {'rep'}, dimensions={0} | all-to-all | bytes 229376 | tf_op jit(solution)/shard_map/all_to_all | solution.py:363
  94.6 0.6 shard_map.93
Async XLA Ops:
  0.6 19.1 %copy-start.2 = (s32[1024]{0:T(1024)S(1)}, s32[1024]{0:T(1024)}, u32[]{:S(2)}) copy-start(s32[1024]{0:T(1024)} %param.8) | copy-start | bytes 12292
  0.6 19.1 %copy-start.3 = (s32[1024]{0:T(1024)S(1)}, s32[1024]{0:T(1024)}, u32[]{:S(2)}) copy-start(s32[1024]{0:T(1024)} %param.9) | copy-start | bytes 12292
  4.9 26.9 %all-to-all-start = ((bf16[64,16,128]{2,1,0:T(8,128)(2,1)}), bf16[64,16,128]{2,1,0:T(8,128)(2,1)S(1)}, u32[]{:S(2)}, u32[]{:S(2)}) async-start(bf16[64,16,128]{2,1,0:T(8,128)(2,1)} %get-tuple-element.13.summary_ref), calls=%async_computation | async-start | bytes 524288 | tf_op jit(solution)/shard_map/all_to_all | solution.py:311
  19.8 1.0 %copy-start = (bf16[64,16,128]{2,1,0:T(8,128)(2,1)S(1)}, bf16[64,16,128]{2,1,0:T(8,128)(2,1)}, u32[]{:S(2)}) copy-start(bf16[64,16,128]{2,1,0:T(8,128)(2,1)} %get-tuple-element.13.summary_ref) | copy-start | bytes 786436
  35.8 21.9 %copy-start.1 = (f32[8,1024]{1,0:T(8,128)S(1)}, f32[8,1024]{1,0:T(8,128)}, u32[]{:S(2)}) copy-start(f32[8,1024]{1,0:T(8,128)} %get-tuple-element.15.weight_ref) | copy-start | bytes 98308
  35.8 8.1 %collective-permute-start = (bf16[256,1280]{1,0:T(8,128)(2,1)}, bf16[256,1280]{1,0:T(8,128)(2,1)S(1)}, u32[]{:S(2)}, u32[]{:S(2)}) collective-permute-start(bf16[256,1280]{1,0:T(8,128)(2,1)} %get-tuple-element.19), channel_id=1, source_target_pairs={{0,1},{1,0},{2,3},{3,2},{4,5},{5,4},{6,7},{7,6},{8,9},{9,8},{10,11... | collective-permute-start | bytes 1966088 | tf_op jit(solution)/shard_map/ppermute | solution.py:334
  38.2 19.5 %all-to-all-start.1 = ((bf16[64,16,128]{2,1,0:T(8,128)(2,1)}), bf16[64,16,128]{2,1,0:T(8,128)(2,1)S(1)}, u32[]{:S(2)}, u32[]{:S(2)}) async-start(bf16[64,16,128]{2,1,0:T(8,128)(2,1)} %get-tuple-element.17), calls=%async_computation.1 | async-start | bytes 524288 | tf_op jit(solution)/shard_map/all_to_all | solution.py:333
  44.7 15.6 %collective-permute-start.1 = (bf16[768,128]{1,0:T(8,128)(2,1)S(1)}, bf16[768,128]{1,0:T(8,128)(2,1)S(1)}, u32[]{:S(2)}, u32[]{:S(2)}) collective-permute-start(bf16[768,128]{1,0:T(8,128)(2,1)S(1)} %get-tuple-element.21), channel_id=1, source_target_pairs={{0,496},{1,81},{16,480},{17,65},{32,464},{33,113},{48,448},{49,97}... | collective-permute-start | bytes 589832 | tf_op jit(solution)/shard_map/ppermute | solution.py:344
  49.0 11.3 %collective-permute-start.2 = (bf16[768,128]{1,0:T(8,128)(2,1)S(1)}, bf16[768,128]{1,0:T(8,128)(2,1)S(1)}, u32[]{:S(2)}, u32[]{:S(2)}) collective-permute-start(bf16[768,128]{1,0:T(8,128)(2,1)S(1)} %get-tuple-element.22), channel_id=1, source_target_pairs={{0,16},{1,49},{16,0},{17,33},{32,48},{33,17},{48,32},{49,1},{2,18}... | collective-permute-start | bytes 589832 | tf_op jit(solution)/shard_map/ppermute | solution.py:344
  52.8 7.9 %collective-permute-start.3 = (bf16[768,128]{1,0:T(8,128)(2,1)S(1)}, bf16[768,128]{1,0:T(8,128)(2,1)S(1)}, u32[]{:S(2)}, u32[]{:S(2)}) collective-permute-start(bf16[768,128]{1,0:T(8,128)(2,1)S(1)} %get-tuple-element.23), channel_id=1, source_target_pairs={{0,64},{1,449},{64,0},{65,129},{128,192},{129,65},{192,128},{193,2... | collective-permute-start | bytes 589832 | tf_op jit(solution)/shard_map/ppermute | solution.py:344

commit v12 on v11

--- a/solution.py
+++ b/solution.py
@@ -71,25 +71,15 @@
     return jnp.concatenate(pieces, axis=1).astype(BF16)
 
 
-def pool_kernel(users, slots, *refs):
-    sources, (summary_ref, weight_ref), held, sems = refs[:5], refs[5:7], refs[7:12], refs[12]
-    copies = [pltpu.make_async_copy(source, target, sems.at[i]) for i, (source, target) in enumerate(zip(sources, held))]
-    for copy in copies:
-        copy.start()
-    user_ref, day_ref, score_ref, events_ref, value_ref = held
+def pool_kernel(users, slots, user_ref, day_ref, score_ref, events_ref, value_ref, summary_ref, weight_ref):
     heads, width = score_ref.shape
     expand = one_hot(iota((3 * heads, width), 1) // (width // heads) == iota((3 * heads, width), 0) % heads)
-    copies[0].wait()
-    copies[1].wait()
     rows = slot_rows(user_ref, day_ref, users, slots)
-    copies[2].wait()
-    copies[3].wait()
     exponent = jnp.exp(nt(score_ref[...], events_ref[...]))
     denominator = join3(nt(split3(exponent), rows))
     weight = exponent / join3(nn(split3(denominator), rows))
     weight_ref[...] = weight
     wide = tn(split3(weight), expand)
-    copies[4].wait()
     weighted = (nn(events_ref[...], value_ref[...]) * wide).astype(BF16)
     summary_ref[...] = to_blocks(nn(rows, weighted), users)
 
@@ -297,16 +287,7 @@
         [block, ((heads, count), F32)],
         (user_row, day_row, score_weight.T, events, value_weight),
         flops=2 * count * width * (width + slots),
-        whole=(0, 1, 2, 3, 4),
-        scratch=[
-            pltpu.VMEM((1, count), jnp.int32),
-            pltpu.VMEM((1, count), jnp.int32),
-            pltpu.VMEM((heads, width), BF16),
-            pltpu.VMEM((count, width), BF16),
-            pltpu.VMEM((width, width), BF16),
-            pltpu.SemaphoreType.DMA((5,)),
-        ],
-        limit=60,
+        held=(0, 1, 2, 3, 4),
     )
     by_user = lax.all_to_all(summary, DAY, split_axis=0, concat_axis=0, tiled=True)
     centred, qkv_held = call(

time: 96.3 us -> 96.1 us (level)
  waiting for transfers between devices: 7.21 us -> 8.6 us
  local copies, waits for them, and re-layouts: 0.99 us -> 0.01 us
    all_to_all x1, waiting for transfers between devices: 6.77 us -> 8.14 us  [shards(): lax.all_to_all(summary, DAY, split_axis=0, concat_axis=0, tiled=True)]
    unnamed x8 -> x4, local copies, waits for them, and re-layouts: 0.99 us -> 0.01 us
where the time goes in v12:
time: 96.1 us; the launch traced here: 95.1 us
  starting transfers between devices  35.9 us (37%)
  blocking collectives  33.6 us (35%)
  Pallas kernels  16.3 us (17%)
  waiting for transfers between devices  8.6 us (9%)
    all_to_all x1, blocking collectives, shards(): lax.all_to_all(partial_sums, DAY, split_axis=0, concat_axis=0, tiled=True)  22.2 us
    pallas_call x8, Pallas kernels, call(): pl.pallas_call(kernel, out_shape=[pltpu.HBM(s, t) if i in out_whole + out...  16.3 us
    all_to_all x1, starting transfers between devices, shards(): lax.all_to_all(summary, DAY, split_axis=0, concat_axis=0, tiled=True)  14.8 us
    ppermute x3, starting transfers between devices, shards(): lax.ppermute(packs[step], axes, neighbours(sizes_of, far))  13 us
    all_to_all x1, blocking collectives, shards(): lax.all_to_all(merged, 'rep', split_axis=0, concat_axis=0, tiled=True)  11.3 us
    all_to_all x1, waiting for transfers between devices, shards(): lax.all_to_all(summary, DAY, split_axis=0, concat_axis=0, tiled=True)  8.14 us
    all_to_all x1, starting transfers between devices, shards(): lax.all_to_all(grad_summary, DAY, split_axis=0, concat_axis=0, tiled=True)  5.71 us
    ppermute x1, starting transfers between devices, shards(): lax.ppermute(send, 'core', [(i, cores - 1 - i) for i in range(cores)])  2.35 us
  transfers between devices with their start and end apart: 6, of which 2 were waited for; matrix products, arithmetic and copies ran while one was open for 0% of the time, Pallas kernels for 8%

profile of v12, /device:TPU:1, one launch (start us, length us, event | category | flops | bytes accessed | tf_op | source)
XLA Modules:
  0.0 95.1 jit_solution(14174242473093536521)
XLA Ops:
  0.6 0.0 copy-start
  0.6 0.0 copy-start.1
  0.7 4.1 %shard_map.86 = (bf16[64,16,128]{2,1,0:T(8,128)(2,1)}, f32[8,1024]{1,0:T(8,128)S(1)}) custom-call(s32[1,1024]{1,0:T(1,128)} %bitcast.6, s32[1,1024]{1,0:T(1,128)} %bitcast.9, bf16[8,512]{1,0:T(8,128)(2,1)} %bitcast.13, bf16[1024,512]{1,0:T(8,128)(2,1)} %events_ref.5, bf16[512,512]{1,0:T(8,128)(2,1)} %value_ref.3), custom_call_target="tpu_custom_call" | custom-call | flops 805306368 | bytes 1884160 | tf_op jit(solution)/shard_map/pallas_call | solution.py:242
  4.8 14.8 %all-to-all-start = ((bf16[64,16,128]{2,1,0:T(8,128)(2,1)}), bf16[64,16,128]{2,1,0:T(8,128)(2,1)S(1)}, u32[]{:S(2)}, u32[]{:S(2)}) async-start(bf16[64,16,128]{2,1,0:T(8,128)(2,1)} %get-tuple-element.13.summary_ref), calls=%async_computation | async-start | bytes 524288 | tf_op jit(solution)/shard_map/all_to_all | solution.py:292
  19.6 0.0 copy-done
  19.7 0.0 copy-done.1
  19.7 3.8 %shard_map.87 = (bf16[1024,512]{1,0:T(8,128)(2,1)}, bf16[512,1536]{1,0:T(8,128)(2,1)S(1)}) custom-call(s32[1,1024]{1,0:T(1,128)S(1)} %bitcast.7, s32[1,1024]{1,0:T(1,128)S(1)} %bitcast.10, bf16[1024,512]{1,0:T(8,128)(2,1)} %events_ref.5, bf16[512,512]{1,0:T(8,128)(2,1)} %value_ref.3, bf16[64,16,128]{2,1,0:T(8,128)(2,1)} %get-tuple-element.13.summary_ref, ...), custom_call_target="tpu_custom_call" | custom-call | flops 805306368 | bytes 6037504 | tf_op jit(solution)/shard_map/pallas_call | solution.py:242
  23.5 8.1 %all-to-all-done.x_ref = bf16[64,16,128]{2,1,0:T(8,128)(2,1)S(1)} async-done(((bf16[64,16,128]{2,1,0:T(8,128)(2,1)}), bf16[64,16,128]{2,1,0:T(8,128)(2,1)S(1)}, u32[]{:S(2)}, u32[]{:S(2)}) %all-to-all-start) | async-done | bytes 262176 | tf_op jit(solution)/shard_map/all_to_all | solution.py:292
  31.6 4.1 %shard_map.88 = (bf16[64,16,128]{2,1,0:T(8,128)(2,1)}, bf16[256,1280]{1,0:T(8,128)(2,1)S(1)}, bf16[256,1280]{1,0:T(8,128)(2,1)}) custom-call(s32[1]{0:T(128)} %bitcast.3.core_ref, bf16[64,16,128]{2,1,0:T(8,128)(2,1)S(1)} %all-to-all-done.x_ref, bf16[256,512]{1,0:T(8,128)(2,1)} %bitcast.12, bf16[512,1536]{1,0:T(8,128)(2,1)S(1)} %get-tuple-element.16.qkv_weight_ref), custom_call_target="tpu_custom_call" | custom-call | flops 1744830464 | bytes 3670020 | tf_op jit(solution)/shard_map/pallas_call | solution.py:242
  35.7 2.4 %collective-permute-start = (bf16[256,1280]{1,0:T(8,128)(2,1)}, bf16[256,1280]{1,0:T(8,128)(2,1)S(1)}, u32[]{:S(2)}, u32[]{:S(2)}) collective-permute-start(bf16[256,1280]{1,0:T(8,128)(2,1)} %get-tuple-element.19), channel_id=1, source_target_pairs={{0,1},{1,0},{2,3},{3,2},{4,5},{5,4},{6,7},{7,6},{8,9},{9,8},{10,11... | collective-permute-start | bytes 1966088 | tf_op jit(solution)/shard_map/ppermute | solution.py:315
  38.1 5.7 %all-to-all-start.1 = ((bf16[64,16,128]{2,1,0:T(8,128)(2,1)}), bf16[64,16,128]{2,1,0:T(8,128)(2,1)S(1)}, u32[]{:S(2)}, u32[]{:S(2)}) async-start(bf16[64,16,128]{2,1,0:T(8,128)(2,1)} %get-tuple-element.17), calls=%async_computation.1 | async-start | bytes 524288 | tf_op jit(solution)/shard_map/all_to_all | solution.py:314
  43.8 0.0 collective-permute-done.theirs_ref
  43.8 0.8 shard_map.90
  44.6 4.3 %collective-permute-start.1 = (bf16[768,128]{1,0:T(8,128)(2,1)S(1)}, bf16[768,128]{1,0:T(8,128)(2,1)S(1)}, u32[]{:S(2)}, u32[]{:S(2)}) collective-permute-start(bf16[768,128]{1,0:T(8,128)(2,1)S(1)} %get-tuple-element.21), channel_id=1, source_target_pairs={{0,496},{1,81},{16,480},{17,65},{32,464},{33,113},{48,448},{49,97}... | collective-permute-start | bytes 589832 | tf_op jit(solution)/shard_map/ppermute | solution.py:325
  48.9 3.8 %collective-permute-start.2 = (bf16[768,128]{1,0:T(8,128)(2,1)S(1)}, bf16[768,128]{1,0:T(8,128)(2,1)S(1)}, u32[]{:S(2)}, u32[]{:S(2)}) collective-permute-start(bf16[768,128]{1,0:T(8,128)(2,1)S(1)} %get-tuple-element.22), channel_id=1, source_target_pairs={{0,16},{1,49},{16,0},{17,33},{32,48},{33,17},{48,32},{49,1},{2,18}... | collective-permute-start | bytes 589832 | tf_op jit(solution)/shard_map/ppermute | solution.py:325
  52.7 4.9 %collective-permute-start.3 = (bf16[768,128]{1,0:T(8,128)(2,1)S(1)}, bf16[768,128]{1,0:T(8,128)(2,1)S(1)}, u32[]{:S(2)}, u32[]{:S(2)}) collective-permute-start(bf16[768,128]{1,0:T(8,128)(2,1)S(1)} %get-tuple-element.23), channel_id=1, source_target_pairs={{0,64},{1,449},{64,0},{65,129},{128,192},{129,65},{192,128},{193,2... | collective-permute-start | bytes 589832 | tf_op jit(solution)/shard_map/ppermute | solution.py:325
  57.6 0.0 all-to-all-done.1.grad_ref
  57.6 2.6 %shard_map.89.score_ref = f32[512,128]{1,0:T(8,128)S(1)} custom-call(s32[1,1024]{1,0:T(1,128)S(1)} %bitcast.8, s32[1,1024]{1,0:T(1,128)S(1)} %bitcast.11, bf16[1024,512]{1,0:T(8,128)(2,1)} %events_ref.5, bf16[1024,512]{1,0:T(8,128)(2,1)} %get-tuple-element.14.centred_ref, f32[8,1024]{1,0:T(8,128)S(1)} %get-tuple-element.15.weight_ref, ...), custom_call_target="tpu_custom_call" | custom-call | flops 536870912 | bytes 2662400 | tf_op jit(solution)/shard_map/pallas_call | solution.py:242
  60.1 0.0 collective-permute-done.1.a_ref
  60.2 0.0 collective-permute-done.2.b_ref
  60.2 0.4 collective-permute-done.3.c_ref
  60.6 0.2 shard_map.91
  60.8 22.2 %all_to_all.20.x_ref = bf16[64,8,256]{2,1,0:T(8,128)(2,1)S(1)} all-to-all(bf16[64,8,256]{2,1,0:T(8,128)(2,1)S(1)} %shard_map.91), channel_id=1, replica_groups=mesh['rep'=8,'x'=4,'z'=8,'core'=2] {'x','z','core'}, dimensions={0} | all-to-all | bytes 524288 | tf_op jit(solution)/shard_map/all_to_all | solution.py:340
  83.0 0.1 shard_map.92
  83.1 11.3 %all_to_all.21.x_ref = bf16[8,8,896]{2,1,0:T(8,128)(2,1)S(1)} all-to-all(bf16[8,8,896]{2,1,0:T(8,128)(2,1)S(1)} %shard_map.92), channel_id=1, replica_groups=mesh['rep'=8,'x'=4,'z'=8,'core'=2] {'rep'}, dimensions={0} | all-to-all | bytes 229376 | tf_op jit(solution)/shard_map/all_to_all | solution.py:344
  94.5 0.6 shard_map.93
Async XLA Ops:
  0.6 19.0 %copy-start = (s32[1024]{0:T(1024)S(1)}, s32[1024]{0:T(1024)}, u32[]{:S(2)}) copy-start(s32[1024]{0:T(1024)} %param.8) | copy-start | bytes 12292
  0.6 19.0 %copy-start.1 = (s32[1024]{0:T(1024)S(1)}, s32[1024]{0:T(1024)}, u32[]{:S(2)}) copy-start(s32[1024]{0:T(1024)} %param.9) | copy-start | bytes 12292
  4.8 26.8 %all-to-all-start = ((bf16[64,16,128]{2,1,0:T(8,128)(2,1)}), bf16[64,16,128]{2,1,0:T(8,128)(2,1)S(1)}, u32[]{:S(2)}, u32[]{:S(2)}) async-start(bf16[64,16,128]{2,1,0:T(8,128)(2,1)} %get-tuple-element.13.summary_ref), calls=%async_computation | async-start | bytes 524288 | tf_op jit(solution)/shard_map/all_to_all | solution.py:292
  35.7 8.1 %collective-permute-start = (bf16[256,1280]{1,0:T(8,128)(2,1)}, bf16[256,1280]{1,0:T(8,128)(2,1)S(1)}, u32[]{:S(2)}, u32[]{:S(2)}) collective-permute-start(bf16[256,1280]{1,0:T(8,128)(2,1)} %get-tuple-element.19), channel_id=1, source_target_pairs={{0,1},{1,0},{2,3},{3,2},{4,5},{5,4},{6,7},{7,6},{8,9},{9,8},{10,11... | collective-permute-start | bytes 1966088 | tf_op jit(solution)/shard_map/ppermute | solution.py:315
  38.1 19.5 %all-to-all-start.1 = ((bf16[64,16,128]{2,1,0:T(8,128)(2,1)}), bf16[64,16,128]{2,1,0:T(8,128)(2,1)S(1)}, u32[]{:S(2)}, u32[]{:S(2)}) async-start(bf16[64,16,128]{2,1,0:T(8,128)(2,1)} %get-tuple-element.17), calls=%async_computation.1 | async-start | bytes 524288 | tf_op jit(solution)/shard_map/all_to_all | solution.py:314
  44.6 15.6 %collective-permute-start.1 = (bf16[768,128]{1,0:T(8,128)(2,1)S(1)}, bf16[768,128]{1,0:T(8,128)(2,1)S(1)}, u32[]{:S(2)}, u32[]{:S(2)}) collective-permute-start(bf16[768,128]{1,0:T(8,128)(2,1)S(1)} %get-tuple-element.21), channel_id=1, source_target_pairs={{0,496},{1,81},{16,480},{17,65},{32,464},{33,113},{48,448},{49,97}... | collective-permute-start | bytes 589832 | tf_op jit(solution)/shard_map/ppermute | solution.py:325
  48.9 11.3 %collective-permute-start.2 = (bf16[768,128]{1,0:T(8,128)(2,1)S(1)}, bf16[768,128]{1,0:T(8,128)(2,1)S(1)}, u32[]{:S(2)}, u32[]{:S(2)}) collective-permute-start(bf16[768,128]{1,0:T(8,128)(2,1)S(1)} %get-tuple-element.22), channel_id=1, source_target_pairs={{0,16},{1,49},{16,0},{17,33},{32,48},{33,17},{48,32},{49,1},{2,18}... | collective-permute-start | bytes 589832 | tf_op jit(solution)/shard_map/ppermute | solution.py:325
  52.7 7.9 %collective-permute-start.3 = (bf16[768,128]{1,0:T(8,128)(2,1)S(1)}, bf16[768,128]{1,0:T(8,128)(2,1)S(1)}, u32[]{:S(2)}, u32[]{:S(2)}) collective-permute-start(bf16[768,128]{1,0:T(8,128)(2,1)S(1)} %get-tuple-element.23), channel_id=1, source_target_pairs={{0,64},{1,449},{64,0},{65,129},{128,192},{129,65},{192,128},{193,2... | collective-permute-start | bytes 589832 | tf_op jit(solution)/shard_map/ppermute | solution.py:325

commit v13 on v12

--- a/solution.py
+++ b/solution.py
@@ -325,8 +325,8 @@
         lax.ppermute(packs[step], axes, neighbours(sizes_of, far))
         for step, axes, sizes_of, far in (
             (3, ("rep", "x", "core"), (groups, x_size, cores), 0),
+            (2, ("rep", "core"), (groups, cores), 1),
             (1, ("x", "core"), (x_size, cores), 1),
-            (2, ("rep", "core"), (groups, cores), 1),
         )
     ]
     (score,) = call(

time: 96.1 us -> 95.9 us (level)
  blocking collectives: 33.6 us -> 32.5 us
    all_to_all x1, blocking collectives: 22.2 us -> 20.8 us  [shards(): lax.all_to_all(partial_sums, DAY, split_axis=0, concat_axis=0, tiled=True)]
where the time goes in v13:
time: 95.9 us; the launch traced here: 94.8 us
  starting transfers between devices  35.9 us (37%)
  blocking collectives  32.5 us (34%)
  Pallas kernels  16.3 us (17%)
  waiting for transfers between devices  9.38 us (10%)
    all_to_all x1, blocking collectives, shards(): lax.all_to_all(partial_sums, DAY, split_axis=0, concat_axis=0, tiled=True)  20.8 us
    pallas_call x8, Pallas kernels, call(): pl.pallas_call(kernel, out_shape=[pltpu.HBM(s, t) if i in out_whole + out...  16.3 us
    all_to_all x1, starting transfers between devices, shards(): lax.all_to_all(summary, DAY, split_axis=0, concat_axis=0, tiled=True)  14.8 us
    ppermute x3, starting transfers between devices, shards(): lax.ppermute(packs[step], axes, neighbours(sizes_of, far))  13 us
    all_to_all x1, blocking collectives, shards(): lax.all_to_all(merged, 'rep', split_axis=0, concat_axis=0, tiled=True)  11.7 us
    all_to_all x1, waiting for transfers between devices, shards(): lax.all_to_all(summary, DAY, split_axis=0, concat_axis=0, tiled=True)  8.14 us
    all_to_all x1, starting transfers between devices, shards(): lax.all_to_all(grad_summary, DAY, split_axis=0, concat_axis=0, tiled=True)  5.71 us
    ppermute x1, starting transfers between devices, shards(): lax.ppermute(send, 'core', [(i, cores - 1 - i) for i in range(cores)])  2.35 us
  transfers between devices with their start and end apart: 6, of which 2 were waited for; matrix products, arithmetic and copies ran while one was open for 0% of the time, Pallas kernels for 8%

profile of v13, /device:TPU:1, one launch (start us, length us, event | category | flops | bytes accessed | tf_op | source)
XLA Modules:
  0.0 94.8 jit_solution(1461414225771449914)
XLA Ops:
  0.6 0.0 copy-start
  0.6 0.0 copy-start.1
  0.7 4.1 %shard_map.86 = (bf16[64,16,128]{2,1,0:T(8,128)(2,1)}, f32[8,1024]{1,0:T(8,128)S(1)}) custom-call(s32[1,1024]{1,0:T(1,128)} %bitcast.6, s32[1,1024]{1,0:T(1,128)} %bitcast.9, bf16[8,512]{1,0:T(8,128)(2,1)} %bitcast.13, bf16[1024,512]{1,0:T(8,128)(2,1)} %events_ref.5, bf16[512,512]{1,0:T(8,128)(2,1)} %value_ref.3), custom_call_target="tpu_custom_call" | custom-call | flops 805306368 | bytes 1884160 | tf_op jit(solution)/shard_map/pallas_call | solution.py:242
  4.8 14.8 %all-to-all-start = ((bf16[64,16,128]{2,1,0:T(8,128)(2,1)}), bf16[64,16,128]{2,1,0:T(8,128)(2,1)S(1)}, u32[]{:S(2)}, u32[]{:S(2)}) async-start(bf16[64,16,128]{2,1,0:T(8,128)(2,1)} %get-tuple-element.13.summary_ref), calls=%async_computation | async-start | bytes 524288 | tf_op jit(solution)/shard_map/all_to_all | solution.py:292
  19.6 0.0 copy-done
  19.7 0.0 copy-done.1
  19.7 3.8 %shard_map.87 = (bf16[1024,512]{1,0:T(8,128)(2,1)}, bf16[512,1536]{1,0:T(8,128)(2,1)S(1)}) custom-call(s32[1,1024]{1,0:T(1,128)S(1)} %bitcast.7, s32[1,1024]{1,0:T(1,128)S(1)} %bitcast.10, bf16[1024,512]{1,0:T(8,128)(2,1)} %events_ref.5, bf16[512,512]{1,0:T(8,128)(2,1)} %value_ref.3, bf16[64,16,128]{2,1,0:T(8,128)(2,1)} %get-tuple-element.13.summary_ref, ...), custom_call_target="tpu_custom_call" | custom-call | flops 805306368 | bytes 6037504 | tf_op jit(solution)/shard_map/pallas_call | solution.py:242
  23.5 8.1 %all-to-all-done.x_ref = bf16[64,16,128]{2,1,0:T(8,128)(2,1)S(1)} async-done(((bf16[64,16,128]{2,1,0:T(8,128)(2,1)}), bf16[64,16,128]{2,1,0:T(8,128)(2,1)S(1)}, u32[]{:S(2)}, u32[]{:S(2)}) %all-to-all-start) | async-done | bytes 262176 | tf_op jit(solution)/shard_map/all_to_all | solution.py:292
  31.6 4.1 %shard_map.88 = (bf16[64,16,128]{2,1,0:T(8,128)(2,1)}, bf16[256,1280]{1,0:T(8,128)(2,1)S(1)}, bf16[256,1280]{1,0:T(8,128)(2,1)}) custom-call(s32[1]{0:T(128)} %bitcast.3.core_ref, bf16[64,16,128]{2,1,0:T(8,128)(2,1)S(1)} %all-to-all-done.x_ref, bf16[256,512]{1,0:T(8,128)(2,1)} %bitcast.12, bf16[512,1536]{1,0:T(8,128)(2,1)S(1)} %get-tuple-element.16.qkv_weight_ref), custom_call_target="tpu_custom_call" | custom-call | flops 1744830464 | bytes 3670020 | tf_op jit(solution)/shard_map/pallas_call | solution.py:242
  35.7 2.4 %collective-permute-start = (bf16[256,1280]{1,0:T(8,128)(2,1)}, bf16[256,1280]{1,0:T(8,128)(2,1)S(1)}, u32[]{:S(2)}, u32[]{:S(2)}) collective-permute-start(bf16[256,1280]{1,0:T(8,128)(2,1)} %get-tuple-element.19), channel_id=1, source_target_pairs={{0,1},{1,0},{2,3},{3,2},{4,5},{5,4},{6,7},{7,6},{8,9},{9,8},{10,11... | collective-permute-start | bytes 1966088 | tf_op jit(solution)/shard_map/ppermute | solution.py:315
  38.1 5.7 %all-to-all-start.1 = ((bf16[64,16,128]{2,1,0:T(8,128)(2,1)}), bf16[64,16,128]{2,1,0:T(8,128)(2,1)S(1)}, u32[]{:S(2)}, u32[]{:S(2)}) async-start(bf16[64,16,128]{2,1,0:T(8,128)(2,1)} %get-tuple-element.17), calls=%async_computation.1 | async-start | bytes 524288 | tf_op jit(solution)/shard_map/all_to_all | solution.py:314
  43.8 0.0 collective-permute-done.theirs_ref
  43.8 0.8 shard_map.90
  44.6 4.3 %collective-permute-start.1 = (bf16[768,128]{1,0:T(8,128)(2,1)S(1)}, bf16[768,128]{1,0:T(8,128)(2,1)S(1)}, u32[]{:S(2)}, u32[]{:S(2)}) collective-permute-start(bf16[768,128]{1,0:T(8,128)(2,1)S(1)} %get-tuple-element.21), channel_id=1, source_target_pairs={{0,496},{1,81},{16,480},{17,65},{32,464},{33,113},{48,448},{49,97}... | collective-permute-start | bytes 589832 | tf_op jit(solution)/shard_map/ppermute | solution.py:325
  48.9 4.9 %collective-permute-start.2 = (bf16[768,128]{1,0:T(8,128)(2,1)S(1)}, bf16[768,128]{1,0:T(8,128)(2,1)S(1)}, u32[]{:S(2)}, u32[]{:S(2)}) collective-permute-start(bf16[768,128]{1,0:T(8,128)(2,1)S(1)} %get-tuple-element.22), channel_id=1, source_target_pairs={{0,64},{1,449},{64,0},{65,129},{128,192},{129,65},{192,128},{193,2... | collective-permute-start | bytes 589832 | tf_op jit(solution)/shard_map/ppermute | solution.py:325
  53.8 3.8 %collective-permute-start.3 = (bf16[768,128]{1,0:T(8,128)(2,1)S(1)}, bf16[768,128]{1,0:T(8,128)(2,1)S(1)}, u32[]{:S(2)}, u32[]{:S(2)}) collective-permute-start(bf16[768,128]{1,0:T(8,128)(2,1)S(1)} %get-tuple-element.23), channel_id=1, source_target_pairs={{0,16},{1,49},{16,0},{17,33},{32,48},{33,17},{48,32},{49,1},{2,18}... | collective-permute-start | bytes 589832 | tf_op jit(solution)/shard_map/ppermute | solution.py:325
  57.6 0.0 all-to-all-done.1.grad_ref
  57.6 2.6 %shard_map.89.score_ref = f32[512,128]{1,0:T(8,128)S(1)} custom-call(s32[1,1024]{1,0:T(1,128)S(1)} %bitcast.8, s32[1,1024]{1,0:T(1,128)S(1)} %bitcast.11, bf16[1024,512]{1,0:T(8,128)(2,1)} %events_ref.5, bf16[1024,512]{1,0:T(8,128)(2,1)} %get-tuple-element.14.centred_ref, f32[8,1024]{1,0:T(8,128)S(1)} %get-tuple-element.15.weight_ref, ...), custom_call_target="tpu_custom_call" | custom-call | flops 536870912 | bytes 2662400 | tf_op jit(solution)/shard_map/pallas_call | solution.py:242
  60.1 0.0 collective-permute-done.1.a_ref
  60.2 0.0 collective-permute-done.2.b_ref
  60.2 1.2 %collective-permute-done.3.c_ref = bf16[768,128]{1,0:T(8,128)(2,1)S(1)} collective-permute-done((bf16[768,128]{1,0:T(8,128)(2,1)S(1)}, bf16[768,128]{1,0:T(8,128)(2,1)S(1)}, u32[]{:S(2)}, u32[]{:S(2)}) %collective-permute-start.3) | collective-permute-done | bytes 196640 | tf_op jit(solution)/shard_map/ppermute | solution.py:325
  61.4 0.2 shard_map.91
  61.6 20.8 %all_to_all.20.x_ref = bf16[64,8,256]{2,1,0:T(8,128)(2,1)S(1)} all-to-all(bf16[64,8,256]{2,1,0:T(8,128)(2,1)S(1)} %shard_map.91), channel_id=1, replica_groups=mesh['rep'=8,'x'=4,'z'=8,'core'=2] {'x','z','core'}, dimensions={0} | all-to-all | bytes 524288 | tf_op jit(solution)/shard_map/all_to_all | solution.py:340
  82.4 0.1 shard_map.92
  82.5 11.7 %all_to_all.21.x_ref = bf16[8,8,896]{2,1,0:T(8,128)(2,1)S(1)} all-to-all(bf16[8,8,896]{2,1,0:T(8,128)(2,1)S(1)} %shard_map.92), channel_id=1, replica_groups=mesh['rep'=8,'x'=4,'z'=8,'core'=2] {'rep'}, dimensions={0} | all-to-all | bytes 229376 | tf_op jit(solution)/shard_map/all_to_all | solution.py:344
  94.2 0.6 shard_map.93
Async XLA Ops:
  0.6 19.0 %copy-start = (s32[1024]{0:T(1024)S(1)}, s32[1024]{0:T(1024)}, u32[]{:S(2)}) copy-start(s32[1024]{0:T(1024)} %param.8) | copy-start | bytes 12292
  0.6 19.0 %copy-start.1 = (s32[1024]{0:T(1024)S(1)}, s32[1024]{0:T(1024)}, u32[]{:S(2)}) copy-start(s32[1024]{0:T(1024)} %param.9) | copy-start | bytes 12292
  4.8 26.8 %all-to-all-start = ((bf16[64,16,128]{2,1,0:T(8,128)(2,1)}), bf16[64,16,128]{2,1,0:T(8,128)(2,1)S(1)}, u32[]{:S(2)}, u32[]{:S(2)}) async-start(bf16[64,16,128]{2,1,0:T(8,128)(2,1)} %get-tuple-element.13.summary_ref), calls=%async_computation | async-start | bytes 524288 | tf_op jit(solution)/shard_map/all_to_all | solution.py:292
  35.7 8.1 %collective-permute-start = (bf16[256,1280]{1,0:T(8,128)(2,1)}, bf16[256,1280]{1,0:T(8,128)(2,1)S(1)}, u32[]{:S(2)}, u32[]{:S(2)}) collective-permute-start(bf16[256,1280]{1,0:T(8,128)(2,1)} %get-tuple-element.19), channel_id=1, source_target_pairs={{0,1},{1,0},{2,3},{3,2},{4,5},{5,4},{6,7},{7,6},{8,9},{9,8},{10,11... | collective-permute-start | bytes 1966088 | tf_op jit(solution)/shard_map/ppermute | solution.py:315
  38.1 19.5 %all-to-all-start.1 = ((bf16[64,16,128]{2,1,0:T(8,128)(2,1)}), bf16[64,16,128]{2,1,0:T(8,128)(2,1)S(1)}, u32[]{:S(2)}, u32[]{:S(2)}) async-start(bf16[64,16,128]{2,1,0:T(8,128)(2,1)} %get-tuple-element.17), calls=%async_computation.1 | async-start | bytes 524288 | tf_op jit(solution)/shard_map/all_to_all | solution.py:314
  44.6 15.6 %collective-permute-start.1 = (bf16[768,128]{1,0:T(8,128)(2,1)S(1)}, bf16[768,128]{1,0:T(8,128)(2,1)S(1)}, u32[]{:S(2)}, u32[]{:S(2)}) collective-permute-start(bf16[768,128]{1,0:T(8,128)(2,1)S(1)} %get-tuple-element.21), channel_id=1, source_target_pairs={{0,496},{1,81},{16,480},{17,65},{32,464},{33,113},{48,448},{49,97}... | collective-permute-start | bytes 589832 | tf_op jit(solution)/shard_map/ppermute | solution.py:325
  48.9 11.3 %collective-permute-start.2 = (bf16[768,128]{1,0:T(8,128)(2,1)S(1)}, bf16[768,128]{1,0:T(8,128)(2,1)S(1)}, u32[]{:S(2)}, u32[]{:S(2)}) collective-permute-start(bf16[768,128]{1,0:T(8,128)(2,1)S(1)} %get-tuple-element.22), channel_id=1, source_target_pairs={{0,64},{1,449},{64,0},{65,129},{128,192},{129,65},{192,128},{193,2... | collective-permute-start | bytes 589832 | tf_op jit(solution)/shard_map/ppermute | solution.py:325
  53.8 7.6 %collective-permute-start.3 = (bf16[768,128]{1,0:T(8,128)(2,1)S(1)}, bf16[768,128]{1,0:T(8,128)(2,1)S(1)}, u32[]{:S(2)}, u32[]{:S(2)}) collective-permute-start(bf16[768,128]{1,0:T(8,128)(2,1)S(1)} %get-tuple-element.23), channel_id=1, source_target_pairs={{0,16},{1,49},{16,0},{17,33},{32,48},{33,17},{48,32},{49,1},{2,18}... | collective-permute-start | bytes 589832 | tf_op jit(solution)/shard_map/ppermute | solution.py:325

commit v14 on v13

--- a/solution.py
+++ b/solution.py
@@ -75,12 +75,12 @@
     heads, width = score_ref.shape
     expand = one_hot(iota((3 * heads, width), 1) // (width // heads) == iota((3 * heads, width), 0) % heads)
     rows = slot_rows(user_ref, day_ref, users, slots)
+    values = nn(events_ref[...], value_ref[...])
     exponent = jnp.exp(nt(score_ref[...], events_ref[...]))
     denominator = join3(nt(split3(exponent), rows))
     weight = exponent / join3(nn(split3(denominator), rows))
     weight_ref[...] = weight
-    wide = tn(split3(weight), expand)
-    weighted = (nn(events_ref[...], value_ref[...]) * wide).astype(BF16)
+    weighted = (values * tn(split3(weight), expand)).astype(BF16)
     summary_ref[...] = to_blocks(nn(rows, weighted), users)
 
 

time: 95.9 us -> 95.8 us (level)
  no operation moved by 1% of the time
where the time goes in v14:
time: 95.8 us; the launch traced here: 94.8 us
  starting transfers between devices  35.9 us (37%)
  blocking collectives  32.5 us (34%)
  Pallas kernels  16.3 us (17%)
  waiting for transfers between devices  9.36 us (10%)
    all_to_all x1, blocking collectives, shards(): lax.all_to_all(partial_sums, DAY, split_axis=0, concat_axis=0, tiled=True)  20.8 us
    pallas_call x8, Pallas kernels, call(): pl.pallas_call(kernel, out_shape=[pltpu.HBM(s, t) if i in out_whole + out...  16.3 us
    all_to_all x1, starting transfers between devices, shards(): lax.all_to_all(summary, DAY, split_axis=0, concat_axis=0, tiled=True)  14.8 us
    ppermute x3, starting transfers between devices, shards(): lax.ppermute(packs[step], axes, neighbours(sizes_of, far))  13 us
    all_to_all x1, blocking collectives, shards(): lax.all_to_all(merged, 'rep', split_axis=0, concat_axis=0, tiled=True)  11.7 us
    all_to_all x1, waiting for transfers between devices, shards(): lax.all_to_all(summary, DAY, split_axis=0, concat_axis=0, tiled=True)  8.14 us
    all_to_all x1, starting transfers between devices, shards(): lax.all_to_all(grad_summary, DAY, split_axis=0, concat_axis=0, tiled=True)  5.7 us
    ppermute x1, starting transfers between devices, shards(): lax.ppermute(send, 'core', [(i, cores - 1 - i) for i in range(cores)])  2.36 us
  transfers between devices with their start and end apart: 6, of which 2 were waited for; matrix products, arithmetic and copies ran while one was open for 0% of the time, Pallas kernels for 8%

profile of v14, /device:TPU:1, one launch (start us, length us, event | category | flops | bytes accessed | tf_op | source)
XLA Modules:
  0.0 94.8 jit_solution(8465704392964689443)
XLA Ops:
  0.6 0.0 copy-start
  0.6 0.0 copy-start.1
  0.7 4.1 %shard_map.86 = (bf16[64,16,128]{2,1,0:T(8,128)(2,1)}, f32[8,1024]{1,0:T(8,128)S(1)}) custom-call(s32[1,1024]{1,0:T(1,128)} %bitcast.6, s32[1,1024]{1,0:T(1,128)} %bitcast.9, bf16[8,512]{1,0:T(8,128)(2,1)} %bitcast.13, bf16[1024,512]{1,0:T(8,128)(2,1)} %events_ref.5, bf16[512,512]{1,0:T(8,128)(2,1)} %value_ref.3), custom_call_target="tpu_custom_call" | custom-call | flops 805306368 | bytes 1884160 | tf_op jit(solution)/shard_map/pallas_call | solution.py:242
  4.8 14.8 %all-to-all-start = ((bf16[64,16,128]{2,1,0:T(8,128)(2,1)}), bf16[64,16,128]{2,1,0:T(8,128)(2,1)S(1)}, u32[]{:S(2)}, u32[]{:S(2)}) async-start(bf16[64,16,128]{2,1,0:T(8,128)(2,1)} %get-tuple-element.13.summary_ref), calls=%async_computation | async-start | bytes 524288 | tf_op jit(solution)/shard_map/all_to_all | solution.py:292
  19.6 0.0 copy-done
  19.6 0.0 copy-done.1
  19.7 3.8 %shard_map.87 = (bf16[1024,512]{1,0:T(8,128)(2,1)}, bf16[512,1536]{1,0:T(8,128)(2,1)S(1)}) custom-call(s32[1,1024]{1,0:T(1,128)S(1)} %bitcast.7, s32[1,1024]{1,0:T(1,128)S(1)} %bitcast.10, bf16[1024,512]{1,0:T(8,128)(2,1)} %events_ref.5, bf16[512,512]{1,0:T(8,128)(2,1)} %value_ref.3, bf16[64,16,128]{2,1,0:T(8,128)(2,1)} %get-tuple-element.13.summary_ref, ...), custom_call_target="tpu_custom_call" | custom-call | flops 805306368 | bytes 6037504 | tf_op jit(solution)/shard_map/pallas_call | solution.py:242
  23.5 8.1 %all-to-all-done.x_ref = bf16[64,16,128]{2,1,0:T(8,128)(2,1)S(1)} async-done(((bf16[64,16,128]{2,1,0:T(8,128)(2,1)}), bf16[64,16,128]{2,1,0:T(8,128)(2,1)S(1)}, u32[]{:S(2)}, u32[]{:S(2)}) %all-to-all-start) | async-done | bytes 262176 | tf_op jit(solution)/shard_map/all_to_all | solution.py:292
  31.6 4.1 %shard_map.88 = (bf16[64,16,128]{2,1,0:T(8,128)(2,1)}, bf16[256,1280]{1,0:T(8,128)(2,1)S(1)}, bf16[256,1280]{1,0:T(8,128)(2,1)}) custom-call(s32[1]{0:T(128)} %bitcast.3.core_ref, bf16[64,16,128]{2,1,0:T(8,128)(2,1)S(1)} %all-to-all-done.x_ref, bf16[256,512]{1,0:T(8,128)(2,1)} %bitcast.12, bf16[512,1536]{1,0:T(8,128)(2,1)S(1)} %get-tuple-element.16.qkv_weight_ref), custom_call_target="tpu_custom_call" | custom-call | flops 1744830464 | bytes 3670020 | tf_op jit(solution)/shard_map/pallas_call | solution.py:242
  35.7 2.4 %collective-permute-start = (bf16[256,1280]{1,0:T(8,128)(2,1)}, bf16[256,1280]{1,0:T(8,128)(2,1)S(1)}, u32[]{:S(2)}, u32[]{:S(2)}) collective-permute-start(bf16[256,1280]{1,0:T(8,128)(2,1)} %get-tuple-element.19), channel_id=1, source_target_pairs={{0,1},{1,0},{2,3},{3,2},{4,5},{5,4},{6,7},{7,6},{8,9},{9,8},{10,11... | collective-permute-start | bytes 1966088 | tf_op jit(solution)/shard_map/ppermute | solution.py:315
  38.1 5.7 %all-to-all-start.1 = ((bf16[64,16,128]{2,1,0:T(8,128)(2,1)}), bf16[64,16,128]{2,1,0:T(8,128)(2,1)S(1)}, u32[]{:S(2)}, u32[]{:S(2)}) async-start(bf16[64,16,128]{2,1,0:T(8,128)(2,1)} %get-tuple-element.17), calls=%async_computation.1 | async-start | bytes 524288 | tf_op jit(solution)/shard_map/all_to_all | solution.py:314
  43.8 0.0 collective-permute-done.theirs_ref
  43.8 0.8 shard_map.90
  44.6 4.3 %collective-permute-start.1 = (bf16[768,128]{1,0:T(8,128)(2,1)S(1)}, bf16[768,128]{1,0:T(8,128)(2,1)S(1)}, u32[]{:S(2)}, u32[]{:S(2)}) collective-permute-start(bf16[768,128]{1,0:T(8,128)(2,1)S(1)} %get-tuple-element.21), channel_id=1, source_target_pairs={{0,496},{1,81},{16,480},{17,65},{32,464},{33,113},{48,448},{49,97}... | collective-permute-start | bytes 589832 | tf_op jit(solution)/shard_map/ppermute | solution.py:325
  48.9 4.9 %collective-permute-start.2 = (bf16[768,128]{1,0:T(8,128)(2,1)S(1)}, bf16[768,128]{1,0:T(8,128)(2,1)S(1)}, u32[]{:S(2)}, u32[]{:S(2)}) collective-permute-start(bf16[768,128]{1,0:T(8,128)(2,1)S(1)} %get-tuple-element.22), channel_id=1, source_target_pairs={{0,64},{1,449},{64,0},{65,129},{128,192},{129,65},{192,128},{193,2... | collective-permute-start | bytes 589832 | tf_op jit(solution)/shard_map/ppermute | solution.py:325
  53.8 3.8 %collective-permute-start.3 = (bf16[768,128]{1,0:T(8,128)(2,1)S(1)}, bf16[768,128]{1,0:T(8,128)(2,1)S(1)}, u32[]{:S(2)}, u32[]{:S(2)}) collective-permute-start(bf16[768,128]{1,0:T(8,128)(2,1)S(1)} %get-tuple-element.23), channel_id=1, source_target_pairs={{0,16},{1,49},{16,0},{17,33},{32,48},{33,17},{48,32},{49,1},{2,18}... | collective-permute-start | bytes 589832 | tf_op jit(solution)/shard_map/ppermute | solution.py:325
  57.6 0.0 all-to-all-done.1.grad_ref
  57.6 2.6 %shard_map.89.score_ref = f32[512,128]{1,0:T(8,128)S(1)} custom-call(s32[1,1024]{1,0:T(1,128)S(1)} %bitcast.8, s32[1,1024]{1,0:T(1,128)S(1)} %bitcast.11, bf16[1024,512]{1,0:T(8,128)(2,1)} %events_ref.5, bf16[1024,512]{1,0:T(8,128)(2,1)} %get-tuple-element.14.centred_ref, f32[8,1024]{1,0:T(8,128)S(1)} %get-tuple-element.15.weight_ref, ...), custom_call_target="tpu_custom_call" | custom-call | flops 536870912 | bytes 2662400 | tf_op jit(solution)/shard_map/pallas_call | solution.py:242
  60.2 0.0 collective-permute-done.1.a_ref
  60.2 0.0 collective-permute-done.2.b_ref
  60.2 1.2 %collective-permute-done.3.c_ref = bf16[768,128]{1,0:T(8,128)(2,1)S(1)} collective-permute-done((bf16[768,128]{1,0:T(8,128)(2,1)S(1)}, bf16[768,128]{1,0:T(8,128)(2,1)S(1)}, u32[]{:S(2)}, u32[]{:S(2)}) %collective-permute-start.3) | collective-permute-done | bytes 196640 | tf_op jit(solution)/shard_map/ppermute | solution.py:325
  61.4 0.2 shard_map.91
  61.6 20.8 %all_to_all.20.x_ref = bf16[64,8,256]{2,1,0:T(8,128)(2,1)S(1)} all-to-all(bf16[64,8,256]{2,1,0:T(8,128)(2,1)S(1)} %shard_map.91), channel_id=1, replica_groups=mesh['rep'=8,'x'=4,'z'=8,'core'=2] {'x','z','core'}, dimensions={0} | all-to-all | bytes 524288 | tf_op jit(solution)/shard_map/all_to_all | solution.py:340
  82.4 0.1 shard_map.92
  82.5 11.7 %all_to_all.21.x_ref = bf16[8,8,896]{2,1,0:T(8,128)(2,1)S(1)} all-to-all(bf16[8,8,896]{2,1,0:T(8,128)(2,1)S(1)} %shard_map.92), channel_id=1, replica_groups=mesh['rep'=8,'x'=4,'z'=8,'core'=2] {'rep'}, dimensions={0} | all-to-all | bytes 229376 | tf_op jit(solution)/shard_map/all_to_all | solution.py:344
  94.2 0.6 shard_map.93
Async XLA Ops:
  0.6 19.0 %copy-start = (s32[1024]{0:T(1024)S(1)}, s32[1024]{0:T(1024)}, u32[]{:S(2)}) copy-start(s32[1024]{0:T(1024)} %param.8) | copy-start | bytes 12292
  0.6 19.0 %copy-start.1 = (s32[1024]{0:T(1024)S(1)}, s32[1024]{0:T(1024)}, u32[]{:S(2)}) copy-start(s32[1024]{0:T(1024)} %param.9) | copy-start | bytes 12292
  4.8 26.8 %all-to-all-start = ((bf16[64,16,128]{2,1,0:T(8,128)(2,1)}), bf16[64,16,128]{2,1,0:T(8,128)(2,1)S(1)}, u32[]{:S(2)}, u32[]{:S(2)}) async-start(bf16[64,16,128]{2,1,0:T(8,128)(2,1)} %get-tuple-element.13.summary_ref), calls=%async_computation | async-start | bytes 524288 | tf_op jit(solution)/shard_map/all_to_all | solution.py:292
  35.7 8.1 %collective-permute-start = (bf16[256,1280]{1,0:T(8,128)(2,1)}, bf16[256,1280]{1,0:T(8,128)(2,1)S(1)}, u32[]{:S(2)}, u32[]{:S(2)}) collective-permute-start(bf16[256,1280]{1,0:T(8,128)(2,1)} %get-tuple-element.19), channel_id=1, source_target_pairs={{0,1},{1,0},{2,3},{3,2},{4,5},{5,4},{6,7},{7,6},{8,9},{9,8},{10,11... | collective-permute-start | bytes 1966088 | tf_op jit(solution)/shard_map/ppermute | solution.py:315
  38.1 19.5 %all-to-all-start.1 = ((bf16[64,16,128]{2,1,0:T(8,128)(2,1)}), bf16[64,16,128]{2,1,0:T(8,128)(2,1)S(1)}, u32[]{:S(2)}, u32[]{:S(2)}) async-start(bf16[64,16,128]{2,1,0:T(8,128)(2,1)} %get-tuple-element.17), calls=%async_computation.1 | async-start | bytes 524288 | tf_op jit(solution)/shard_map/all_to_all | solution.py:314
  44.6 15.6 %collective-permute-start.1 = (bf16[768,128]{1,0:T(8,128)(2,1)S(1)}, bf16[768,128]{1,0:T(8,128)(2,1)S(1)}, u32[]{:S(2)}, u32[]{:S(2)}) collective-permute-start(bf16[768,128]{1,0:T(8,128)(2,1)S(1)} %get-tuple-element.21), channel_id=1, source_target_pairs={{0,496},{1,81},{16,480},{17,65},{32,464},{33,113},{48,448},{49,97}... | collective-permute-start | bytes 589832 | tf_op jit(solution)/shard_map/ppermute | solution.py:325
  48.9 11.3 %collective-permute-start.2 = (bf16[768,128]{1,0:T(8,128)(2,1)S(1)}, bf16[768,128]{1,0:T(8,128)(2,1)S(1)}, u32[]{:S(2)}, u32[]{:S(2)}) collective-permute-start(bf16[768,128]{1,0:T(8,128)(2,1)S(1)} %get-tuple-element.22), channel_id=1, source_target_pairs={{0,64},{1,449},{64,0},{65,129},{128,192},{129,65},{192,128},{193,2... | collective-permute-start | bytes 589832 | tf_op jit(solution)/shard_map/ppermute | solution.py:325
  53.8 7.6 %collective-permute-start.3 = (bf16[768,128]{1,0:T(8,128)(2,1)S(1)}, bf16[768,128]{1,0:T(8,128)(2,1)S(1)}, u32[]{:S(2)}, u32[]{:S(2)}) collective-permute-start(bf16[768,128]{1,0:T(8,128)(2,1)S(1)} %get-tuple-element.23), channel_id=1, source_target_pairs={{0,16},{1,49},{16,0},{17,33},{32,48},{33,17},{48,32},{49,1},{2,18}... | collective-permute-start | bytes 589832 | tf_op jit(solution)/shard_map/ppermute | solution.py:325
